TPU v7x, 128 devices: a whole 4x4x4 slice. The times are simulated.
128 devices in a mesh: tm: 32 (over y, x, core), state: 4 (over z).
Axes of the slice: x: 4, y: 4, z: 4, core: 2. Of those that a mesh axis runs over, the one named last changes fastest.
Arguments:
- dynamics: float32 [512, 49152], P('tm', 'state'), may hold values from -0.05 to 1.05, as said below
- band: int32 [512, 4, 2], P('tm', 'state'), may hold values from 0 to 1
- observed: float32 [512, 256], P('tm', 'state'), may hold values from -60 to 60
- obs_mask: int32 [512, 256], P('tm', 'state'), may hold values 0 or 1
- filter_gain: float32 [512, 256], P('tm', 'state'), may hold values from 0.0005 to 0.02
- smooth_gain: float32 [512, 256], P('tm', 'state'), may hold values from 0.97 to 0.9995
Outputs:
- filtered: float32 [512, 256], P('tm', 'state')
- smoothed: float32 [512, 256], P('tm', 'state')
Inputs may be any that keep to these rules, and one draw needn't show every extreme that they name: `dynamics`: entries r * 3 * 64 to (r + 1) * 3 * 64 - 1 of a step hold row r's couplings to the block before, its own block and the block after; entries that would reach outside the state are never used.
All inputs are finite; a program needn't handle non-finite values. No bound on the sum of `obs_mask` on one device may be relied on, other than what follows from the above.
Results may differ from a plain program's by a relative error of at most 0.0003.
Values sent between devices are 32-bit elements; how exact they have to be, the bound alone decides.
No kernel may reach another device: no remote copies, remote signals or barrier semaphores. Data moves between devices by JAX's collectives and lax.ppermute only.
A program may use at most 64 MiB of HBM per device.

v0:
```python
import jax
import jax.numpy as jnp
from jax import lax
from jax.sharding import PartitionSpec as P

BLOCK = 64


highest = lax.Precision.HIGHEST


def from_behind(block, axis, distance):
    devices = range(lax.axis_size(axis))
    route = [(i - distance, i) for i in devices if i - distance in devices]
    return lax.ppermute(block, axis, route)


def entering_2(part, axis, combine, identity, reverse):
    count = lax.axis_size(axis)
    place = lax.axis_index(axis)
    ahead = count - 1 - place if reverse else place
    gathered = jax.tree.map(lambda a: lax.all_gather(a, axis), part)
    state = jax.tree.map(lambda a, e: jnp.zeros_like(a) + jnp.asarray(e, a.dtype), part, identity)

    def one(lap, state):
        source = count - 1 - lap if reverse else lap
        return combine(
            state, jax.tree.map(lambda a: lax.dynamic_index_in_dim(a, source, 0, False), gathered)
        )

    return lax.fori_loop(0, ahead, one, state)


def neighbours(matrix, blocks):
    total = matrix.shape[-2]
    rows = total // blocks
    leading = matrix.shape[:-2]
    padded = jnp.pad(matrix, [(0, 0)] * len(leading) + [(rows, rows), (0, 0)])
    shifted = [
        padded[..., offset * rows : offset * rows + total, :].reshape(
            leading + (blocks, rows, matrix.shape[-1])
        )
        for offset in range(3)
    ]
    return jnp.concatenate(shifted, axis=-2)


def band_apply(panels, matrix):
    gathered = neighbours(matrix, panels.shape[-3])
    result = jnp.einsum("...ibc,...icw->...ibw", panels, gathered, precision=highest)
    return result.reshape(matrix.shape)


def band_transpose(panels, matrix):
    blocks = panels.shape[-3]
    rows = panels.shape[-2]
    leading = matrix.shape[:-2]
    split_rows = matrix.reshape(leading + (blocks, rows, matrix.shape[-1]))
    contrib = jnp.einsum("...ibc,...ibw->...icw", panels, split_rows, precision=highest)
    summed = 0.0
    for offset in range(3):
        piece = contrib[..., offset * rows : (offset + 1) * rows, :]
        summed = summed + jnp.pad(
            piece, [(0, 0)] * len(leading) + [(offset, 2 - offset), (0, 0), (0, 0)]
        )
    return summed[..., 1 : blocks + 1, :, :].reshape(matrix.shape)


def compose(earlier, later):
    matrix = jnp.dot(later[0], earlier[0], precision=highest)
    vector = jnp.dot(later[0], earlier[1], precision=highest) + later[1]
    return (matrix, vector)


def shards(dynamics, band, observed, obs_mask, filter_gain, smooth_gain):
    steps = dynamics.shape[0]
    rows = BLOCK
    blocks = lax.axis_size("state")
    state_dim = rows * blocks
    lower = jnp.broadcast_to(band[:, :, 0:1].astype(jnp.float32), (steps, 1, rows))
    upper = jnp.broadcast_to(band[:, :, 1:2].astype(jnp.float32), (steps, 1, rows))
    factor = jnp.concatenate([lower, jnp.ones_like(lower), upper], axis=2)
    panels = dynamics.reshape(steps, rows, 3 * rows) * factor
    weight = obs_mask.astype(jnp.float32) * filter_gain
    drive = weight * observed
    ahead = from_behind(panels[0:1], "tm", -1)
    every, weight_all, drive_all, smooth_all = (
        lax.all_gather(jnp.concatenate([panels, ahead], axis=0), "state", axis=1, tiled=True),
        lax.all_gather(weight, "state", axis=1, tiled=True),
        lax.all_gather(drive, "state", axis=1, tiled=True),
        lax.all_gather(smooth_gain, "state", axis=1, tiled=True),
    )
    every = every.reshape(steps + 1, blocks, rows, 3 * rows)
    current = every[:steps]
    following = every[1:]
    keep_all = 1.0 - weight_all
    column = lax.axis_index("state") * rows
    identity_full = jnp.eye(state_dim, dtype=jnp.float32)
    zero_vec = jnp.zeros((state_dim,), jnp.float32)
    start_cols = lax.dynamic_slice_in_dim(identity_full, column, rows, 1)

    def forward(carry, inputs):
        matrix, vector = carry
        step_panels, step_keep, step_drive = inputs
        matrix = step_keep[:, None] * band_apply(step_panels, matrix)
        vector = step_keep * band_apply(step_panels, vector[:, None])[:, 0] + step_drive
        return ((matrix, vector), (matrix, vector))

    (summary, leave_vec), (prefixes, partials) = lax.scan(
        forward, (start_cols, zero_vec), (current, keep_all, drive_all)
    )
    summary = lax.all_gather(summary, "state", axis=1, tiled=True)
    entering = entering_2((summary, leave_vec), "tm", compose, (identity_full, zero_vec), False)[1]
    local_enter = lax.dynamic_slice_in_dim(entering, column, rows, 0)
    filtered_all = partials + lax.psum(
        jnp.einsum("tsw,w->ts", prefixes, local_enter, precision=highest), "state"
    )
    pushed = band_apply(following, filtered_all[..., None])
    offsets = filtered_all - smooth_all * band_transpose(following, pushed)[..., 0]

    def backward(carry, inputs):
        matrix, vector = carry
        step_panels, step_gain, step_offset = inputs
        matrix = step_gain[:, None] * band_transpose(step_panels, matrix)
        vector = step_gain * band_transpose(step_panels, vector[:, None])[:, 0] + step_offset
        return ((matrix, vector), (matrix, vector))

    (back_summary, back_vec), (suffixes, back_partials) = lax.scan(
        backward, (start_cols, zero_vec), (following, smooth_all, offsets), reverse=True
    )
    back_summary = lax.all_gather(back_summary, "state", axis=1, tiled=True)
    after = entering_2((back_summary, back_vec), "tm", compose, (identity_full, zero_vec), True)[1]
    filtered_own = lax.dynamic_slice_in_dim(filtered_all, column, rows, 1)
    local_after = lax.dynamic_slice_in_dim(after, column, rows, 0)
    smooth_terms = jnp.einsum("tsw,w->ts", suffixes, local_after, precision=highest)
    smoothed_own = lax.dynamic_slice_in_dim(back_partials, column, rows, 1) + lax.psum_scatter(
        smooth_terms, "state", scatter_dimension=1, tiled=True
    )
    return (filtered_own, smoothed_own)


def solution(mesh):
    in_specs = (
        P("tm", "state"),
        P("tm", "state", None),
        P("tm", "state"),
        P("tm", "state"),
        P("tm", "state"),
        P("tm", "state"),
    )
    out_specs = (P("tm", "state"), P("tm", "state"))
    return jax.shard_map(shards, mesh=mesh, in_specs=in_specs, out_specs=out_specs, check_vma=False)
```

profile of v0, /device:TPU:0, one launch (start us, length us, event | category | flops | bytes accessed | tf_op | source)
XLA Modules:
  0.0 495.7 jit_solution(15058667124394403904)
XLA Ops:
  8.0 1.6 reshape.241
  10.0 1.3 collective-permute-start
  11.3 1.8 collective-permute-done
  14.5 13.2 %all-gather.4 = f32[4,64,16]{1,2,0:T(8,128)S(1)} all-gather(f32[1,64,16]{1,2,0:T(8,128)S(1)} %get-tuple-element.587), channel_id=1, replica_groups=mesh['tm'=32,'state'=4] {'state'}, dimensions={0}, use_global_device_ids=true | all-gather | bytes 20480 | tf_op jit(solution)/shard_map/all_gather | solution.py:89
  27.8 11.9 %all-gather.5 = f32[4,64,16]{1,2,0:T(8,128)S(1)} all-gather(f32[1,64,16]{1,2,0:T(8,128)S(1)} %get-tuple-element.586), channel_id=1, replica_groups=mesh['tm'=32,'state'=4] {'state'}, dimensions={0}, use_global_device_ids=true | all-gather | bytes 20480 | tf_op jit(solution)/shard_map/all_gather | solution.py:90
  39.9 31.6 %all-gather.13.cloned.1.call-done = f32[17,256,192]{2,1,0:T(8,128)} async-done(((f32[17,64,192]{2,1,0:T(8,128)}), f32[17,256,192]{2,1,0:T(8,128)}) %all-gather.13.cloned.1.call-update) | async-done | bytes 3342352 | tf_op jit(solution)/shard_map/all_gather | solution.py:88
  71.5 7.6 %fusion.46 = (f32[16,256,192]{2,1,0:T(8,128)}, f32[16,256,192]{2,1,0:T(8,128)}) fusion(f32[17,256,192]{2,1,0:T(8,128)} %all-gather.13.cloned.1.call-done), kind=kLoop, calls=%fused_computation.93 | loop fusion | bytes 12582912 | tf_op jit(solution)/shard_map/slice | solution.py:95
  79.1 62.9 %while.68 = (s32[]{:T(128)}, f32[256,64]{1,0:T(8,128)S(1)}, f32[256]{0:T(256)S(1)}, f32[16,256,64]{2,1,0:T(8,128)S(1)}, f32[16,256]{1,0:T(8,128)S(1)}, /*index=5...) while((s32[]{:T(128)}, f32[256,64]{1,0:T(8,128)S(1)}, ...), condition=%wide.region_1.2_spmd.clone, body=%wide.region_0.1_spmd.clone.sunk | while | flops 38472448 | bytes 1810555 | solution.py:109
  79.5 1.3 fusion.91
  81.3 1.4 fusion.89
  83.5 1.3 fusion.91
  85.2 1.4 fusion.89
  87.4 1.3 fusion.91
  89.1 1.4 fusion.89
  91.3 1.3 fusion.91
  93.0 1.4 fusion.89
  95.2 1.3 fusion.91
  97.0 1.4 fusion.89
  99.2 1.3 fusion.91
  100.9 1.4 fusion.89
  103.1 1.3 fusion.91
  104.8 1.4 fusion.89
  107.1 1.3 fusion.91
  108.8 1.4 fusion.89
  112.7 1.4 fusion.89
  116.6 1.4 fusion.89
  120.6 1.4 fusion.89
  124.5 1.4 fusion.89
  128.4 1.4 fusion.89
  132.4 1.4 fusion.89
  136.3 1.4 fusion.89
  140.2 1.4 fusion.89
  142.1 13.3 %all_gather.45 = f32[256,256]{0,1:T(8,128)} all-gather(f32[256,64]{0,1:T(8,128)S(1)} %copy.54), channel_id=1, replica_groups=mesh['tm'=32,'state'=4] {'state'}, dimensions={1}, use_global_device_ids=true | all-gather | bytes 327680 | tf_op jit(solution)/shard_map/all_gather | solution.py:112
  155.5 11.9 %all-gather.7 = f32[4,64,16]{1,2,0:T(8,128)S(1)} all-gather(f32[1,64,16]{1,2,0:T(8,128)S(1)} %bitcast.231), channel_id=1, replica_groups=mesh['tm'=32,'state'=4] {'state'}, dimensions={0}, use_global_device_ids=true | all-gather | bytes 20480 | tf_op jit(solution)/shard_map/all_gather | solution.py:91
  167.5 24.2 %all-gather.6 = f32[32,1,256]{2,1,0:T(1,128)S(1)} all-gather(f32[1,1,256]{2,1,0:T(1,128)S(1)} %bitcast.225), channel_id=3, replica_groups=mesh['tm'=32,'state'=4] {'tm'}, dimensions={0}, use_global_device_ids=true | all-gather | bytes 33792 | tf_op jit(solution)/shard_map/all_gather | solution.py:22
  191.6 22.9 %all-gather.15.cloned.1.call-done = f32[8192,256]{0,1:T(8,128)} async-done(((f32[256,256]{0,1:T(8,128)}), f32[8192,256]{0,1:T(8,128)}) %all-gather.15.cloned.1.call-update) | async-done | bytes 8388624 | tf_op jit(solution)/shard_map/all_gather | solution.py:22
  214.6 9.0 %copy.68 = f32[8192,256]{1,0:T(8,128)} copy(f32[8192,256]{0,1:T(8,128)} %all-gather.15.cloned.1.call-done) | data formatting | bytes 16777216 | tf_op jit(solution)/shard_map/while | solution.py:31
  223.5 1.9 fusion.40
  225.5 17.1 %psum.7 = f32[16,256]{1,0:T(8,128)S(1)} all-reduce(f32[16,256]{1,0:T(8,128)S(1)} %bitcast.221), channel_id=1, replica_groups=mesh['tm'=32,'state'=4] {'state'}, use_global_device_ids=true, to_apply=%region_4.5 | all-reduce | flops 4096 | bytes 32768 | tf_op jit(solution)/shard_map/psum | solution.py:115
  243.0 6.0 %convolution_bitcast_fusion = f32[16,4,64,1]{2,3,1,0:T(1,128)S(1)} fusion(f32[16,4,64,192]{3,2,1,0:T(8,128)} %bitcast.190, f32[16,4,192,1]{2,1,0,3:T(4,128)S(1)} %pad_maximum_fusion.2), kind=kOutput, calls=%fused_computation.61 | convolution fusion | flops 9437184 | bytes 3211264 | tf_op jit(solution)/shard_map/...ibc,...icw->...ibw/dot_general | solution.py:50
  249.1 2.3 fusion.48
  251.8 57.7 %while.69 = (s32[]{:T(128)}, f32[256,64]{0,1:T(8,128)S(1)}, f32[256]{0:T(256)S(1)}, f32[16,256,64]{1,2,0:T(8,128)S(1)}, f32[16,256]{1,0:T(8,128)S(1)}, /*index=5...) while((s32[]{:T(128)}, f32[256,64]{0,1:T(8,128)S(1)}, ...), condition=%wide.region_6.7_spmd.clone, body=%wide.region_5.6_spmd.clone.sunk | while | flops 38406144 | bytes 2273943 | solution.py:128
  253.4 1.3 fusion.97
  257.0 1.3 fusion.97
  260.6 1.3 fusion.97
  264.2 1.3 fusion.97
  267.8 1.3 fusion.97
  271.4 1.3 fusion.97
  275.0 1.3 fusion.97
  278.6 1.3 fusion.97
  282.2 1.3 fusion.97
  285.8 1.3 fusion.97
  289.4 1.3 fusion.97
  293.0 1.3 fusion.97
  296.6 1.3 fusion.97
  300.2 1.3 fusion.97
  303.9 1.3 fusion.97
  307.5 1.3 fusion.97
  309.4 13.0 %all_gather.51 = f32[256,256]{0,1:T(8,128)} all-gather(f32[256,64]{0,1:T(8,128)S(1)} %get-tuple-element.405), channel_id=1, replica_groups=mesh['tm'=32,'state'=4] {'state'}, dimensions={1}, use_global_device_ids=true | all-gather | bytes 327680 | tf_op jit(solution)/shard_map/all_gather | solution.py:131
  322.5 61.2 %all-gather.8 = f32[32,1,256]{2,1,0:T(1,128)S(1)} all-gather(f32[1,1,256]{2,1,0:T(1,128)S(1)} %bitcast.224), channel_id=5, replica_groups=mesh['tm'=32,'state'=4] {'tm'}, dimensions={0}, use_global_device_ids=true | all-gather | bytes 33792 | tf_op jit(solution)/shard_map/all_gather | solution.py:22
  383.7 35.2 %all-gather.17.cloned.1.call-done = f32[8192,256]{0,1:T(8,128)} async-done(((f32[256,256]{0,1:T(8,128)}), f32[8192,256]{0,1:T(8,128)}) %all-gather.17.cloned.1.call-update) | async-done | bytes 8388624 | tf_op jit(solution)/shard_map/all_gather | solution.py:22
  418.9 9.0 %copy.69 = f32[8192,256]{1,0:T(8,128)} copy(f32[8192,256]{0,1:T(8,128)} %all-gather.17.cloned.1.call-done) | data formatting | bytes 16777216 | tf_op jit(solution)/shard_map/while | solution.py:31
  427.9 41.1 %while.67 = (s32[]{:T(128)}, f32[256]{0:T(256)S(1)}, s32[]{:T(128)}, f32[32,256,256]{2,1,0:T(8,128)}, f32[32,256]{1,0:T(8,128)S(1)}, /*index=5*/s32[]{:T(128)}, s32[]{:T(128)}, s32[]{:T(128)}, s32[]{:T(128)}) while((s32[]{:T(128)}, f32[256]{0:T(256)S(1)}, s32[]{:T(128)}, f32[32,256,256]{2,1,0:T(8,128)}, f32[32,256]{1,0:T(8,128)S(1)}, ...), condition=%wide.region_8.9_spmd, body=%wide.region_7.8_spmd.sunk | while | flops 786694 | bytes 269459 | solution.py:31
  471.2 16.5 %reduce-scatter.4.cloned.1.call-done = f32[64,16]{1,0:T(8,128)} async-done(((f32[256,16]{1,0:T(8,128)}), f32[64,16]{1,0:T(8,128)}) %reduce-scatter.4.cloned.1.call-update) | async-done | bytes 4112
  (759 shorter events, 110.8 us)
Async XLA Ops:
  7.2 7.3 %copy-start.1 = (f32[16,64]{1,0:T(8,128)S(1)}, f32[16,64]{1,0:T(8,128)}, u32[]{:S(2)}) copy-start(f32[16,64]{1,0:T(8,128)} %param.16) | copy-start | bytes 12292
  7.2 7.3 %copy-start.3 = (s32[16,64]{1,0:T(8,128)S(1)}, s32[16,64]{1,0:T(8,128)}, u32[]{:S(2)}) copy-start(s32[16,64]{1,0:T(8,128)} %param.17) | copy-start | bytes 12292
  7.2 7.3 %copy-start.2 = (f32[16,64]{1,0:T(8,128)S(1)}, f32[16,64]{1,0:T(8,128)}, u32[]{:S(2)}) copy-start(f32[16,64]{1,0:T(8,128)} %param.18) | copy-start | bytes 12292
  7.2 64.3 %all-gather.13.cloned.1.call-start = ((), (), s32[]{:S(2)}) async-start(), calls=%async_computation.1 | async-start | bytes 5570560 | tf_op jit(solution)/shard_map/all_gather | solution.py:88
  10.0 3.1 collective-permute-start
  14.3 200.3 %all-gather.15.cloned.1.call-start = ((), (), s32[]{:S(2)}) async-start(), calls=%async_computation.2 | async-start | bytes 8650752 | tf_op jit(solution)/shard_map/all_gather | solution.py:22
  79.1 76.3 %copy-start.4 = (f32[16,64]{1,0:T(8,128)S(1)}, f32[16,64]{1,0:T(8,128)}, u32[]{:S(2)}) copy-start(f32[16,64]{1,0:T(8,128)} %param.19) | copy-start | bytes 12292
  155.4 263.5 %all-gather.17.cloned.1.call-start = ((), (), s32[]{:S(2)}) async-start(), calls=%async_computation.3 | async-start | bytes 8650752 | tf_op jit(solution)/shard_map/all_gather | solution.py:22
  242.9 6.2 %copy-start = (f32[16,256,192]{2,1,0:T(8,128)S(1)}, f32[16,256,192]{2,1,0:T(8,128)}, u32[]{:S(2)}) copy-start(f32[16,256,192]{2,1,0:T(8,128)} %get-tuple-element.579) | copy-start | bytes 9437188
  322.5 165.2 %reduce-scatter.4.cloned.1.call-start = ((), (), s32[]{:S(2)}) async-start(), calls=%async_computation.4 | async-start | bytes 163840
Sparse Core Ops, SparseCore 0:
  14.4 57.0 all-gather.12
  155.5 59.0 all-gather.14
  322.6 96.2 all-gather.16
  470.6 17.0 reduce-scatter.3
where the time goes:
time: 499 us; the launch traced here: 496 us
  blocking collectives  166 us (33%)
  matrix products  133 us (27%)
  waiting for transfers between devices  108 us (22%)
  local copies, waits for them, and re-layouts  60.3 us (12%)
  between operations  14 us (3%)
  other arithmetic  9.04 us (2%)
    all_gather x2, blocking collectives, entering_2(): gathered = jax.tree.map(lambda a: lax.all_gather(a, axis), part)  85.3 us
    all_gather x2, waiting for transfers between devices, entering_2(): gathered = jax.tree.map(lambda a: lax.all_gather(a, axis), part)  58.1 us
    dot_general x33, matrix products, band_apply(): jnp.einsum('...ibc,...icw->...ibw', panels, gathered, precision=highest)  49.5 us
    dot_general x33, matrix products, band_transpose(): jnp.einsum('...ibc,...ibw->...icw', panels, split_rows, precision=highest)  42.7 us
    dot_general x31, matrix products, compose(): vector = jnp.dot(later[0], earlier[1], precision=highest) + later[1]  38.4 us
    all_gather x1, waiting for transfers between devices, shards(): lax.all_gather(jnp.concatenate([panels, ahead], axis=0), 'state', axis=1,...  31.6 us
    while x2, local copies, waits for them, and re-layouts, entering_2(): return lax.fori_loop(0, ahead, one, state)  18 us
    psum x1, blocking collectives, shards(): lax.psum(jnp.einsum('tsw,w->ts', prefixes, local_enter, precision=highest...  17.1 us
  transfers between devices with their start and end apart: 5, of which 5 were waited for; matrix products, arithmetic and copies ran while one was open for 0% of the time, Pallas kernels for 0%

commit v1 on v0

v1 whole, which is shorter than its diff:
```python
import jax
import jax.numpy as jnp
from jax import lax
from jax.experimental import pallas as pl
from jax.experimental.pallas import tpu as pltpu
from jax.sharding import PartitionSpec as P

BLOCK = 64
STATE = 256
BLOCKS = 4
STEPS = 16
AUG = STATE + 8
MIB = 1 << 20

f32 = jnp.float32
bf16 = jnp.bfloat16


def split(a):
    hi = a.astype(bf16)
    return hi, (a - hi.astype(f32)).astype(bf16)


def dot_nn(a, b):
    return lax.dot_general(a, b, (((1,), (0,)), ((), ())), preferred_element_type=f32)


def dot_nt(a, b):
    return lax.dot_general(a, b, (((1,), (1,)), ((), ())), preferred_element_type=f32)


def three(dot, a, b):
    ahi, alo = a
    bhi, blo = b
    return dot(ahi, bhi) + (dot(alo, bhi) + dot(ahi, blo))


def mul_nn(a, b):
    return three(dot_nn, split(a), split(b))


def mul_nt(a, b):
    return three(dot_nt, split(a), split(b))


def first_row(row):
    spread = jnp.broadcast_to(row, (8, row.shape[1]))
    return jnp.where(lax.broadcasted_iota(jnp.int32, spread.shape, 0) == 0, spread, 0.0)


def identity_matrix():
    rows = lax.broadcasted_iota(jnp.int32, (STATE, STATE), 0)
    cols = lax.broadcasted_iota(jnp.int32, (STATE, STATE), 1)
    return jnp.where(rows == cols, 1.0, 0.0).astype(f32)


def call(kernel, outs, args, scratch=(), limit=40, flops=0):
    vmem = pl.BlockSpec(memory_space=pltpu.VMEM)
    smem = pl.BlockSpec(memory_space=pltpu.SMEM)
    moved = sum(a.size * a.dtype.itemsize for a in args) + sum(
        o.size * o.dtype.itemsize for o in outs
    )
    return pl.pallas_call(
        kernel,
        out_shape=outs,
        in_specs=[smem if a.size < 8 else vmem for a in args],
        out_specs=[vmem] * len(outs),
        scratch_shapes=list(scratch),
        compiler_params=pltpu.CompilerParams(vmem_limit_bytes=limit * MIB),
        cost_estimate=pl.CostEstimate(flops=flops, bytes_accessed=moved, transcendentals=0),
    )(*args)


def arr(*shape, dtype=f32):
    return jax.ShapeDtypeStruct(shape, dtype)


NA = BLOCK * STEPS
NB = NA // 2
PACKED = NA + NB + 2 * STEPS


def pack_kernel(dyn_ref, lower_ref, upper_ref, obs_ref, mask_ref, fgain_ref, sgain_ref, out_ref):
    lower, upper = lower_ref[...], upper_ref[...]
    half = BLOCK // 2
    wide = 3 * BLOCK
    for r in range(BLOCK):
        before = dyn_ref[:, r * wide : r * wide + BLOCK] * lower
        own = dyn_ref[:, r * wide + BLOCK : r * wide + 2 * BLOCK]
        out_ref[r * STEPS : (r + 1) * STEPS, :] = jnp.concatenate([before, own], axis=1)
    for r in range(half):
        s = r + half
        near = dyn_ref[:, r * wide + 2 * BLOCK : (r + 1) * wide] * upper
        far = dyn_ref[:, s * wide + 2 * BLOCK : (s + 1) * wide] * upper
        out_ref[NA + r * STEPS : NA + (r + 1) * STEPS, :] = jnp.concatenate([near, far], axis=1)
    weight = mask_ref[...].astype(f32) * fgain_ref[...]
    drive = weight * obs_ref[...]
    gain = sgain_ref[...]
    out_ref[NA + NB : NA + NB + STEPS, :] = jnp.concatenate([weight, drive], axis=1)
    out_ref[NA + NB + STEPS :, :] = jnp.concatenate([gain, gain], axis=1)


def forward_kernel(pos_ref, m0, m1, m2, m3, fhi_ref, flo_ref, vec_ref, x_ref):
    place = pos_ref[0]
    zeros64 = jnp.zeros((BLOCK, BLOCK), f32)
    vec_w = vec_d = vec_g = None
    for s, m in enumerate((m0, m1, m2, m3)):
        block = lax.rem(place - s + BLOCKS, BLOCKS)
        shift = lax.rem(block + BLOCKS - 1, BLOCKS) * BLOCK
        rows = pl.ds(pl.multiple_of(block * BLOCK, BLOCK), BLOCK)
        for t in range(STEPS):
            left = m[pl.ds(t, BLOCK, stride=STEPS), :]
            pair = m[pl.ds(NA + t, BLOCK // 2, stride=STEPS), :]
            after = jnp.concatenate([pair[:, :BLOCK], pair[:, BLOCK:]], axis=0)
            full = jnp.concatenate([left, after, zeros64], axis=1)
            hi, lo = split(pltpu.roll(full, shift, 1))
            fhi_ref[t, rows, :] = hi
            flo_ref[t, rows, :] = lo
        wd = m[NA + NB : NA + NB + STEPS, :]
        g = m[NA + NB + STEPS :, :]
        zero = jnp.zeros((STEPS, STATE - BLOCK), f32)
        place_at = block * BLOCK
        w_part = pltpu.roll(jnp.concatenate([wd[:, :BLOCK], zero], axis=1), place_at, 1)
        d_part = pltpu.roll(jnp.concatenate([wd[:, BLOCK:], zero], axis=1), place_at, 1)
        g_part = pltpu.roll(jnp.concatenate([g[:, :BLOCK], zero], axis=1), place_at, 1)
        vec_w = w_part if vec_w is None else vec_w + w_part
        vec_d = d_part if vec_d is None else vec_d + d_part
        vec_g = g_part if vec_g is None else vec_g + g_part
    vec_ref[0] = vec_w
    vec_ref[1] = vec_d
    vec_ref[2] = vec_g
    state = jnp.concatenate([identity_matrix(), jnp.zeros((8, STATE), f32)], axis=0)
    for t in range(STEPS):
        state = three(dot_nt, split(state), (fhi_ref[t], flo_ref[t])) * (1.0 - vec_w[t : t + 1])
        state = jnp.concatenate(
            [state[:STATE], state[STATE:] + first_row(vec_d[t : t + 1])], axis=0
        )
    x_ref[...] = state


def composite_kernel(fhi_ref, flo_ref, vec_ref, y_ref, z_ref):
    x = jnp.concatenate([identity_matrix(), jnp.zeros((8, STATE), f32)], axis=0)
    y = identity_matrix()
    z = jnp.zeros((AUG, STATE), f32)
    for t in range(STEPS):
        w, d, g = vec_ref[0, t : t + 1, :], vec_ref[1, t : t + 1, :], vec_ref[2, t : t + 1, :]
        step = (fhi_ref[t], flo_ref[t])
        moved = three(dot_nt, split(x), step)
        back = three(dot_nt, split(y), step)
        drive = first_row(d)
        kept = moved * (1.0 - w)
        taken = -(moved * w)
        x = jnp.concatenate([kept[:STATE], kept[STATE:] + drive], axis=0)
        right = jnp.concatenate([taken[:STATE], taken[STATE:] + drive], axis=0)
        z = z + mul_nt(right, back)
        y = back * g
    y_ref[...] = y
    z_ref[...] = z


def then(first, second):
    both = mul_nn(first, second[:STATE])
    return jnp.concatenate([both[:STATE], both[STATE:] + second[STATE:]], axis=0)


def pair_forward_kernel(pos_ref, own_ref, other_ref, x_ref):
    own, other = own_ref[...], other_ref[...]
    lead = pos_ref[3] == 0
    x_ref[...] = then(jnp.where(lead, own, other), jnp.where(lead, other, own))


def pair_back_kernel(pos_ref, x_own, x_other, yz_own, yz_other, y_ref, z_ref):
    lead = pos_ref[3] == 0
    xl = jnp.where(lead, x_own[...], x_other[...])
    yl = jnp.where(lead, yz_own[:STATE], yz_other[:STATE])
    yr = jnp.where(lead, yz_other[:STATE], yz_own[:STATE])
    zl = jnp.where(lead, yz_own[STATE:], yz_other[STATE:])
    zr = jnp.where(lead, yz_other[STATE:], yz_own[STATE:])
    y_ref[...] = mul_nn(yl, yr)
    inner = then(xl, zr)
    z_ref[...] = zl + mul_nt(inner, yl)


def ordered(scratch, refs, place):
    for s, ref in enumerate(refs):
        scratch[lax.rem(place - s + 4, 4)] = ref[...]


def row_forward_kernel(pos_ref, a0, a1, a2, a3, whole_ref, before_ref, scr):
    x = pos_ref[1]
    ordered(scr, (a0, a1, a2, a3), x)
    run = scr[0]
    before = jnp.concatenate([identity_matrix(), jnp.zeros((8, STATE), f32)], axis=0)
    before = jnp.where(x == 1, run, before)
    for i in range(1, 4):
        run = then(run, scr[i])
        if i < 3:
            before = jnp.where(x == i + 1, run, before)
    whole_ref[...] = run
    before_ref[...] = before


def enter_kernel(
    pos_ref, r0, r1, r2, r3, before_ref, x_own, x_other, z_chip, yz_own, yz_other,
    enter_ref, vchip_ref, mid_ref, scr,
):
    y = pos_ref[2]
    ordered(scr, (r0, r1, r2, r3), y)
    m = jnp.zeros((8, STATE), f32)
    for g in range(3):
        u = scr[g, STATE:, :]
        after = u if g == 0 else mul_nn(m, scr[g, :STATE, :]) + u
        m = jnp.where(y > g, after, m)
    m = mul_nn(m, before_ref[:STATE]) + before_ref[STATE:]
    lead = pos_ref[3] == 0
    x_lead = jnp.where(lead, x_own[...], x_other[...])
    mid = mul_nn(m, x_lead[:STATE]) + x_lead[STATE:]
    enter_ref[...] = jnp.where(lead, m, mid)
    vchip_ref[...] = mul_nn(m, z_chip[:STATE]) + z_chip[STATE:]
    z_last = jnp.where(lead, yz_other[STATE:], yz_own[STATE:])
    mid_ref[...] = mul_nn(mid, z_last[:STATE]) + z_last[STATE:]


def row_back_kernel(pos_ref, y0, y1, y2, y3, whole_ref, after_ref, scr):
    x = pos_ref[1]
    ordered(scr, (y0, y1, y2, y3), x)
    run = scr[3]
    after = jnp.where(x == 2, run, identity_matrix())
    for i in (2, 1, 0):
        run = mul_nn(scr[i], run)
        if i > 0:
            after = jnp.where(x == i - 1, run, after)
    whole_ref[...] = run
    after_ref[...] = after


def row_v_kernel(pos_ref, v0, v1, v2, v3, y0, y1, y2, y3, whole_ref, after_ref, vscr, yscr):
    x = pos_ref[1]
    ordered(vscr, (v0, v1, v2, v3), x)
    ordered(yscr, (y0, y1, y2, y3), x)
    run = vscr[3]
    after = jnp.where(x == 2, run, 0.0)
    for i in (2, 1, 0):
        run = vscr[i] + mul_nt(run, yscr[i])
        if i > 0:
            after = jnp.where(x == i - 1, run, after)
    whole_ref[...] = run
    after_ref[...] = after


def local_kernel(enter_ref, fhi_ref, flo_ref, vec_ref, m_ref, e_ref):
    m = enter_ref[...]
    for t in range(STEPS):
        w, d = vec_ref[0, t : t + 1, :], vec_ref[1, t : t + 1, :]
        p = three(dot_nt, split(m), (fhi_ref[t], flo_ref[t]))
        e = first_row(d) - w * p
        m = p + e
        m_ref[t : t + 1, :] = m[0:1]
        e_ref[t : t + 1, :] = e[0:1]


def smooth_kernel(
    pos_ref, v0, v1, v2, v3, y0, y1, y2, y3, yafter_ref, vafter_ref, yz_other, mid_ref,
    fhi_ref, flo_ref, vec_ref, m_ref, e_ref, filt_ref, smooth_ref, vscr, yscr,
):
    place = pos_ref[0]
    y = pos_ref[2]
    ordered(vscr, (v0, v1, v2, v3), y)
    ordered(yscr, (y0, y1, y2, y3), y)
    sigma = jnp.zeros((8, STATE), f32)
    for g in (3, 2, 1):
        after = vscr[g] if g == 3 else mul_nt(sigma, yscr[g]) + vscr[g]
        sigma = jnp.where(y < g, after, sigma)
    sigma = mul_nt(sigma, yafter_ref[...]) + vafter_ref[...]
    crossed = mul_nt(sigma, yz_other[:STATE]) + mid_ref[...]
    sigma = jnp.where(pos_ref[3] == 0, crossed, sigma)
    rows = [None] * STEPS
    for t in range(STEPS - 1, -1, -1):
        q = vec_ref[2, t : t + 1, :] * sigma
        rows[t] = m_ref[t : t + 1, :] + q[0:1]
        if t > 0:
            sigma = three(
                dot_nn, split(q + first_row(e_ref[t : t + 1, :])), (fhi_ref[t], flo_ref[t])
            )
    smooth = jnp.concatenate(rows, axis=0)
    filt = m_ref[...]
    out_f = filt[:, :BLOCK]
    out_s = smooth[:, :BLOCK]
    for b in range(1, BLOCKS):
        part = slice(b * BLOCK, (b + 1) * BLOCK)
        out_f = jnp.where(place == b, filt[:, part], out_f)
        out_s = jnp.where(place == b, smooth[:, part], out_s)
    filt_ref[...] = out_f
    smooth_ref[...] = out_s


def over_z(a, s):
    return lax.ppermute(a, "state", [(i, (i + s) % 4) for i in range(4)])


def over_core(a):
    return lax.ppermute(a, "tm", [(i, i ^ 1) for i in range(32)])


def chip(x, y, c):
    return (y * 4 + x) * 2 + c


CHIPS = [(x, y, c) for y in range(4) for x in range(4) for c in range(2)]


def over_x(a, s):
    return lax.ppermute(a, "tm", [(chip(x, y, c), chip((x + s) % 4, y, c)) for x, y, c in CHIPS])


def over_y(a, s):
    return lax.ppermute(a, "tm", [(chip(x, y, c), chip(x, (y + s) % 4, c)) for x, y, c in CHIPS])


def gather(move, a):
    return [a] + [move(a, s) for s in (1, 2, 3)]


def shards(dynamics, band, observed, obs_mask, filter_gain, smooth_gain):
    z = lax.axis_index("state")
    tm = lax.axis_index("tm")
    pos = jnp.stack([z, (tm // 2) % 4, tm // 8, tm % 2]).astype(jnp.int32)
    lower = jnp.where(z > 0, band[:, :, 0], 0).astype(f32)
    upper = jnp.where(z < BLOCKS - 1, band[:, :, 1], 0).astype(f32)
    (packed,) = call(
        pack_kernel,
        [arr(PACKED, 128)],
        [dynamics, lower, upper, observed, obs_mask, filter_gain, smooth_gain],
    )
    parts = gather(over_z, packed)
    fhi, flo, vec, x_own = call(
        forward_kernel,
        [arr(STEPS, STATE, STATE, dtype=bf16)] * 2 + [arr(3, STEPS, STATE), arr(AUG, STATE)],
        [pos] + parts,
    )
    x_other = over_core(x_own)
    (x_chip,) = call(pair_forward_kernel, [arr(AUG, STATE)], [pos, x_own, x_other])
    x_chips = gather(over_x, x_chip)
    y_own, z_own = call(
        composite_kernel, [arr(STATE, STATE), arr(AUG, STATE)], [fhi, flo, vec]
    )
    yz_own = jnp.concatenate([y_own, z_own], axis=0)
    yz_other = over_core(yz_own)
    y_chip, z_chip = call(
        pair_back_kernel,
        [arr(STATE, STATE), arr(AUG, STATE)],
        [pos, x_own, x_other, yz_own, yz_other],
    )
    x_row, x_before = call(
        row_forward_kernel,
        [arr(AUG, STATE)] * 2,
        [pos] + x_chips,
        [pltpu.VMEM((4, AUG, STATE), f32)],
    )
    x_rows = gather(over_y, x_row)
    y_chips = gather(over_x, y_chip)
    enter, v_chip, v_mid = call(
        enter_kernel,
        [arr(8, STATE)] * 3,
        [pos] + x_rows + [x_before, x_own, x_other, z_chip, yz_own, yz_other],
        [pltpu.VMEM((4, AUG, STATE), f32)],
    )
    v_chips = gather(over_x, v_chip)
    y_row, y_after = call(
        row_back_kernel,
        [arr(STATE, STATE)] * 2,
        [pos] + y_chips,
        [pltpu.VMEM((4, STATE, STATE), f32)],
    )
    y_rows = gather(over_y, y_row)
    m_all, e_all = call(local_kernel, [arr(STEPS, STATE)] * 2, [enter, fhi, flo, vec])
    v_row, v_after = call(
        row_v_kernel,
        [arr(8, STATE)] * 2,
        [pos] + v_chips + y_chips,
        [pltpu.VMEM((4, 8, STATE), f32), pltpu.VMEM((4, STATE, STATE), f32)],
    )
    v_rows = gather(over_y, v_row)
    filtered, smoothed = call(
        smooth_kernel,
        [arr(STEPS, BLOCK)] * 2,
        [pos] + v_rows + y_rows + [y_after, v_after, yz_other, v_mid, fhi, flo, vec, m_all, e_all],
        [pltpu.VMEM((4, 8, STATE), f32), pltpu.VMEM((4, STATE, STATE), f32)],
    )
    return filtered, smoothed


def solution(mesh):
    in_specs = (
        P("tm", "state"),
        P("tm", "state", None),
        P("tm", "state"),
        P("tm", "state"),
        P("tm", "state"),
        P("tm", "state"),
    )
    out_specs = (P("tm", "state"), P("tm", "state"))
    return jax.shard_map(shards, mesh=mesh, in_specs=in_specs, out_specs=out_specs, check_vma=False)
```

time: 499 us -> 133 us (0.27)
  blocking collectives: 166 us -> 0 us
  matrix products: 133 us -> 0 us
  local copies, waits for them, and re-layouts: 60.3 us -> 4.13 us
  waiting for transfers between devices: 108 us -> 67.2 us
  Pallas kernels: 0 us -> 30.2 us
  starting transfers between devices: 1.46 us -> 29.1 us
  between operations: 14 us -> 0.78 us
  other arithmetic: 9.04 us -> 0.84 us
    all_gather x7 -> x0, blocking collectives: 149 us -> none  [the longest x2 85.3 us: entering_2(): gathered = jax.tree.map(lambda a: lax.all_gather(a, axis), part)]
    dot_general x99 -> x0, matrix products: 133 us -> none  [the longest x33 49.5 us: band_apply(): jnp.einsum('...ibc,...icw->...ibw', panels, gathered, precision=highest)]
    all_gather x3 -> x0, waiting for transfers between devices: 89.7 us -> none  [the longest x2 58.1 us: entering_2(): gathered = jax.tree.map(lambda a: lax.all_gather(a, axis), part)]
    ppermute x1 -> x23, waiting for transfers between devices: 1.85 us -> 67.2 us  [the longest x3 36.4 us: over_z(): return lax.ppermute(a, 'state', [(i, (i + s) % 4) for i in range(4)])]
    pallas_call x0 -> x11, Pallas kernels: none -> 30.2 us  [call(): pl.pallas_call(kernel, out_shape=outs, in_specs=[smem if a.size < 8 else...]
    ppermute x1 -> x23, starting transfers between devices: 1.29 us -> 29.1 us  [the longest x9 12.7 us: over_y(): lax.ppermute(a, 'tm', [(chip(x, y, c), chip(x, (y + s) % 4, c)) for x, y,...]
    reshape x212 -> x0, local copies, waits for them, and re-layouts: 21.8 us -> none  [the longest x99 8.74 us: neighbours(): padded[..., offset * rows:offset * rows + total, :]]
    while x3 -> x0, local copies, waits for them, and re-layouts: 18.1 us -> none  [the longest x2 18 us: entering_2(): return lax.fori_loop(0, ahead, one, state)]
  transfers between devices with their start and end apart: 5 -> 23, of which waited for: 5 -> 10; matrix products, arithmetic and copies ran while one was open for 0% -> 0% of each run, Pallas kernels for 0% -> 9%
where the time goes in v1:
time: 133 us; the launch traced here: 132 us
  waiting for transfers between devices  67.2 us (51%)
  Pallas kernels  30.2 us (23%)
  starting transfers between devices  29.1 us (22%)
  local copies, waits for them, and re-layouts  4.13 us (3%)
    ppermute x3, waiting for transfers between devices, over_z(): return lax.ppermute(a, 'state', [(i, (i + s) % 4) for i in range(4)])  36.4 us
    pallas_call x11, Pallas kernels, call(): pl.pallas_call(kernel, out_shape=outs, in_specs=[smem if a.size < 8 else...  30.2 us
    ppermute x9, waiting for transfers between devices, over_x(): lax.ppermute(a, 'tm', [(chip(x, y, c), chip((x + s) % 4, y, c)) for x, y,...  28.9 us
    ppermute x9, starting transfers between devices, over_y(): lax.ppermute(a, 'tm', [(chip(x, y, c), chip(x, (y + s) % 4, c)) for x, y,...  12.7 us
    ppermute x9, starting transfers between devices, over_x(): lax.ppermute(a, 'tm', [(chip(x, y, c), chip((x + s) % 4, y, c)) for x, y,...  10.4 us
    ppermute x3, starting transfers between devices, over_z(): return lax.ppermute(a, 'state', [(i, (i + s) % 4) for i in range(4)])  5.45 us
    unnamed x11, local copies, waits for them, and re-layouts  3.94 us
  transfers between devices with their start and end apart: 23, of which 10 were waited for; matrix products, arithmetic and copies ran while one was open for 0% of the time, Pallas kernels for 9%

profile of v1, /device:TPU:0, one launch (start us, length us, event | category | flops | bytes accessed | tf_op | source)
XLA Modules:
  0.0 132.2 jit_solution(3329708870925125760)
XLA Ops:
  0.6 0.8 fusion.3
  1.4 0.1 copy.9.upper_ref
  1.5 0.1 copy.8.lower_ref
  1.6 1.1 copy-done
  2.7 0.7 copy-done.1
  3.4 0.7 copy-done.2
  4.1 0.7 copy-done.3
  4.8 0.7 copy-done.4
  5.5 0.4 shard_map.77.m0
  5.9 4.2 %collective-permute-start.2 = (f32[1568,128]{1,0:T(8,128)S(1)}, f32[1568,128]{1,0:T(8,128)S(1)}, u32[]{:S(2)}, u32[]{:S(2)}) collective-permute-start(f32[1568,128]{1,0:T(8,128)S(1)} %shard_map.77.m0), channel_id=1, source_target_pairs={{0,3},{1,0},{2,1},{3,2},{4,7},{5,4},{6,5},{7,6},{8,11},{9,8},{10,9... | collective-permute-start | bytes 2408456 | tf_op jit(solution)/shard_map/ppermute | solution.py:298
  10.1 0.0 collective-permute-start.1
  10.1 1.3 collective-permute-start
  11.4 0.1 pad_add_fusion.pos_ref
  11.4 33.0 %collective-permute-done.2.m3 = f32[1568,128]{1,0:T(8,128)S(1)} collective-permute-done((f32[1568,128]{1,0:T(8,128)S(1)}, f32[1568,128]{1,0:T(8,128)S(1)}, u32[]{:S(2)}, u32[]{:S(2)}) %collective-permute-start.2) | collective-permute-done | bytes 802848 | tf_op jit(solution)/shard_map/ppermute | solution.py:298
  44.4 0.0 collective-permute-done.1.m2
  44.5 3.4 %collective-permute-done.m1 = f32[1568,128]{1,0:T(8,128)S(1)} collective-permute-done((f32[1568,128]{1,0:T(8,128)S(1)}, f32[1568,128]{1,0:T(8,128)S(1)}, u32[]{:S(2)}, u32[]{:S(2)}) %collective-permute-start) | collective-permute-done | bytes 802848 | tf_op jit(solution)/shard_map/ppermute | solution.py:298
  47.9 5.4 %shard_map.78 = (bf16[16,256,256]{2,1,0:T(8,128)(2,1)S(1)}, bf16[16,256,256]{2,1,0:T(8,128)(2,1)S(1)}, f32[3,16,256]{2,1,0:T(8,128)S(1)}, f32[264,256]{1,0:T(8,128)S(1)}) custom-call(s32[4]{0:T(128)S(1)} %pad_add_fusion.pos_ref, f32[1568,128]{1,0:T(8,128)S(1)} %shard_map.77.m0, f32[1568,128]{1,0:T(8,128)S(1)} %collective-permute-done.m1, ...), custom_call_target="tpu_custom_call" | custom-call | bytes 7725072 | tf_op jit(solution)/shard_map/pallas_call | solution.py:63
  53.3 7.3 %shard_map.81 = (f32[256,256]{1,0:T(8,128)S(1)}, f32[264,256]{1,0:T(8,128)S(1)}) custom-call(bf16[16,256,256]{2,1,0:T(8,128)(2,1)S(1)} %get-tuple-element.24.fhi_ref, bf16[16,256,256]{2,1,0:T(8,128)(2,1)S(1)} %get-tuple-element.25.flo_ref, f32[3,16,256]{2,1,0:T(8,128)S(1)} %get-tuple-element.26.vec_ref), custom_call_target="tpu_custom_call" | custom-call | bytes 4775936 | tf_op jit(solution)/shard_map/pallas_call | solution.py:63
  60.7 0.1 collective-permute-start.10
  60.8 0.5 collective-permute-start.3
  61.3 1.8 %collective-permute-done.3.other_ref.x_other = f32[264,256]{1,0:T(8,128)S(1)} collective-permute-done((f32[264,256]{1,0:T(8,128)S(1)}, f32[264,256]{1,0:T(8,128)S(1)}, u32[]{:S(2)}, u32[]{:S(2)}) %collective-permute-start.3) | collective-permute-done | bytes 270368 | tf_op jit(solution)/shard_map/ppermute | solution.py:302
  63.1 0.8 shard_map.79.a0
  63.9 3.0 %collective-permute-start.6 = (f32[264,256]{1,0:T(8,128)S(1)}, f32[264,256]{1,0:T(8,128)S(1)}, u32[]{:S(2)}, u32[]{:S(2)}) collective-permute-start(f32[264,256]{1,0:T(8,128)S(1)} %shard_map.79.a0), channel_id=1, source_target_pairs={{0,24},{4,28},{8,0},{12,4},{16,8},{20,12},{24,16},{28,20},{32,56},... | collective-permute-start | bytes 811016 | tf_op jit(solution)/shard_map/ppermute | solution.py:313
  66.9 0.8 collective-permute-start.5
  67.7 0.9 collective-permute-start.4
  68.6 0.0 collective-permute-done.10.yz_other
  68.6 1.2 shard_map.82
  69.8 2.4 %collective-permute-start.16 = (f32[256,256]{1,0:T(8,128)S(1)}, f32[256,256]{1,0:T(8,128)S(1)}, u32[]{:S(2)}, u32[]{:S(2)}) collective-permute-start(f32[256,256]{1,0:T(8,128)S(1)} %get-tuple-element.31.y0), channel_id=1, source_target_pairs={{0,24},{4,28},{8,0},{12,4},{16,8},{20,12},{24,16},{28,20},{32,56},... | collective-permute-start | bytes 786440 | tf_op jit(solution)/shard_map/ppermute | solution.py:313
  72.2 7.2 %collective-permute-done.6.a3 = f32[264,256]{1,0:T(8,128)S(1)} collective-permute-done((f32[264,256]{1,0:T(8,128)S(1)}, f32[264,256]{1,0:T(8,128)S(1)}, u32[]{:S(2)}, u32[]{:S(2)}) %collective-permute-start.6) | collective-permute-done | bytes 270368 | tf_op jit(solution)/shard_map/ppermute | solution.py:313
  79.4 0.0 collective-permute-done.5.a2
  79.4 3.0 %collective-permute-done.4.a1 = f32[264,256]{1,0:T(8,128)S(1)} collective-permute-done((f32[264,256]{1,0:T(8,128)S(1)}, f32[264,256]{1,0:T(8,128)S(1)}, u32[]{:S(2)}, u32[]{:S(2)}) %collective-permute-start.4) | collective-permute-done | bytes 270368 | tf_op jit(solution)/shard_map/ppermute | solution.py:313
  82.5 1.5 %shard_map.80 = (f32[264,256]{1,0:T(8,128)S(1)}, f32[264,256]{1,0:T(8,128)S(1)}) custom-call(s32[4]{0:T(128)S(1)} %pad_add_fusion.pos_ref, f32[264,256]{1,0:T(8,128)S(1)} %shard_map.79.a0, f32[264,256]{1,0:T(8,128)S(1)} %collective-permute-done.4.a1, f32[264,256]{1,0:T(8,128)S(1)} %collective-permute-done.5.a2, f32[264,256]{1,0:T(8,128)S(1)} %collective-permute-done.6.a3), custom_call_target="tpu_custom_call" | custom-call | bytes 1622032 | tf_op jit(solution)/shard_map/pallas_call | solution.py:63
  83.9 3.1 %collective-permute-start.9 = (f32[264,256]{1,0:T(8,128)S(1)}, f32[264,256]{1,0:T(8,128)S(1)}, u32[]{:S(2)}, u32[]{:S(2)}) collective-permute-start(f32[264,256]{1,0:T(8,128)S(1)} %get-tuple-element.22.r0), channel_id=1, source_target_pairs={{0,96},{4,100},{8,104},{12,108},{16,112},{20,116},{24,120},{28,124... | collective-permute-start | bytes 811016 | tf_op jit(solution)/shard_map/ppermute | solution.py:317
  87.0 0.8 collective-permute-start.15
  87.8 0.9 collective-permute-start.14
  88.7 0.6 collective-permute-start.8
  89.3 0.0 collective-permute-done.16.y3
  89.3 1.0 collective-permute-start.7
  90.3 7.5 %collective-permute-done.15.y2 = f32[256,256]{1,0:T(8,128)S(1)} collective-permute-done((f32[256,256]{1,0:T(8,128)S(1)}, f32[256,256]{1,0:T(8,128)S(1)}, u32[]{:S(2)}, u32[]{:S(2)}) %collective-permute-start.15) | collective-permute-done | bytes 262176 | tf_op jit(solution)/shard_map/ppermute | solution.py:313
  97.8 4.3 %collective-permute-done.14.y1 = f32[256,256]{1,0:T(8,128)S(1)} collective-permute-done((f32[256,256]{1,0:T(8,128)S(1)}, f32[256,256]{1,0:T(8,128)S(1)}, u32[]{:S(2)}, u32[]{:S(2)}) %collective-permute-start.14) | collective-permute-done | bytes 262176 | tf_op jit(solution)/shard_map/ppermute | solution.py:313
  102.1 1.6 %shard_map.85 = (f32[256,256]{1,0:T(8,128)S(1)}, f32[256,256]{1,0:T(8,128)S(1)}) custom-call(s32[4]{0:T(128)S(1)} %pad_add_fusion.pos_ref, f32[256,256]{1,0:T(8,128)S(1)} %get-tuple-element.31.y0, f32[256,256]{1,0:T(8,128)S(1)} %collective-permute-done.14.y1, f32[256,256]{1,0:T(8,128)S(1)} %collective-permute-done.15.y2, ...), custom_call_target="tpu_custom_call" | custom-call | bytes 1572880 | tf_op jit(solution)/shard_map/pallas_call | solution.py:63
  103.7 0.8 collective-permute-start.22
  104.5 0.3 collective-permute-start.21
  104.8 0.0 collective-permute-done.9.r3
  104.8 1.0 collective-permute-start.20
  105.8 0.0 collective-permute-done.8.r2
  105.8 0.0 collective-permute-done.7.r1
  105.8 1.5 %shard_map.83 = (f32[8,256]{1,0:T(8,128)S(1)}, f32[8,256]{1,0:T(8,128)S(1)}, f32[8,256]{1,0:T(8,128)S(1)}) custom-call(s32[4]{0:T(128)S(1)} %pad_add_fusion.pos_ref, f32[264,256]{1,0:T(8,128)S(1)} %get-tuple-element.22.r0, f32[264,256]{1,0:T(8,128)S(1)} %collective-permute-done.7.r1, f32[264,256]{1,0:T(8,128)S(1)} %collective-permute-done.8.r2, ...), custom_call_target="tpu_custom_call" | custom-call | bytes 3252240 | tf_op jit(solution)/shard_map/pallas_call | solution.py:63
  107.3 0.6 collective-permute-start.13
  107.9 1.0 collective-permute-start.12
  108.9 2.0 %collective-permute-done.13.v3 = f32[8,256]{1,0:T(8,128)S(1)} collective-permute-done((f32[8,256]{1,0:T(8,128)S(1)}, f32[8,256]{1,0:T(8,128)S(1)}, u32[]{:S(2)}, u32[]{:S(2)}) %collective-permute-start.13) | collective-permute-done | bytes 8224 | tf_op jit(solution)/shard_map/ppermute | solution.py:313
  111.0 0.0 collective-permute-start.11
  111.0 2.1 %collective-permute-done.12.v2 = f32[8,256]{1,0:T(8,128)S(1)} collective-permute-done((f32[8,256]{1,0:T(8,128)S(1)}, f32[8,256]{1,0:T(8,128)S(1)}, u32[]{:S(2)}, u32[]{:S(2)}) %collective-permute-start.12) | collective-permute-done | bytes 8224 | tf_op jit(solution)/shard_map/ppermute | solution.py:313
  113.1 2.8 %collective-permute-done.11.v1 = f32[8,256]{1,0:T(8,128)S(1)} collective-permute-done((f32[8,256]{1,0:T(8,128)S(1)}, f32[8,256]{1,0:T(8,128)S(1)}, u32[]{:S(2)}, u32[]{:S(2)}) %collective-permute-start.11) | collective-permute-done | bytes 8224 | tf_op jit(solution)/shard_map/ppermute | solution.py:313
  115.8 1.2 shard_map.84
  117.0 2.7 %collective-permute-start.19 = (f32[8,256]{1,0:T(8,128)S(1)}, f32[8,256]{1,0:T(8,128)S(1)}, u32[]{:S(2)}, u32[]{:S(2)}) collective-permute-start(f32[8,256]{1,0:T(8,128)S(1)} %get-tuple-element.32.v0), channel_id=1, source_target_pairs={{0,96},{4,100},{8,104},{12,108},{16,112},{20,116},{24,120},{28,124... | collective-permute-start | bytes 24584 | tf_op jit(solution)/shard_map/ppermute | solution.py:317
  119.7 1.6 %collective-permute-start.18 = (f32[8,256]{1,0:T(8,128)S(1)}, f32[8,256]{1,0:T(8,128)S(1)}, u32[]{:S(2)}, u32[]{:S(2)}) collective-permute-start(f32[8,256]{1,0:T(8,128)S(1)} %get-tuple-element.32.v0), channel_id=1, source_target_pairs={{0,64},{4,68},{8,72},{12,76},{16,80},{20,84},{24,88},{28,92},{32,9... | collective-permute-start | bytes 24584 | tf_op jit(solution)/shard_map/ppermute | solution.py:317
  121.3 0.0 collective-permute-done.19.v3
  121.3 1.6 %collective-permute-start.17 = (f32[8,256]{1,0:T(8,128)S(1)}, f32[8,256]{1,0:T(8,128)S(1)}, u32[]{:S(2)}, u32[]{:S(2)}) collective-permute-start(f32[8,256]{1,0:T(8,128)S(1)} %get-tuple-element.32.v0), channel_id=1, source_target_pairs={{0,32},{4,36},{8,40},{12,44},{16,48},{20,52},{24,56},{28,60},{32,6... | collective-permute-start | bytes 24584 | tf_op jit(solution)/shard_map/ppermute | solution.py:317
  122.9 4.1 %shard_map.86 = (f32[16,256]{1,0:T(8,128)S(1)}, f32[16,256]{1,0:T(8,128)S(1)}) custom-call(f32[8,256]{1,0:T(8,128)S(1)} %get-tuple-element.37.enter_ref, bf16[16,256,256]{2,1,0:T(8,128)(2,1)S(1)} %get-tuple-element.24.fhi_ref, bf16[16,256,256]{2,1,0:T(8,128)(2,1)S(1)} %get-tuple-element.25.flo_ref, f32[3,16,256]{2,1,0:T(8,128)S(1)} %get-tuple-element.26.vec_ref), custom_call_target="tpu_custom_call" | custom-call | bytes 4284416 | tf_op jit(solution)/shard_map/pallas_call | solution.py:63
  127.0 0.0 collective-permute-done.17.v1
  127.1 0.0 collective-permute-done.21.y2
  127.1 0.0 collective-permute-done.20.y1
  127.1 5.1 %shard_map.87 = (f32[16,64]{1,0:T(8,128)}, f32[16,64]{1,0:T(8,128)}) custom-call(s32[4]{0:T(128)S(1)} %pad_add_fusion.pos_ref, f32[8,256]{1,0:T(8,128)S(1)} %get-tuple-element.32.v0, f32[8,256]{1,0:T(8,128)S(1)} %collective-permute-done.17.v1, f32[8,256]{1,0:T(8,128)S(1)} %collective-permute-done.18.v2, f32[8,256]{1,0:T(8,128)S(1)} %collective-permute-done.19.v3, ...), custom_call_target="tpu_custom_call" | custom-call | bytes 6176784 | tf_op jit(solution)/shard_map/pallas_call | solution.py:63
  (9 shorter events, 0.1 us)
Async XLA Ops:
  1.6 1.1 copy-start
  2.7 0.7 copy-start.1
  3.4 0.7 copy-start.2
  4.1 0.7 copy-start.3
  4.8 0.7 copy-start.4
  5.9 38.5 %collective-permute-start.2 = (f32[1568,128]{1,0:T(8,128)S(1)}, f32[1568,128]{1,0:T(8,128)S(1)}, u32[]{:S(2)}, u32[]{:S(2)}) collective-permute-start(f32[1568,128]{1,0:T(8,128)S(1)} %shard_map.77.m0), channel_id=1, source_target_pairs={{0,3},{1,0},{2,1},{3,2},{4,7},{5,4},{6,5},{7,6},{8,11},{9,8},{10,9... | collective-permute-start | bytes 2408456 | tf_op jit(solution)/shard_map/ppermute | solution.py:298
  10.1 34.4 %collective-permute-start.1 = (f32[1568,128]{1,0:T(8,128)S(1)}, f32[1568,128]{1,0:T(8,128)S(1)}, u32[]{:S(2)}, u32[]{:S(2)}) collective-permute-start(f32[1568,128]{1,0:T(8,128)S(1)} %shard_map.77.m0), channel_id=1, source_target_pairs={{0,2},{1,3},{2,0},{3,1},{4,6},{5,7},{6,4},{7,5},{8,10},{9,11},{10,... | collective-permute-start | bytes 2408456 | tf_op jit(solution)/shard_map/ppermute | solution.py:298
  10.1 37.8 %collective-permute-start = (f32[1568,128]{1,0:T(8,128)S(1)}, f32[1568,128]{1,0:T(8,128)S(1)}, u32[]{:S(2)}, u32[]{:S(2)}) collective-permute-start(f32[1568,128]{1,0:T(8,128)S(1)} %shard_map.77.m0), channel_id=1, source_target_pairs={{0,1},{1,2},{2,3},{3,0},{4,5},{5,6},{6,7},{7,4},{8,9},{9,10},{10,1... | collective-permute-start | bytes 2408456 | tf_op jit(solution)/shard_map/ppermute | solution.py:298
  60.7 7.9 %collective-permute-start.10 = (f32[520,256]{1,0:T(8,128)S(1)}, f32[520,256]{1,0:T(8,128)S(1)}, u32[]{:S(2)}, u32[]{:S(2)}) collective-permute-start(f32[520,256]{1,0:T(8,128)S(1)} %constant_dynamic-update-slice_fusion.yz_own), channel_id=1, source_target_pairs={{0,4},{4,0},{8,12},{12,8},{16,20},{20,16},{24,28},{28,24},{32,36},... | collective-permute-start | bytes 1597448 | tf_op jit(solution)/shard_map/ppermute | solution.py:302
  60.8 2.3 %collective-permute-start.3 = (f32[264,256]{1,0:T(8,128)S(1)}, f32[264,256]{1,0:T(8,128)S(1)}, u32[]{:S(2)}, u32[]{:S(2)}) collective-permute-start(f32[264,256]{1,0:T(8,128)S(1)} %get-tuple-element.21.own_ref.x_own), channel_id=1, source_target_pairs={{0,4},{4,0},{8,12},{12,8},{16,20},{20,16},{24,28},{28,24},{32,36},... | collective-permute-start | bytes 811016 | tf_op jit(solution)/shard_map/ppermute | solution.py:302
  63.9 15.5 %collective-permute-start.6 = (f32[264,256]{1,0:T(8,128)S(1)}, f32[264,256]{1,0:T(8,128)S(1)}, u32[]{:S(2)}, u32[]{:S(2)}) collective-permute-start(f32[264,256]{1,0:T(8,128)S(1)} %shard_map.79.a0), channel_id=1, source_target_pairs={{0,24},{4,28},{8,0},{12,4},{16,8},{20,12},{24,16},{28,20},{32,56},... | collective-permute-start | bytes 811016 | tf_op jit(solution)/shard_map/ppermute | solution.py:313
  66.9 12.5 %collective-permute-start.5 = (f32[264,256]{1,0:T(8,128)S(1)}, f32[264,256]{1,0:T(8,128)S(1)}, u32[]{:S(2)}, u32[]{:S(2)}) collective-permute-start(f32[264,256]{1,0:T(8,128)S(1)} %shard_map.79.a0), channel_id=1, source_target_pairs={{0,16},{4,20},{8,24},{12,28},{16,0},{20,4},{24,8},{28,12},{32,48},... | collective-permute-start | bytes 811016 | tf_op jit(solution)/shard_map/ppermute | solution.py:313
  67.7 14.7 %collective-permute-start.4 = (f32[264,256]{1,0:T(8,128)S(1)}, f32[264,256]{1,0:T(8,128)S(1)}, u32[]{:S(2)}, u32[]{:S(2)}) collective-permute-start(f32[264,256]{1,0:T(8,128)S(1)} %shard_map.79.a0), channel_id=1, source_target_pairs={{0,8},{4,12},{8,16},{12,20},{16,24},{20,28},{24,0},{28,4},{32,40},... | collective-permute-start | bytes 811016 | tf_op jit(solution)/shard_map/ppermute | solution.py:313
  69.8 19.5 %collective-permute-start.16 = (f32[256,256]{1,0:T(8,128)S(1)}, f32[256,256]{1,0:T(8,128)S(1)}, u32[]{:S(2)}, u32[]{:S(2)}) collective-permute-start(f32[256,256]{1,0:T(8,128)S(1)} %get-tuple-element.31.y0), channel_id=1, source_target_pairs={{0,24},{4,28},{8,0},{12,4},{16,8},{20,12},{24,16},{28,20},{32,56},... | collective-permute-start | bytes 786440 | tf_op jit(solution)/shard_map/ppermute | solution.py:313
  83.9 20.9 %collective-permute-start.9 = (f32[264,256]{1,0:T(8,128)S(1)}, f32[264,256]{1,0:T(8,128)S(1)}, u32[]{:S(2)}, u32[]{:S(2)}) collective-permute-start(f32[264,256]{1,0:T(8,128)S(1)} %get-tuple-element.22.r0), channel_id=1, source_target_pairs={{0,96},{4,100},{8,104},{12,108},{16,112},{20,116},{24,120},{28,124... | collective-permute-start | bytes 811016 | tf_op jit(solution)/shard_map/ppermute | solution.py:317
  87.0 10.8 %collective-permute-start.15 = (f32[256,256]{1,0:T(8,128)S(1)}, f32[256,256]{1,0:T(8,128)S(1)}, u32[]{:S(2)}, u32[]{:S(2)}) collective-permute-start(f32[256,256]{1,0:T(8,128)S(1)} %get-tuple-element.31.y0), channel_id=1, source_target_pairs={{0,16},{4,20},{8,24},{12,28},{16,0},{20,4},{24,8},{28,12},{32,48},... | collective-permute-start | bytes 786440 | tf_op jit(solution)/shard_map/ppermute | solution.py:313
  87.8 14.3 %collective-permute-start.14 = (f32[256,256]{1,0:T(8,128)S(1)}, f32[256,256]{1,0:T(8,128)S(1)}, u32[]{:S(2)}, u32[]{:S(2)}) collective-permute-start(f32[256,256]{1,0:T(8,128)S(1)} %get-tuple-element.31.y0), channel_id=1, source_target_pairs={{0,8},{4,12},{8,16},{12,20},{16,24},{20,28},{24,0},{28,4},{32,40},... | collective-permute-start | bytes 786440 | tf_op jit(solution)/shard_map/ppermute | solution.py:313
  88.7 17.1 %collective-permute-start.8 = (f32[264,256]{1,0:T(8,128)S(1)}, f32[264,256]{1,0:T(8,128)S(1)}, u32[]{:S(2)}, u32[]{:S(2)}) collective-permute-start(f32[264,256]{1,0:T(8,128)S(1)} %get-tuple-element.22.r0), channel_id=1, source_target_pairs={{0,64},{4,68},{8,72},{12,76},{16,80},{20,84},{24,88},{28,92},{32,9... | collective-permute-start | bytes 811016 | tf_op jit(solution)/shard_map/ppermute | solution.py:317
  89.3 16.5 %collective-permute-start.7 = (f32[264,256]{1,0:T(8,128)S(1)}, f32[264,256]{1,0:T(8,128)S(1)}, u32[]{:S(2)}, u32[]{:S(2)}) collective-permute-start(f32[264,256]{1,0:T(8,128)S(1)} %get-tuple-element.22.r0), channel_id=1, source_target_pairs={{0,32},{4,36},{8,40},{12,44},{16,48},{20,52},{24,56},{28,60},{32,6... | collective-permute-start | bytes 811016 | tf_op jit(solution)/shard_map/ppermute | solution.py:317
  103.7 23.4 %collective-permute-start.22 = (f32[256,256]{1,0:T(8,128)S(1)}, f32[256,256]{1,0:T(8,128)S(1)}, u32[]{:S(2)}, u32[]{:S(2)}) collective-permute-start(f32[256,256]{1,0:T(8,128)S(1)} %get-tuple-element.33.y0), channel_id=1, source_target_pairs={{0,96},{4,100},{8,104},{12,108},{16,112},{20,116},{24,120},{28,124... | collective-permute-start | bytes 786440 | tf_op jit(solution)/shard_map/ppermute | solution.py:317
  104.5 22.6 %collective-permute-start.21 = (f32[256,256]{1,0:T(8,128)S(1)}, f32[256,256]{1,0:T(8,128)S(1)}, u32[]{:S(2)}, u32[]{:S(2)}) collective-permute-start(f32[256,256]{1,0:T(8,128)S(1)} %get-tuple-element.33.y0), channel_id=1, source_target_pairs={{0,64},{4,68},{8,72},{12,76},{16,80},{20,84},{24,88},{28,92},{32,9... | collective-permute-start | bytes 786440 | tf_op jit(solution)/shard_map/ppermute | solution.py:317
  104.8 22.2 %collective-permute-start.20 = (f32[256,256]{1,0:T(8,128)S(1)}, f32[256,256]{1,0:T(8,128)S(1)}, u32[]{:S(2)}, u32[]{:S(2)}) collective-permute-start(f32[256,256]{1,0:T(8,128)S(1)} %get-tuple-element.33.y0), channel_id=1, source_target_pairs={{0,32},{4,36},{8,40},{12,44},{16,48},{20,52},{24,56},{28,60},{32,6... | collective-permute-start | bytes 786440 | tf_op jit(solution)/shard_map/ppermute | solution.py:317
  107.3 3.7 %collective-permute-start.13 = (f32[8,256]{1,0:T(8,128)S(1)}, f32[8,256]{1,0:T(8,128)S(1)}, u32[]{:S(2)}, u32[]{:S(2)}) collective-permute-start(f32[8,256]{1,0:T(8,128)S(1)} %get-tuple-element.30.v0), channel_id=1, source_target_pairs={{0,24},{4,28},{8,0},{12,4},{16,8},{20,12},{24,16},{28,20},{32,56},... | collective-permute-start | bytes 24584 | tf_op jit(solution)/shard_map/ppermute | solution.py:313
  107.9 5.2 %collective-permute-start.12 = (f32[8,256]{1,0:T(8,128)S(1)}, f32[8,256]{1,0:T(8,128)S(1)}, u32[]{:S(2)}, u32[]{:S(2)}) collective-permute-start(f32[8,256]{1,0:T(8,128)S(1)} %get-tuple-element.30.v0), channel_id=1, source_target_pairs={{0,16},{4,20},{8,24},{12,28},{16,0},{20,4},{24,8},{28,12},{32,48},... | collective-permute-start | bytes 24584 | tf_op jit(solution)/shard_map/ppermute | solution.py:313
  111.0 4.9 %collective-permute-start.11 = (f32[8,256]{1,0:T(8,128)S(1)}, f32[8,256]{1,0:T(8,128)S(1)}, u32[]{:S(2)}, u32[]{:S(2)}) collective-permute-start(f32[8,256]{1,0:T(8,128)S(1)} %get-tuple-element.30.v0), channel_id=1, source_target_pairs={{0,8},{4,12},{8,16},{12,20},{16,24},{20,28},{24,0},{28,4},{32,40},... | collective-permute-start | bytes 24584 | tf_op jit(solution)/shard_map/ppermute | solution.py:313
  117.0 4.3 %collective-permute-start.19 = (f32[8,256]{1,0:T(8,128)S(1)}, f32[8,256]{1,0:T(8,128)S(1)}, u32[]{:S(2)}, u32[]{:S(2)}) collective-permute-start(f32[8,256]{1,0:T(8,128)S(1)} %get-tuple-element.32.v0), channel_id=1, source_target_pairs={{0,96},{4,100},{8,104},{12,108},{16,112},{20,116},{24,120},{28,124... | collective-permute-start | bytes 24584 | tf_op jit(solution)/shard_map/ppermute | solution.py:317
  119.7 7.3 %collective-permute-start.18 = (f32[8,256]{1,0:T(8,128)S(1)}, f32[8,256]{1,0:T(8,128)S(1)}, u32[]{:S(2)}, u32[]{:S(2)}) collective-permute-start(f32[8,256]{1,0:T(8,128)S(1)} %get-tuple-element.32.v0), channel_id=1, source_target_pairs={{0,64},{4,68},{8,72},{12,76},{16,80},{20,84},{24,88},{28,92},{32,9... | collective-permute-start | bytes 24584 | tf_op jit(solution)/shard_map/ppermute | solution.py:317
  121.3 5.7 %collective-permute-start.17 = (f32[8,256]{1,0:T(8,128)S(1)}, f32[8,256]{1,0:T(8,128)S(1)}, u32[]{:S(2)}, u32[]{:S(2)}) collective-permute-start(f32[8,256]{1,0:T(8,128)S(1)} %get-tuple-element.32.v0), channel_id=1, source_target_pairs={{0,32},{4,36},{8,40},{12,44},{16,48},{20,52},{24,56},{28,60},{32,6... | collective-permute-start | bytes 24584 | tf_op jit(solution)/shard_map/ppermute | solution.py:317

commit v2 on v0

v2 whole, which is shorter than its diff:
```python
import functools

import jax
import jax.numpy as jnp
from jax import lax
from jax.experimental import pallas as pl
from jax.experimental.pallas import tpu as pltpu
from jax.sharding import PartitionSpec as P

BLOCK = 64
STATE = 256
BLOCKS = 4
STEPS = 16
SIZES = (4, 4, 4, 4)
RELAYS = (1, 1, 3, 3)
CHUNKS = len(SIZES)
STARTS = tuple(sum(SIZES[:q]) for q in range(CHUNKS))
AUG = STATE + 8
MIB = 1 << 20

f32 = jnp.float32
bf16 = jnp.bfloat16


def split(a):
    hi = a.astype(bf16)
    return hi, (a - hi.astype(f32)).astype(bf16)


def dot_nn(a, b):
    return lax.dot_general(a, b, (((1,), (0,)), ((), ())), preferred_element_type=f32)


def dot_nt(a, b):
    return lax.dot_general(a, b, (((1,), (1,)), ((), ())), preferred_element_type=f32)


def three(dot, a, b):
    ahi, alo = a
    bhi, blo = b
    return dot(ahi, bhi) + (dot(alo, bhi) + dot(ahi, blo))


def rows_by(dot, a, b):
    high = a.astype(bf16).astype(f32)
    both = jnp.concatenate([high, a - high], axis=0).astype(bf16)
    wide = dot(both, b[0]) + dot(both, b[1])
    return wide[:8] + wide[8:]


def mul_by(dot, a, b):
    if a.shape[0] == 8:
        return rows_by(dot, a, split(b))
    return three(dot, split(a), split(b))


def mul_nn(a, b):
    return mul_by(dot_nn, a, b)


def mul_nt(a, b):
    return mul_by(dot_nt, a, b)


def first_row(row):
    spread = jnp.broadcast_to(row, (8, row.shape[1]))
    return jnp.where(lax.broadcasted_iota(jnp.int32, spread.shape, 0) == 0, spread, 0.0)


def identity_matrix():
    rows = lax.broadcasted_iota(jnp.int32, (STATE, STATE), 0)
    cols = lax.broadcasted_iota(jnp.int32, (STATE, STATE), 1)
    return jnp.where(rows == cols, 1.0, 0.0).astype(f32)


def call(kernel, us, outs, args, scratch=(), raw=False, limit=40):
    vmem = pl.BlockSpec(memory_space=pltpu.VMEM)
    moved = sum(a.size * a.dtype.itemsize for a in args) + sum(
        o.size * o.dtype.itemsize for o in outs
    )
    return pl.pallas_call(
        kernel,
        out_shape=outs,
        in_specs=[pl.BlockSpec(memory_space=pltpu.HBM) if raw else vmem] * len(args),
        out_specs=[vmem] * len(outs),
        scratch_shapes=list(scratch),
        compiler_params=pltpu.CompilerParams(vmem_limit_bytes=limit * MIB),
        cost_estimate=pl.CostEstimate(flops=int(us * 1e9), bytes_accessed=moved, transcendentals=0),
    )(*args)


def arr(*shape, dtype=f32):
    return jax.ShapeDtypeStruct(shape, dtype)


def core_of():
    return lax.rem(lax.axis_index("tm"), 2)


def x_of():
    return lax.rem(lax.axis_index("tm") // 2, 4)


def y_of():
    return lax.axis_index("tm") // 8


PER_STEP = BLOCK + BLOCK // 2 + 2
PART_Y = AUG
ROWS = 2 * AUG
ENDS = tuple((q, i) for q in range(CHUNKS) for i in range(SIZES[q]))


def pack_kernel(dyn_hbm, band_hbm, obs_hbm, mask_hbm, fgain_hbm, sgain_hbm, *refs):
    outs = refs[:CHUNKS]
    dyn_ref, band_ref, obs_ref, mask_ref, fgain_ref, sgain_ref, sems = refs[CHUNKS:]
    copies = [
        pltpu.make_async_copy(src, dst, sems.at[i])
        for i, (src, dst) in enumerate(
            (
                (dyn_hbm, dyn_ref),
                (band_hbm, band_ref),
                (obs_hbm, obs_ref),
                (mask_hbm, mask_ref),
                (fgain_hbm, fgain_ref),
                (sgain_hbm, sgain_ref),
            )
        )
    ]
    for copy in copies:
        copy.start()
    for copy in copies:
        copy.wait()
    place = lax.axis_index("state")
    row = lax.broadcasted_iota(jnp.int32, (2, STEPS), 0)
    outside = jnp.where(place == 0, 0, jnp.where(place == BLOCKS - 1, 1, 2))
    band = jnp.where(row == outside, 0, band_ref[...]).astype(f32)
    band = jnp.transpose(jnp.concatenate([band, jnp.zeros((6, STEPS), f32)], axis=0))
    lower, upper = band[:, 0:1], band[:, 1:2]
    half = BLOCK // 2
    wide = 3 * BLOCK

    def put(at, value):
        for t0, size, out in zip(STARTS, SIZES, outs):
            out[at * size : (at + 1) * size, :] = value[t0 : t0 + size]

    for r in range(BLOCK):
        before = dyn_ref[:, r * wide : r * wide + BLOCK] * lower
        own = dyn_ref[:, r * wide + BLOCK : r * wide + 2 * BLOCK]
        put(r, jnp.concatenate([before, own], axis=1))
    for r in range(half):
        s = r + half
        near = dyn_ref[:, r * wide + 2 * BLOCK : (r + 1) * wide] * upper
        far = dyn_ref[:, s * wide + 2 * BLOCK : (s + 1) * wide] * upper
        put(BLOCK + r, jnp.concatenate([near, far], axis=1))
    weight = mask_ref[...].astype(f32) * fgain_ref[...]
    gain = sgain_ref[...]
    put(BLOCK + half, jnp.concatenate([weight, obs_ref[...]], axis=1))
    put(BLOCK + half + 1, jnp.concatenate([gain, gain], axis=1))


def chunk_kernel(first, size, *refs):
    parts = refs[:BLOCKS]
    state_ref, fhi_ref, flo_ref, thi_ref, tlo_ref, vec_ref, out_ref = (
        (None,) if first else ()
    ) + refs[BLOCKS:]
    place = lax.axis_index("state")
    zeros64 = jnp.zeros((BLOCK, BLOCK), f32)
    zero = jnp.zeros((size, STATE - BLOCK), f32)
    vecs = [None] * 3
    pairs_at = BLOCK * size
    vecs_at = pairs_at + BLOCK // 2 * size
    for s, m in enumerate(parts):
        block = lax.rem(place - s + BLOCKS, BLOCKS)
        shift = lax.rem(block + BLOCKS - 1, BLOCKS) * BLOCK
        rows = pl.ds(pl.multiple_of(block * BLOCK, BLOCK), BLOCK)
        for t in range(size):
            left = m[pl.ds(t, BLOCK, stride=size), :]
            pair = m[pl.ds(pairs_at + t, BLOCK // 2, stride=size), :]
            after = jnp.concatenate([pair[:, :BLOCK], pair[:, BLOCK:]], axis=0)
            full = jnp.concatenate([left, after, zeros64], axis=1)
            hi, lo = split(pltpu.roll(full, shift, 1))
            fhi_ref[t, rows, :] = hi
            flo_ref[t, rows, :] = lo
        wo = m[vecs_at : vecs_at + size, :]
        g = m[vecs_at + size : vecs_at + 2 * size, :]
        for i, piece in enumerate((wo[:, :BLOCK], wo[:, BLOCK:], g[:, :BLOCK])):
            piece = pltpu.roll(jnp.concatenate([piece, zero], axis=1), block * BLOCK, 1)
            vecs[i] = piece if vecs[i] is None else vecs[i] + piece
    for i in range(3):
        vec_ref[i] = vecs[i]
    if first:
        x = jnp.concatenate([identity_matrix(), jnp.zeros((8, STATE), f32)], axis=0)
        y = identity_matrix()
    else:
        x = state_ref[:AUG]
        y = state_ref[PART_Y : PART_Y + STATE]
    for t in range(size):
        w, o, g = (vecs[i][t : t + 1, :] for i in range(3))
        step = (fhi_ref[t], flo_ref[t])
        moved = three(dot_nt, split(x), step)
        thi_ref[t], tlo_ref[t] = split(moved[:STATE])
        vec_ref[3, t : t + 1, :] = moved[STATE : STATE + 1]
        kept = moved * (1.0 - w)
        x = jnp.concatenate([kept[:STATE], kept[STATE:] + first_row(w * o)], axis=0)
        y = three(dot_nt, split(y), step) * g
    out_ref[:AUG] = x
    out_ref[PART_Y : PART_Y + STATE] = y
    out_ref[PART_Y + STATE :] = jnp.zeros((8, STATE), f32)


def then(first, second):
    both = mul_nn(first, second[:STATE])
    return jnp.concatenate([both[:STATE], both[STATE:] + second[STATE:]], axis=0)


def pair_kernel(own_ref, other_ref, out_ref):
    core = core_of()
    part = pl.ds(pl.multiple_of(core * AUG, 8), AUG)
    own, other = own_ref[part, :], other_ref[part, :]
    lead = core == 0
    out_ref[...] = then(jnp.where(lead, own, other), jnp.where(lead, other, own))


def pair_z_kernel(own_ref, other_ref, z_own, z_other, z_ref):
    lead = core_of() == 0
    xl = jnp.where(lead, own_ref[:AUG], other_ref[:AUG])
    yl = jnp.where(lead, own_ref[PART_Y : PART_Y + STATE], other_ref[PART_Y : PART_Y + STATE])
    zl = jnp.where(lead, z_own[...], z_other[...])
    zr = jnp.where(lead, z_other[...], z_own[...])
    z_ref[...] = zl + mul_nt(then(xl, zr), yl)


def suffix_kernel(*refs):
    his, los, vecs = (refs[i * CHUNKS : (i + 1) * CHUNKS] for i in range(3))
    shi_ref, slo_ref = refs[-2:]
    run = identity_matrix()
    for t in range(STEPS - 1, 0, -1):
        q, i = ENDS[t]
        run = three(dot_nn, split(run * vecs[q][2, i : i + 1, :]), (his[q][i], los[q][i]))
        shi_ref[t], slo_ref[t] = split(run)


def suffix_z_kernel(*refs):
    his, los, this, tlos, vecs = (refs[i * CHUNKS : (i + 1) * CHUNKS] for i in range(5))
    zhi_ref, zlo_ref, v_ref, z_ref = refs[5 * CHUNKS :]
    z = jnp.zeros((STATE, STATE), f32)
    v = jnp.zeros((8, STATE), f32)
    v_ref[...] = jnp.zeros((STEPS, STATE), f32)
    for t in range(STEPS - 1, -1, -1):
        q, i = ENDS[t]
        w, o, g, p = (vecs[q][k, i : i + 1, :] for k in range(4))
        step = (his[q][i], los[q][i])
        moved = this[q][i].astype(f32) + tlos[q][i].astype(f32)
        z = three(dot_nn, split(z * g - moved * w), step)
        v = rows_by(dot_nn, v * g + first_row(w * (o - p)), step)
        if t > 0:
            zhi_ref[t], zlo_ref[t] = split(z)
            v_ref[t : t + 1, :] = v[0:1]
    z_ref[:STATE] = z
    z_ref[STATE:] = v


def duo_kernel(own, partner, _, out_ref):
    even = lax.rem(x_of(), 2) == 0
    mine, theirs = own[...], partner[...]
    out_ref[...] = then(jnp.where(even, mine, theirs), jnp.where(even, theirs, mine))


def row_kernel(partner, duo, other_duo, *refs):
    whole_ref, side_ref, tail_ref = refs[-3:]
    x = x_of()
    lead = core_of() == 0
    low = x < 2
    mine, theirs, beside = duo[...], other_duo[...], partner[...]
    whole = then(jnp.where(low, mine, theirs), jnp.where(low, theirs, mine))
    whole_ref[...] = whole
    tail_ref[...] = whole[STATE:]
    outer = then(jnp.where(lead, theirs, beside), jnp.where(lead, beside, theirs))
    nothing = jnp.concatenate([identity_matrix(), jnp.zeros((8, STATE), f32)], axis=0)
    depth = jnp.where(lead, x, 3 - x)
    side = jnp.where(depth == 0, nothing, jnp.where(depth == 1, beside, theirs))
    side_ref[...] = jnp.where(depth == 3, outer, side)


def enter_kernel(near, far, tail, side_ref, own_ref, z_chip, means_ref, v_ref):
    y = y_of()
    through = mul_nn(tail[...], far[:STATE]) + far[STATE:]
    inner = jnp.where(y == 3, through, jnp.where(y == 2, far[STATE:], 0.0))
    m = mul_nn(inner, near[:STATE]) + near[STATE:]
    m = mul_nn(m, side_ref[:STATE]) + side_ref[STATE:]
    v = mul_nn(m, z_chip[:STATE]) + z_chip[STATE:]
    v_ref[...] = v
    means_ref[:8] = v
    means_ref[8:16] = m
    means_ref[16:] = mul_nn(m, own_ref[:STATE]) + own_ref[STATE:AUG]


def local_kernel(means_ref, sent_ref, z_other, zhi_ref, zlo_ref, v_ref, *refs):
    this, tlos, vecs = (refs[i * CHUNKS : (i + 1) * CHUNKS] for i in range(3))
    m_ref, h_ref, mid_ref = refs[3 * CHUNKS :]
    mid_ref[...] = mul_nn(means_ref[16:], z_other[:STATE]) + z_other[STATE:]
    enter = jnp.where(core_of() == 0, means_ref[8:16], sent_ref[16:])
    for q in range(CHUNKS):
        rows = [rows_by(dot_nn, enter, (this[q][i], tlos[q][i]))[0:1] for i in range(SIZES[q])]
        p = jnp.concatenate(rows, axis=0) + vecs[q][3]
        e = vecs[q][0] * (vecs[q][1] - p)
        m_ref[STARTS[q] : STARTS[q] + SIZES[q], :] = p + e
    for t in range(STEPS - 1):
        row = rows_by(dot_nn, enter, (zhi_ref[t + 1], zlo_ref[t + 1]))[0:1]
        h_ref[t : t + 1, :] = row + v_ref[t + 1 : t + 2, :]
    h_ref[STEPS - 1 :, :] = jnp.zeros((1, STATE), f32)


def duo_v_kernel(sent, partner_v, own_y, partner_y, _, out_ref):
    even = lax.rem(x_of(), 2) == 0
    mine, theirs = sent[:8], partner_v[...]
    y = jnp.where(even, own_y[:STATE], partner_y[:STATE])
    out_ref[...] = jnp.where(even, mine, theirs) + mul_nt(jnp.where(even, theirs, mine), y)


def row_v_kernel(duo_v, other_v, partner_v, duo_y, other_y, partner_y, whole_ref, after_ref):
    x = x_of()
    low = x < 2
    mine, theirs, beside = duo_v[...], other_v[...], partner_v[...]
    y = jnp.where(low, duo_y[:STATE], other_y[:STATE])
    whole_ref[...] = jnp.where(low, mine, theirs) + mul_nt(jnp.where(low, theirs, mine), y)
    outer = beside + mul_nt(theirs, partner_y[:STATE])
    after = jnp.where(x == 3, 0.0, jnp.where(x == 2, beside, theirs))
    after_ref[...] = jnp.where(x == 0, outer, after)


def leave_kernel(v1, v2, v3, near, far, side_ref, after_ref, *refs):
    out_ref = refs[-1]
    inner = v2[...] + mul_nt(v3[...], far[:STATE])
    sigma = v1[...] + mul_nt(inner, near[:STATE])
    out_ref[...] = mul_nt(sigma, side_ref[:STATE]) + after_ref[...]


def smooth_kernel(sigma_ref, sent_ref, other_ref, mid_ref, shi_ref, slo_ref, *refs):
    vecs = refs[:CHUNKS]
    m_ref, h_ref, filt_ref, smooth_ref = refs[CHUNKS:]
    place = lax.axis_index("state")
    crossed = mul_nt(sent_ref[...], other_ref[PART_Y : PART_Y + STATE]) + mid_ref[...]
    sigma = jnp.where(core_of() == 0, crossed, sigma_ref[...])
    rows = []
    for t in range(STEPS):
        if t == STEPS - 1:
            rows.append(sigma[0:1])
        else:
            rows.append(rows_by(dot_nn, sigma, (shi_ref[t + 1], slo_ref[t + 1]))[0:1])
    gain = jnp.concatenate([v[2] for v in vecs], axis=0)
    filt = m_ref[...]
    smooth = filt + gain * (h_ref[...] + jnp.concatenate(rows, axis=0))
    out_f = filt[:, :BLOCK]
    out_s = smooth[:, :BLOCK]
    for b in range(1, BLOCKS):
        part = slice(b * BLOCK, (b + 1) * BLOCK)
        out_f = jnp.where(place == b, filt[:, part], out_f)
        out_s = jnp.where(place == b, smooth[:, part], out_s)
    filt_ref[...] = out_f
    smooth_ref[...] = out_s


def over_z(a, s):
    return lax.ppermute(a, "state", [(i, (i + s) % 4) for i in range(4)])


def chip(x, y, c):
    return (y * 4 + x) * 2 + c


def over_core(a):
    return lax.ppermute(a, "tm", [(i, i ^ 1) for i in range(32)])


def over_x(a, to, pairs=((0, 0), (1, 1))):
    route = [
        (chip(x, y, c), chip(to(x), y, d)) for y in range(4) for x in range(4) for c, d in pairs
    ]
    return lax.ppermute(a, "tm", route)


def beside(x):
    return x ^ 1


def opposite(x):
    return 3 - x


def over_y(a, up=(), down=()):
    route = [(chip(x, a, 0), chip(x, b, 0)) for a, b in up for x in range(4)]
    route += [(chip(x, a, 1), chip(x, b, 1)) for a, b in down for x in range(4)]
    return lax.ppermute(a, "tm", route)


def gather_z(chunks):
    ahead = [over_z(a, 1) for a in chunks]
    behind = [over_z(a, 3) for a in chunks]
    return [
        [a, ahead[q], over_z(ahead[q] if RELAYS[q] == 1 else behind[q], RELAYS[q]), behind[q]]
        for q, a in enumerate(chunks)
    ]


def shards(dynamics, band, observed, obs_mask, filter_gain, smooth_gain):
    packed = call(
        pack_kernel,
        0,
        [arr(PER_STEP * size, 128) for size in SIZES],
        [dynamics, band.transpose(1, 2, 0).reshape(2, STEPS), observed, obs_mask, filter_gain, smooth_gain],
        [
            pltpu.VMEM((STEPS, 3 * BLOCK * BLOCK), f32),
            pltpu.VMEM((2, STEPS), jnp.int32),
            pltpu.VMEM((STEPS, BLOCK), f32),
            pltpu.VMEM((STEPS, BLOCK), jnp.int32),
            pltpu.VMEM((STEPS, BLOCK), f32),
            pltpu.VMEM((STEPS, BLOCK), f32),
            pltpu.SemaphoreType.DMA((6,)),
        ],
        raw=True,
        limit=60,
    )
    his, los, this, tlos, vecs, state = [], [], [], [], [], []
    for q, parts in enumerate(gather_z(packed)):
        size = SIZES[q]
        kept = call(
            functools.partial(chunk_kernel, q == 0, size),
            0.4 * size,
            [arr(size, STATE, STATE, dtype=bf16)] * 4 + [arr(4, size, STATE), arr(ROWS, STATE)],
            parts + state,
        )
        for store, value in zip((his, los, this, tlos, vecs), kept):
            store.append(value)
        own = kept[-1]
        state = [own]
    other = over_core(own)
    (side_own,) = call(pair_kernel, 0, [arr(AUG, STATE)], [own, other])
    partner = over_x(side_own, beside)
    zhi, zlo, v_all, z_own = call(
        suffix_z_kernel,
        0,
        [arr(STEPS, STATE, STATE, dtype=bf16)] * 2 + [arr(STEPS, STATE), arr(AUG, STATE)],
        his + los + this + tlos + vecs,
    )
    (duo,) = call(duo_kernel, 0, [arr(AUG, STATE)], [side_own, partner, z_own])
    other_duo = over_x(duo, opposite)
    z_other = over_core(z_own)
    shi, slo = call(
        suffix_kernel, 0, [arr(STEPS, STATE, STATE, dtype=bf16)] * 2, his + los + vecs
    )
    whole, side, tail = call(
        row_kernel,
        0,
        [arr(AUG, STATE)] * 2 + [arr(8, STATE)],
        [partner, duo, other_duo, z_other, shi],
    )
    tail = over_y(tail, ((0, 3),))
    near = over_y(whole, ((0, 1), (1, 2), (2, 3)), ((2, 1), (1, 0)))
    far = over_y(whole, ((0, 2), (1, 3)), ((2, 0),))
    (z_chip,) = call(pair_z_kernel, 0, [arr(AUG, STATE)], [own, other, z_own, z_other])
    means, v_chip = call(
        enter_kernel,
        0,
        [arr(24, STATE), arr(8, STATE)],
        [near, far, tail, side, own, z_chip],
    )
    partner_v = over_x(v_chip, beside, ((0, 1),))
    sent = over_core(means)
    m_all, h_all, mid = call(
        local_kernel,
        0,
        [arr(STEPS, STATE)] * 2 + [arr(8, STATE)],
        [means, sent, z_other, zhi, zlo, v_all] + this + tlos + vecs,
    )
    (duo_v,) = call(
        duo_v_kernel, 0, [arr(8, STATE)], [sent, partner_v, side_own, partner, h_all]
    )
    other_v = over_x(duo_v, opposite, ((1, 1),))
    v_row, v_after = call(
        row_v_kernel,
        0,
        [arr(8, STATE)] * 2,
        [duo_v, other_v, partner_v, duo, other_duo, partner],
    )
    v_rows = [
        over_y(v_row, (), ((3, 2), (2, 1), (1, 0))),
        over_y(v_row, (), ((3, 1), (2, 0))),
        over_y(v_row, (), ((3, 0),)),
    ]
    (sigma,) = call(leave_kernel, 0, [arr(8, STATE)], v_rows + [near, far, side, v_after])
    crossed = over_core(sigma)
    filtered, smoothed = call(
        smooth_kernel,
        0,
        [arr(STEPS, BLOCK)] * 2,
        [sigma, crossed, other, mid, shi, slo] + vecs + [m_all, h_all],
    )
    return filtered, smoothed


def solution(mesh):
    in_specs = (
        P("tm", "state"),
        P("tm", "state", None),
        P("tm", "state"),
        P("tm", "state"),
        P("tm", "state"),
        P("tm", "state"),
    )
    out_specs = (P("tm", "state"), P("tm", "state"))
    return jax.shard_map(shards, mesh=mesh, in_specs=in_specs, out_specs=out_specs, check_vma=False)
```

time: 499 us -> 92.7 us (0.19)
  blocking collectives: 166 us -> 0 us
  matrix products: 133 us -> 0 us
  waiting for transfers between devices: 108 us -> 16.2 us
  local copies, waits for them, and re-layouts: 60.3 us -> 0.94 us
  starting transfers between devices: 1.46 us -> 49.5 us
  Pallas kernels: 0 us -> 23.6 us
  between operations: 14 us -> 0.91 us
  other arithmetic: 9.04 us -> 0 us
    all_gather x7 -> x0, blocking collectives: 149 us -> none  [the longest x2 85.3 us: entering_2(): gathered = jax.tree.map(lambda a: lax.all_gather(a, axis), part)]
    dot_general x99 -> x0, matrix products: 133 us -> none  [the longest x33 49.5 us: band_apply(): jnp.einsum('...ibc,...icw->...ibw', panels, gathered, precision=highest)]
    all_gather x3 -> x0, waiting for transfers between devices: 89.7 us -> none  [the longest x2 58.1 us: entering_2(): gathered = jax.tree.map(lambda a: lax.all_gather(a, axis), part)]
    ppermute x1 -> x26, starting transfers between devices: 1.29 us -> 49.5 us  [the longest x12 18.9 us: over_z(): return lax.ppermute(a, 'state', [(i, (i + s) % 4) for i in range(4)])]
    pallas_call x0 -> x17, Pallas kernels: none -> 23.6 us  [call(): pl.pallas_call(kernel, out_shape=outs, in_specs=[pl.BlockSpec(memory_spac...]
    reshape x212 -> x0, local copies, waits for them, and re-layouts: 21.8 us -> none  [the longest x99 8.74 us: neighbours(): padded[..., offset * rows:offset * rows + total, :]]
    while x3 -> x0, local copies, waits for them, and re-layouts: 18.1 us -> none  [the longest x2 18 us: entering_2(): return lax.fori_loop(0, ahead, one, state)]
    psum x1 -> x0, blocking collectives: 17.1 us -> none  [shards(): lax.psum(jnp.einsum('tsw,w->ts', prefixes, local_enter, precision=highest...]
  transfers between devices with their start and end apart: 5 -> 26, of which waited for: 5 -> 11; matrix products, arithmetic and copies ran while one was open for 0% -> 0% of each run, Pallas kernels for 0% -> 17%
where the time goes in v2:
time: 92.7 us; the launch traced here: 91.2 us
  starting transfers between devices  49.5 us (53%)
  Pallas kernels  23.6 us (25%)
  waiting for transfers between devices  16.2 us (17%)
  local copies, waits for them, and re-layouts  0.94 us (1%)
    pallas_call x17, Pallas kernels, call(): pl.pallas_call(kernel, out_shape=outs, in_specs=[pl.BlockSpec(memory_spac...  23.6 us
    ppermute x12, starting transfers between devices, over_z(): return lax.ppermute(a, 'state', [(i, (i + s) % 4) for i in range(4)])  18.9 us
    ppermute x4, starting transfers between devices, over_core(): return lax.ppermute(a, 'tm', [(i, i ^ 1) for i in range(32)])  12.1 us
    ppermute x6, starting transfers between devices, over_y(): return lax.ppermute(a, 'tm', route)  11 us
    ppermute x4, starting transfers between devices, over_x(): return lax.ppermute(a, 'tm', route)  7.55 us
    ppermute x12, waiting for transfers between devices, over_z(): return lax.ppermute(a, 'state', [(i, (i + s) % 4) for i in range(4)])  6.1 us
    ppermute x4, waiting for transfers between devices, over_x(): return lax.ppermute(a, 'tm', route)  5.01 us
    ppermute x4, waiting for transfers between devices, over_core(): return lax.ppermute(a, 'tm', [(i, i ^ 1) for i in range(32)])  2.75 us
  transfers between devices with their start and end apart: 26, of which 11 were waited for; matrix products, arithmetic and copies ran while one was open for 0% of the time, Pallas kernels for 17%

profile of v2, /device:TPU:0, one launch (start us, length us, event | category | flops | bytes accessed | tf_op | source)
XLA Modules:
  0.0 91.2 jit_solution(1825902183624948202)
XLA Ops:
  0.6 2.6 %shard_map.77 = (f32[392,128]{1,0:T(8,128)}, f32[392,128]{1,0:T(8,128)}, f32[392,128]{1,0:T(8,128)}, f32[392,128]{1,0:T(8,128)}) custom-call(f32[16,12288]{1,0:T(8,128)} %dyn_hbm.1, s32[2,16]{1,0:T(2,128)} %bitcast.3, f32[16,64]{1,0:T(8,128)} %obs_hbm.1, s32[16,64]{1,0:T(8,128)} %mask_hbm.1, f32[16,64]{1,0:T(8,128)} %fgain_hbm.1, f32[16,64]{1,0:T(8,128)} %sgain_hbm.1), custom_call_target="tpu_custom_call" | custom-call | bytes 1605760 | tf_op jit(solution)/shard_map/pallas_call | solution.py:81
  3.2 2.1 %collective-permute-start.9 = (f32[392,128]{1,0:T(8,128)}, f32[392,128]{1,0:T(8,128)S(1)}, u32[]{:S(2)}, u32[]{:S(2)}) collective-permute-start(f32[392,128]{1,0:T(8,128)} %get-tuple-element.49.refs_0_), channel_id=1, source_target_pairs={{0,1},{1,2},{2,3},{3,0},{4,5},{5,6},{6,7},{7,4},{8,9},{9,10},{10,1... | collective-permute-start | bytes 602120 | tf_op jit(solution)/shard_map/ppermute | solution.py:366
  5.3 2.2 %collective-permute-start.4 = (f32[392,128]{1,0:T(8,128)}, f32[392,128]{1,0:T(8,128)S(1)}, u32[]{:S(2)}, u32[]{:S(2)}) collective-permute-start(f32[392,128]{1,0:T(8,128)} %get-tuple-element.47.refs_0_), channel_id=1, source_target_pairs={{0,3},{1,0},{2,1},{3,2},{4,7},{5,4},{6,5},{7,6},{8,11},{9,8},{10,9... | collective-permute-start | bytes 602120 | tf_op jit(solution)/shard_map/ppermute | solution.py:366
  7.5 0.0 collective-permute-start.6
  7.5 3.2 %collective-permute-start.11 = (f32[392,128]{1,0:T(8,128)}, f32[392,128]{1,0:T(8,128)S(1)}, u32[]{:S(2)}, u32[]{:S(2)}) collective-permute-start(f32[392,128]{1,0:T(8,128)} %get-tuple-element.49.refs_0_), channel_id=1, source_target_pairs={{0,3},{1,0},{2,1},{3,2},{4,7},{5,4},{6,5},{7,6},{8,11},{9,8},{10,9... | collective-permute-start | bytes 602120 | tf_op jit(solution)/shard_map/ppermute | solution.py:366
  10.7 2.7 %collective-permute-done.9.refs_1_ = f32[392,128]{1,0:T(8,128)S(1)} collective-permute-done((f32[392,128]{1,0:T(8,128)}, f32[392,128]{1,0:T(8,128)S(1)}, u32[]{:S(2)}, u32[]{:S(2)}) %collective-permute-start.9) | collective-permute-done | bytes 200736 | tf_op jit(solution)/shard_map/ppermute | solution.py:366
  13.4 0.0 collective-permute-start.10
  13.4 3.2 %collective-permute-start.1 = (f32[392,128]{1,0:T(8,128)}, f32[392,128]{1,0:T(8,128)S(1)}, u32[]{:S(2)}, u32[]{:S(2)}) collective-permute-start(f32[392,128]{1,0:T(8,128)} %get-tuple-element.46.refs_0_), channel_id=1, source_target_pairs={{0,3},{1,0},{2,1},{3,2},{4,7},{5,4},{6,5},{7,6},{8,11},{9,8},{10,9... | collective-permute-start | bytes 602120 | tf_op jit(solution)/shard_map/ppermute | solution.py:366
  16.7 0.0 collective-permute-done.4.refs_3_
  16.7 0.8 collective-permute-start.8
  17.5 0.2 collective-permute-done.6.refs_1_
  17.7 1.0 %collective-permute-start.7 = (f32[392,128]{1,0:T(8,128)S(1)}, f32[392,128]{1,0:T(8,128)S(1)}, u32[]{:S(2)}, u32[]{:S(2)}) collective-permute-start(f32[392,128]{1,0:T(8,128)S(1)} %collective-permute-done.6.refs_1_), channel_id=1, source_target_pairs={{0,1},{1,2},{2,3},{3,0},{4,5},{5,6},{6,7},{7,4},{8,9},{9,10},{10,1... | collective-permute-start | bytes 602120 | tf_op jit(solution)/shard_map/ppermute | solution.py:366
  18.7 0.0 collective-permute-done.11.refs_3_
  18.7 0.9 %collective-permute-start.3 = (f32[392,128]{1,0:T(8,128)}, f32[392,128]{1,0:T(8,128)S(1)}, u32[]{:S(2)}, u32[]{:S(2)}) collective-permute-start(f32[392,128]{1,0:T(8,128)} %get-tuple-element.47.refs_0_), channel_id=1, source_target_pairs={{0,1},{1,2},{2,3},{3,0},{4,5},{5,6},{6,7},{7,4},{8,9},{9,10},{10,1... | collective-permute-start | bytes 602120 | tf_op jit(solution)/shard_map/ppermute | solution.py:366
  19.6 2.7 %collective-permute-done.10.refs_2_ = f32[392,128]{1,0:T(8,128)S(1)} collective-permute-done((f32[392,128]{1,0:T(8,128)S(1)}, f32[392,128]{1,0:T(8,128)S(1)}, u32[]{:S(2)}, u32[]{:S(2)}) %collective-permute-start.10) | collective-permute-done | bytes 200736 | tf_op jit(solution)/shard_map/ppermute | solution.py:366
  22.4 1.7 %collective-permute-start.5 = (f32[392,128]{1,0:T(8,128)S(1)}, f32[392,128]{1,0:T(8,128)S(1)}, u32[]{:S(2)}, u32[]{:S(2)}) collective-permute-start(f32[392,128]{1,0:T(8,128)S(1)} %collective-permute-done.4.refs_3_), channel_id=1, source_target_pairs={{0,3},{1,0},{2,1},{3,2},{4,7},{5,4},{6,5},{7,6},{8,11},{9,8},{10,9... | collective-permute-start | bytes 602120 | tf_op jit(solution)/shard_map/ppermute | solution.py:366
  24.1 0.9 %copy-done.3 = f32[392,128]{1,0:T(8,128)S(1)} copy-done((f32[392,128]{1,0:T(8,128)S(1)}, f32[392,128]{1,0:T(8,128)}, u32[]{:S(2)}) %copy-start.3) | copy-done | bytes 200728
  25.0 1.6 %shard_map.78 = (bf16[4,256,256]{2,1,0:T(8,128)(2,1)S(1)}, bf16[4,256,256]{2,1,0:T(8,128)(2,1)S(1)}, bf16[4,256,256]{2,1,0:T(8,128)(2,1)S(1)}, bf16[4,256,256]{2...) custom-call(f32[392,128]{1,0:T(8,128)S(1)} %copy-done.3, ...), custom_call_target="tpu_custom_call" | custom-call | flops 1600000000 | bytes 3457024 | tf_op jit(solution)/shard_map/pallas_call | solution.py:81
  26.7 0.0 collective-permute-done.1.refs_3_
  26.7 0.3 collective-permute-start
  27.0 0.0 collective-permute-done.8.refs_3_
  27.0 3.3 %collective-permute-start.2 = (f32[392,128]{1,0:T(8,128)S(1)}, f32[392,128]{1,0:T(8,128)S(1)}, u32[]{:S(2)}, u32[]{:S(2)}) collective-permute-start(f32[392,128]{1,0:T(8,128)S(1)} %collective-permute-done.1.refs_3_), channel_id=1, source_target_pairs={{0,3},{1,0},{2,1},{3,2},{4,7},{5,4},{6,5},{7,6},{8,11},{9,8},{10,9... | collective-permute-start | bytes 602120 | tf_op jit(solution)/shard_map/ppermute | solution.py:366
  30.3 0.0 collective-permute-done.7.refs_2_
  30.3 1.6 %shard_map.79 = (bf16[4,256,256]{2,1,0:T(8,128)(2,1)S(1)}, bf16[4,256,256]{2,1,0:T(8,128)(2,1)S(1)}, bf16[4,256,256]{2,1,0:T(8,128)(2,1)S(1)}, bf16[4,256,256]{2...) custom-call(f32[392,128]{1,0:T(8,128)S(1)} %copy-done.2, ...), custom_call_target="tpu_custom_call" | custom-call | flops 1600000000 | bytes 3997696 | tf_op jit(solution)/shard_map/pallas_call | solution.py:81
  32.0 0.0 collective-permute-done.5.refs_2_
  32.0 1.6 %shard_map.80 = (bf16[4,256,256]{2,1,0:T(8,128)(2,1)S(1)}, bf16[4,256,256]{2,1,0:T(8,128)(2,1)S(1)}, bf16[4,256,256]{2,1,0:T(8,128)(2,1)S(1)}, bf16[4,256,256]{2...) custom-call(f32[392,128]{1,0:T(8,128)S(1)} %copy-done.1, ...), custom_call_target="tpu_custom_call" | custom-call | flops 1600000000 | bytes 3997696 | tf_op jit(solution)/shard_map/pallas_call | solution.py:81
  33.7 0.4 collective-permute-done.refs_1_
  34.1 0.0 collective-permute-done.2.refs_2_
  34.1 1.6 %shard_map.81 = (bf16[4,256,256]{2,1,0:T(8,128)(2,1)S(1)}, bf16[4,256,256]{2,1,0:T(8,128)(2,1)S(1)}, bf16[4,256,256]{2,1,0:T(8,128)(2,1)S(1)}, bf16[4,256,256]{2...) custom-call(f32[392,128]{1,0:T(8,128)S(1)} %copy-done, ...), custom_call_target="tpu_custom_call" | custom-call | flops 1600000000 | bytes 3997696 | tf_op jit(solution)/shard_map/pallas_call | solution.py:81
  35.7 0.1 collective-permute-start.12
  35.8 1.9 %collective-permute-done.12.other_ref = f32[528,256]{1,0:T(8,128)S(1)} collective-permute-done((f32[528,256]{1,0:T(8,128)S(1)}, f32[528,256]{1,0:T(8,128)S(1)}, u32[]{:S(2)}, u32[]{:S(2)}) %collective-permute-start.12) | collective-permute-done | bytes 540704 | tf_op jit(solution)/shard_map/ppermute | solution.py:374
  37.8 0.3 shard_map.82.own.own_y
  38.1 1.7 %collective-permute-start.13 = (f32[264,256]{1,0:T(8,128)S(1)}, f32[264,256]{1,0:T(8,128)S(1)}, u32[]{:S(2)}, u32[]{:S(2)}) collective-permute-start(f32[264,256]{1,0:T(8,128)S(1)} %shard_map.82.own.own_y), channel_id=1, source_target_pairs={{0,8},{4,12},{8,0},{12,4},{16,24},{20,28},{24,16},{28,20},{32,40},... | collective-permute-start | bytes 811016 | tf_op jit(solution)/shard_map/ppermute | solution.py:381
  39.8 4.3 %shard_map.83 = (bf16[16,256,256]{2,1,0:T(8,128)(2,1)S(1)}, bf16[16,256,256]{2,1,0:T(8,128)(2,1)S(1)}, f32[16,256]{1,0:T(8,128)S(1)}, f32[264,256]{1,0:T(8,128)S(1)}) custom-call(bf16[4,256,256]{2,1,0:T(8,128)(2,1)S(1)} %get-tuple-element.54.refs_0_, bf16[4,256,256]{2,1,0:T(8,128)(2,1)S(1)} %get-tuple-element.55.refs_1_, ...), custom_call_target="tpu_custom_call" | custom-call | bytes 12935168 | tf_op jit(solution)/shard_map/pallas_call | solution.py:81
  44.1 0.1 collective-permute-start.15
  44.2 2.7 %collective-permute-done.13.partner.partner_y = f32[264,256]{1,0:T(8,128)S(1)} collective-permute-done((f32[264,256]{1,0:T(8,128)S(1)}, f32[264,256]{1,0:T(8,128)S(1)}, u32[]{:S(2)}, u32[]{:S(2)}) %collective-permute-start.13) | collective-permute-done | bytes 270368 | tf_op jit(solution)/shard_map/ppermute | solution.py:381
  46.8 0.3 shard_map.84.duo.duo_y
  47.1 2.8 %collective-permute-start.14 = (f32[264,256]{1,0:T(8,128)S(1)}, f32[264,256]{1,0:T(8,128)S(1)}, u32[]{:S(2)}, u32[]{:S(2)}) collective-permute-start(f32[264,256]{1,0:T(8,128)S(1)} %shard_map.84.duo.duo_y), channel_id=1, source_target_pairs={{0,24},{4,28},{8,16},{12,20},{16,8},{20,12},{24,0},{28,4},{32,56},... | collective-permute-start | bytes 811016 | tf_op jit(solution)/shard_map/ppermute | solution.py:381
  50.0 3.9 %shard_map.85 = (bf16[16,256,256]{2,1,0:T(8,128)(2,1)S(1)}, bf16[16,256,256]{2,1,0:T(8,128)(2,1)S(1)}) custom-call(bf16[4,256,256]{2,1,0:T(8,128)(2,1)S(1)} %get-tuple-element.54.refs_0_, bf16[4,256,256]{2,1,0:T(8,128)(2,1)S(1)} %get-tuple-element.55.refs_1_, bf16[4,256,256]{2,1,0:T(8,128)(2,1)S(1)} %get-tuple-element.56.refs_2_, ...), custom_call_target="tpu_custom_call" | custom-call | bytes 8454144 | tf_op jit(solution)/shard_map/pallas_call | solution.py:81
  53.9 2.2 %collective-permute-done.14.other_duo.other_y = f32[264,256]{1,0:T(8,128)S(1)} collective-permute-done((f32[264,256]{1,0:T(8,128)S(1)}, f32[264,256]{1,0:T(8,128)S(1)}, u32[]{:S(2)}, u32[]{:S(2)}) %collective-permute-start.14) | collective-permute-done | bytes 270368 | tf_op jit(solution)/shard_map/ppermute | solution.py:381
  56.1 0.5 shard_map.86
  56.6 5.1 %collective-permute-start.17 = (f32[264,256]{1,0:T(8,128)S(1)}, f32[264,256]{1,0:T(8,128)S(1)}, u32[]{:S(2)}, u32[]{:S(2)}) collective-permute-start(f32[264,256]{1,0:T(8,128)S(1)} %get-tuple-element.76), channel_id=1, source_target_pairs={{0,64},{8,72},{16,80},{24,88},{32,96},{40,104},{48,112},{56,120},{... | collective-permute-start | bytes 811016 | tf_op jit(solution)/shard_map/ppermute | solution.py:395
  61.7 2.6 %collective-permute-start.16 = (f32[264,256]{1,0:T(8,128)S(1)}, f32[264,256]{1,0:T(8,128)S(1)}, u32[]{:S(2)}, u32[]{:S(2)}) collective-permute-start(f32[264,256]{1,0:T(8,128)S(1)} %get-tuple-element.76), channel_id=1, source_target_pairs={{0,32},{8,40},{16,48},{24,56},{32,64},{40,72},{48,80},{56,88},{64,... | collective-permute-start | bytes 811016 | tf_op jit(solution)/shard_map/ppermute | solution.py:395
  64.3 1.3 %collective-permute-start.18 = (f32[8,256]{1,0:T(8,128)S(1)}, f32[8,256]{1,0:T(8,128)S(1)}, u32[]{:S(2)}, u32[]{:S(2)}) collective-permute-start(f32[8,256]{1,0:T(8,128)S(1)} %get-tuple-element.77), channel_id=1, source_target_pairs={{0,96},{8,104},{16,112},{24,120},{1,97},{9,105},{17,113},{25,121},... | collective-permute-start | bytes 24584 | tf_op jit(solution)/shard_map/ppermute | solution.py:395
  65.6 0.6 shard_map.87.z_chip
  66.3 0.7 collective-permute-done.18.tail
  67.0 0.0 collective-permute-done.17.far
  67.0 1.6 %collective-permute-done.16.near = f32[264,256]{1,0:T(8,128)S(1)} collective-permute-done((f32[264,256]{1,0:T(8,128)S(1)}, f32[264,256]{1,0:T(8,128)S(1)}, u32[]{:S(2)}, u32[]{:S(2)}) %collective-permute-start.16) | collective-permute-done | bytes 270368 | tf_op jit(solution)/shard_map/ppermute | solution.py:395
  68.6 0.6 shard_map.88
  69.2 2.3 %collective-permute-start.20 = (f32[8,256]{1,0:T(8,128)S(1)}, f32[8,256]{1,0:T(8,128)S(1)}, u32[]{:S(2)}, u32[]{:S(2)}) collective-permute-start(f32[8,256]{1,0:T(8,128)S(1)} %get-tuple-element.80), channel_id=1, source_target_pairs={{0,12},{8,4},{16,28},{24,20},{32,44},{40,36},{48,60},{56,52},{64,7... | collective-permute-start | bytes 24584 | tf_op jit(solution)/shard_map/ppermute | solution.py:381
  71.5 0.0 collective-permute-done.19.sent_ref.sent
  71.5 1.2 %shard_map.89 = (f32[16,256]{1,0:T(8,128)S(1)}, f32[16,256]{1,0:T(8,128)S(1)}, f32[8,256]{1,0:T(8,128)S(1)}) custom-call(f32[24,256]{1,0:T(8,128)S(1)} %get-tuple-element.79.means_ref, f32[24,256]{1,0:T(8,128)S(1)} %collective-permute-done.19.sent_ref.sent, f32[264,256]{1,0:T(8,128)S(1)} %collective-permute-done.15.refs_0_.z_other, ...), custom_call_target="tpu_custom_call" | custom-call | bytes 8830976 | tf_op jit(solution)/shard_map/pallas_call | solution.py:81
  72.8 0.1 collective-permute-done.20.partner_v
  72.8 0.2 shard_map.90.duo_v
  73.0 0.7 collective-permute-start.21
  73.7 0.3 shard_map.91
  74.0 0.7 collective-permute-start.24
  74.7 0.7 collective-permute-start.23
  75.3 0.7 collective-permute-start.22
  76.0 0.0 collective-permute-done.24.v3
  76.0 0.5 shard_map.92.sigma_ref
  76.6 11.9 %collective-permute-start.25 = (f32[8,256]{1,0:T(8,128)S(1)}, f32[8,256]{1,0:T(8,128)S(1)}, u32[]{:S(2)}, u32[]{:S(2)}) collective-permute-start(f32[8,256]{1,0:T(8,128)S(1)} %shard_map.92.sigma_ref), channel_id=1, source_target_pairs={{0,4},{4,0},{8,12},{12,8},{16,20},{20,16},{24,28},{28,24},{32,36},... | collective-permute-start | bytes 24584 | tf_op jit(solution)/shard_map/ppermute | solution.py:374
  88.5 0.8 collective-permute-done.25.sent_ref
  89.4 1.8 %shard_map.93 = (f32[16,64]{1,0:T(8,128)}, f32[16,64]{1,0:T(8,128)}) custom-call(f32[8,256]{1,0:T(8,128)S(1)} %shard_map.92.sigma_ref, f32[8,256]{1,0:T(8,128)S(1)} %collective-permute-done.25.sent_ref, f32[528,256]{1,0:T(8,128)S(1)} %collective-permute-done.12.other_ref, f32[8,256]{1,0:T(8,128)S(1)} %get-tuple-element.87.mid_ref, ...), custom_call_target="tpu_custom_call" | custom-call | bytes 4866048 | tf_op jit(solution)/shard_map/pallas_call | solution.py:81
  (13 shorter events, 0.0 us)
Async XLA Ops:
  3.2 10.2 %collective-permute-start.9 = (f32[392,128]{1,0:T(8,128)}, f32[392,128]{1,0:T(8,128)S(1)}, u32[]{:S(2)}, u32[]{:S(2)}) collective-permute-start(f32[392,128]{1,0:T(8,128)} %get-tuple-element.49.refs_0_), channel_id=1, source_target_pairs={{0,1},{1,2},{2,3},{3,0},{4,5},{5,6},{6,7},{7,4},{8,9},{9,10},{10,1... | collective-permute-start | bytes 602120 | tf_op jit(solution)/shard_map/ppermute | solution.py:366
  5.3 11.4 %collective-permute-start.4 = (f32[392,128]{1,0:T(8,128)}, f32[392,128]{1,0:T(8,128)S(1)}, u32[]{:S(2)}, u32[]{:S(2)}) collective-permute-start(f32[392,128]{1,0:T(8,128)} %get-tuple-element.47.refs_0_), channel_id=1, source_target_pairs={{0,3},{1,0},{2,1},{3,2},{4,7},{5,4},{6,5},{7,6},{8,11},{9,8},{10,9... | collective-permute-start | bytes 602120 | tf_op jit(solution)/shard_map/ppermute | solution.py:366
  7.5 10.2 %collective-permute-start.6 = (f32[392,128]{1,0:T(8,128)}, f32[392,128]{1,0:T(8,128)S(1)}, u32[]{:S(2)}, u32[]{:S(2)}) collective-permute-start(f32[392,128]{1,0:T(8,128)} %get-tuple-element.48.refs_0_), channel_id=1, source_target_pairs={{0,1},{1,2},{2,3},{3,0},{4,5},{5,6},{6,7},{7,4},{8,9},{9,10},{10,1... | collective-permute-start | bytes 602120 | tf_op jit(solution)/shard_map/ppermute | solution.py:366
  7.5 11.2 %collective-permute-start.11 = (f32[392,128]{1,0:T(8,128)}, f32[392,128]{1,0:T(8,128)S(1)}, u32[]{:S(2)}, u32[]{:S(2)}) collective-permute-start(f32[392,128]{1,0:T(8,128)} %get-tuple-element.49.refs_0_), channel_id=1, source_target_pairs={{0,3},{1,0},{2,1},{3,2},{4,7},{5,4},{6,5},{7,6},{8,11},{9,8},{10,9... | collective-permute-start | bytes 602120 | tf_op jit(solution)/shard_map/ppermute | solution.py:366
  13.4 8.9 %collective-permute-start.10 = (f32[392,128]{1,0:T(8,128)S(1)}, f32[392,128]{1,0:T(8,128)S(1)}, u32[]{:S(2)}, u32[]{:S(2)}) collective-permute-start(f32[392,128]{1,0:T(8,128)S(1)} %collective-permute-done.9.refs_1_), channel_id=1, source_target_pairs={{0,1},{1,2},{2,3},{3,0},{4,5},{5,6},{6,7},{7,4},{8,9},{9,10},{10,1... | collective-permute-start | bytes 602120 | tf_op jit(solution)/shard_map/ppermute | solution.py:366
  13.4 13.2 %copy-start = (f32[392,128]{1,0:T(8,128)S(1)}, f32[392,128]{1,0:T(8,128)}, u32[]{:S(2)}) copy-start(f32[392,128]{1,0:T(8,128)} %get-tuple-element.46.refs_0_) | copy-start | bytes 602116
  13.4 16.9 %copy-start.2 = (f32[392,128]{1,0:T(8,128)S(1)}, f32[392,128]{1,0:T(8,128)}, u32[]{:S(2)}) copy-start(f32[392,128]{1,0:T(8,128)} %get-tuple-element.48.refs_0_) | copy-start | bytes 602116
  13.4 13.2 %collective-permute-start.1 = (f32[392,128]{1,0:T(8,128)}, f32[392,128]{1,0:T(8,128)S(1)}, u32[]{:S(2)}, u32[]{:S(2)}) collective-permute-start(f32[392,128]{1,0:T(8,128)} %get-tuple-element.46.refs_0_), channel_id=1, source_target_pairs={{0,3},{1,0},{2,1},{3,2},{4,7},{5,4},{6,5},{7,6},{8,11},{9,8},{10,9... | collective-permute-start | bytes 602120 | tf_op jit(solution)/shard_map/ppermute | solution.py:366
  16.7 10.4 %collective-permute-start.8 = (f32[392,128]{1,0:T(8,128)}, f32[392,128]{1,0:T(8,128)S(1)}, u32[]{:S(2)}, u32[]{:S(2)}) collective-permute-start(f32[392,128]{1,0:T(8,128)} %get-tuple-element.48.refs_0_), channel_id=1, source_target_pairs={{0,3},{1,0},{2,1},{3,2},{4,7},{5,4},{6,5},{7,6},{8,11},{9,8},{10,9... | collective-permute-start | bytes 602120 | tf_op jit(solution)/shard_map/ppermute | solution.py:366
  17.7 12.6 %collective-permute-start.7 = (f32[392,128]{1,0:T(8,128)S(1)}, f32[392,128]{1,0:T(8,128)S(1)}, u32[]{:S(2)}, u32[]{:S(2)}) collective-permute-start(f32[392,128]{1,0:T(8,128)S(1)} %collective-permute-done.6.refs_1_), channel_id=1, source_target_pairs={{0,1},{1,2},{2,3},{3,0},{4,5},{5,6},{6,7},{7,4},{8,9},{9,10},{10,1... | collective-permute-start | bytes 602120 | tf_op jit(solution)/shard_map/ppermute | solution.py:366
  18.7 13.3 %collective-permute-start.3 = (f32[392,128]{1,0:T(8,128)}, f32[392,128]{1,0:T(8,128)S(1)}, u32[]{:S(2)}, u32[]{:S(2)}) collective-permute-start(f32[392,128]{1,0:T(8,128)} %get-tuple-element.47.refs_0_), channel_id=1, source_target_pairs={{0,1},{1,2},{2,3},{3,0},{4,5},{5,6},{6,7},{7,4},{8,9},{9,10},{10,1... | collective-permute-start | bytes 602120 | tf_op jit(solution)/shard_map/ppermute | solution.py:366
  22.4 9.6 %collective-permute-start.5 = (f32[392,128]{1,0:T(8,128)S(1)}, f32[392,128]{1,0:T(8,128)S(1)}, u32[]{:S(2)}, u32[]{:S(2)}) collective-permute-start(f32[392,128]{1,0:T(8,128)S(1)} %collective-permute-done.4.refs_3_), channel_id=1, source_target_pairs={{0,3},{1,0},{2,1},{3,2},{4,7},{5,4},{6,5},{7,6},{8,11},{9,8},{10,9... | collective-permute-start | bytes 602120 | tf_op jit(solution)/shard_map/ppermute | solution.py:366
  24.1 0.9 %copy-start.3 = (f32[392,128]{1,0:T(8,128)S(1)}, f32[392,128]{1,0:T(8,128)}, u32[]{:S(2)}) copy-start(f32[392,128]{1,0:T(8,128)} %get-tuple-element.49.refs_0_) | copy-start | bytes 602116
  26.7 7.4 %collective-permute-start = (f32[392,128]{1,0:T(8,128)S(1)}, f32[392,128]{1,0:T(8,128)S(1)}, u32[]{:S(2)}, u32[]{:S(2)}) collective-permute-start(f32[392,128]{1,0:T(8,128)S(1)} %copy-done), channel_id=1, source_target_pairs={{0,1},{1,2},{2,3},{3,0},{4,5},{5,6},{6,7},{7,4},{8,9},{9,10},{10,1... | collective-permute-start | bytes 602120 | tf_op jit(solution)/shard_map/ppermute | solution.py:366
  27.0 7.1 %collective-permute-start.2 = (f32[392,128]{1,0:T(8,128)S(1)}, f32[392,128]{1,0:T(8,128)S(1)}, u32[]{:S(2)}, u32[]{:S(2)}) collective-permute-start(f32[392,128]{1,0:T(8,128)S(1)} %collective-permute-done.1.refs_3_), channel_id=1, source_target_pairs={{0,3},{1,0},{2,1},{3,2},{4,7},{5,4},{6,5},{7,6},{8,11},{9,8},{10,9... | collective-permute-start | bytes 602120 | tf_op jit(solution)/shard_map/ppermute | solution.py:366
  30.3 1.7 %copy-start.1 = (f32[392,128]{1,0:T(8,128)S(1)}, f32[392,128]{1,0:T(8,128)}, u32[]{:S(2)}) copy-start(f32[392,128]{1,0:T(8,128)} %get-tuple-element.47.refs_0_) | copy-start | bytes 602116
  35.7 2.0 %collective-permute-start.12 = (f32[528,256]{1,0:T(8,128)S(1)}, f32[528,256]{1,0:T(8,128)S(1)}, u32[]{:S(2)}, u32[]{:S(2)}) collective-permute-start(f32[528,256]{1,0:T(8,128)S(1)} %get-tuple-element.53.own_ref), channel_id=1, source_target_pairs={{0,4},{4,0},{8,12},{12,8},{16,20},{20,16},{24,28},{28,24},{32,36},... | collective-permute-start | bytes 1622024 | tf_op jit(solution)/shard_map/ppermute | solution.py:374
  38.1 8.8 %collective-permute-start.13 = (f32[264,256]{1,0:T(8,128)S(1)}, f32[264,256]{1,0:T(8,128)S(1)}, u32[]{:S(2)}, u32[]{:S(2)}) collective-permute-start(f32[264,256]{1,0:T(8,128)S(1)} %shard_map.82.own.own_y), channel_id=1, source_target_pairs={{0,8},{4,12},{8,0},{12,4},{16,24},{20,28},{24,16},{28,20},{32,40},... | collective-permute-start | bytes 811016 | tf_op jit(solution)/shard_map/ppermute | solution.py:381
  44.1 9.8 %collective-permute-start.15 = (f32[264,256]{1,0:T(8,128)S(1)}, f32[264,256]{1,0:T(8,128)S(1)}, u32[]{:S(2)}, u32[]{:S(2)}) collective-permute-start(f32[264,256]{1,0:T(8,128)S(1)} %get-tuple-element.74._.z_own), channel_id=1, source_target_pairs={{0,4},{4,0},{8,12},{12,8},{16,20},{20,16},{24,28},{28,24},{32,36},... | collective-permute-start | bytes 811016 | tf_op jit(solution)/shard_map/ppermute | solution.py:374
  47.1 9.0 %collective-permute-start.14 = (f32[264,256]{1,0:T(8,128)S(1)}, f32[264,256]{1,0:T(8,128)S(1)}, u32[]{:S(2)}, u32[]{:S(2)}) collective-permute-start(f32[264,256]{1,0:T(8,128)S(1)} %shard_map.84.duo.duo_y), channel_id=1, source_target_pairs={{0,24},{4,28},{8,16},{12,20},{16,8},{20,12},{24,0},{28,4},{32,56},... | collective-permute-start | bytes 811016 | tf_op jit(solution)/shard_map/ppermute | solution.py:381
  56.6 10.4 %collective-permute-start.17 = (f32[264,256]{1,0:T(8,128)S(1)}, f32[264,256]{1,0:T(8,128)S(1)}, u32[]{:S(2)}, u32[]{:S(2)}) collective-permute-start(f32[264,256]{1,0:T(8,128)S(1)} %get-tuple-element.76), channel_id=1, source_target_pairs={{0,64},{8,72},{16,80},{24,88},{32,96},{40,104},{48,112},{56,120},{... | collective-permute-start | bytes 811016 | tf_op jit(solution)/shard_map/ppermute | solution.py:395
  61.7 6.9 %collective-permute-start.16 = (f32[264,256]{1,0:T(8,128)S(1)}, f32[264,256]{1,0:T(8,128)S(1)}, u32[]{:S(2)}, u32[]{:S(2)}) collective-permute-start(f32[264,256]{1,0:T(8,128)S(1)} %get-tuple-element.76), channel_id=1, source_target_pairs={{0,32},{8,40},{16,48},{24,56},{32,64},{40,72},{48,80},{56,88},{64,... | collective-permute-start | bytes 811016 | tf_op jit(solution)/shard_map/ppermute | solution.py:395
  64.3 2.6 %collective-permute-start.18 = (f32[8,256]{1,0:T(8,128)S(1)}, f32[8,256]{1,0:T(8,128)S(1)}, u32[]{:S(2)}, u32[]{:S(2)}) collective-permute-start(f32[8,256]{1,0:T(8,128)S(1)} %get-tuple-element.77), channel_id=1, source_target_pairs={{0,96},{8,104},{16,112},{24,120},{1,97},{9,105},{17,113},{25,121},... | collective-permute-start | bytes 24584 | tf_op jit(solution)/shard_map/ppermute | solution.py:395
  69.2 2.3 %collective-permute-start.19 = (f32[24,256]{1,0:T(8,128)S(1)}, f32[24,256]{1,0:T(8,128)S(1)}, u32[]{:S(2)}, u32[]{:S(2)}) collective-permute-start(f32[24,256]{1,0:T(8,128)S(1)} %get-tuple-element.79.means_ref), channel_id=1, source_target_pairs={{0,4},{4,0},{8,12},{12,8},{16,20},{20,16},{24,28},{28,24},{32,36},... | collective-permute-start | bytes 73736 | tf_op jit(solution)/shard_map/ppermute | solution.py:374
  69.2 3.7 %collective-permute-start.20 = (f32[8,256]{1,0:T(8,128)S(1)}, f32[8,256]{1,0:T(8,128)S(1)}, u32[]{:S(2)}, u32[]{:S(2)}) collective-permute-start(f32[8,256]{1,0:T(8,128)S(1)} %get-tuple-element.80), channel_id=1, source_target_pairs={{0,12},{8,4},{16,28},{24,20},{32,44},{40,36},{48,60},{56,52},{64,7... | collective-permute-start | bytes 24584 | tf_op jit(solution)/shard_map/ppermute | solution.py:381
  73.0 0.7 collective-permute-start.21
  74.0 2.0 %collective-permute-start.24 = (f32[8,256]{1,0:T(8,128)S(1)}, f32[8,256]{1,0:T(8,128)S(1)}, u32[]{:S(2)}, u32[]{:S(2)}) collective-permute-start(f32[8,256]{1,0:T(8,128)S(1)} %get-tuple-element.85), channel_id=1, source_target_pairs={{100,4},{108,12},{116,20},{124,28},{101,5},{109,13},{117,21},{125,... | collective-permute-start | bytes 24584 | tf_op jit(solution)/shard_map/ppermute | solution.py:395
  74.7 1.4 %collective-permute-start.23 = (f32[8,256]{1,0:T(8,128)S(1)}, f32[8,256]{1,0:T(8,128)S(1)}, u32[]{:S(2)}, u32[]{:S(2)}) collective-permute-start(f32[8,256]{1,0:T(8,128)S(1)} %get-tuple-element.85), channel_id=1, source_target_pairs={{100,36},{108,44},{116,52},{124,60},{68,4},{76,12},{84,20},{92,28}... | collective-permute-start | bytes 24584 | tf_op jit(solution)/shard_map/ppermute | solution.py:395
  75.3 0.7 collective-permute-start.22
  76.6 12.8 %collective-permute-start.25 = (f32[8,256]{1,0:T(8,128)S(1)}, f32[8,256]{1,0:T(8,128)S(1)}, u32[]{:S(2)}, u32[]{:S(2)}) collective-permute-start(f32[8,256]{1,0:T(8,128)S(1)} %shard_map.92.sigma_ref), channel_id=1, source_target_pairs={{0,4},{4,0},{8,12},{12,8},{16,20},{20,16},{24,28},{28,24},{32,36},... | collective-permute-start | bytes 24584 | tf_op jit(solution)/shard_map/ppermute | solution.py:374

commit v3 on v2

--- a/solution.py
+++ b/solution.py
@@ -231,20 +231,58 @@
     z_ref[...] = zl + mul_nt(then(xl, zr), yl)
 
 
+def own_columns(a):
+    place = lax.axis_index("state")
+    own = a[:, :BLOCK]
+    for b in range(1, BLOCKS):
+        own = jnp.where(place == b, a[:, b * BLOCK : (b + 1) * BLOCK], own)
+    return own
+
+
+def own_pair(first, second):
+    place = lax.axis_index("state")
+    two = 2 * BLOCK
+    odd = lax.rem(place, 2) == 1
+    first, second = (
+        jnp.where(place < 2, a[:, :two], a[:, two:]) for a in (first, second)
+    )
+    low = jnp.where(odd, pltpu.roll(first, BLOCK, 1), first)
+    high = jnp.where(odd, second, pltpu.roll(second, BLOCK, 1))
+    lane = lax.broadcasted_iota(jnp.int32, low.shape, 1)
+    return jnp.where(lane < BLOCK, low, high)
+
+
+def put_pair(hi_ref, lo_ref, slot, first, second):
+    at = slot % 4 * BLOCK
+    part = slice(at, at + 2 * BLOCK)
+    hi_ref[slot // 4, :, part], lo_ref[slot // 4, :, part] = split(own_pair(first, second))
+
+
+def by_steps(row, hi_ref, lo_ref):
+    rows = []
+    for k in range(STEPS // 4):
+        wide = rows_by(dot_nn, row, (hi_ref[k], lo_ref[k]))[0:1]
+        rows += [wide[:, i * BLOCK : (i + 1) * BLOCK] for i in range(4)]
+    return jnp.concatenate(rows, axis=0)
+
+
 def suffix_kernel(*refs):
     his, los, vecs = (refs[i * CHUNKS : (i + 1) * CHUNKS] for i in range(3))
     shi_ref, slo_ref = refs[-2:]
-    run = identity_matrix()
+    run = held = identity_matrix()
     for t in range(STEPS - 1, 0, -1):
         q, i = ENDS[t]
         run = three(dot_nn, split(run * vecs[q][2, i : i + 1, :]), (his[q][i], los[q][i]))
-        shi_ref[t], slo_ref[t] = split(run)
+        if t % 2 == 0:
+            held = run
+        else:
+            put_pair(shi_ref, slo_ref, t - 1, run, held)
 
 
 def suffix_z_kernel(*refs):
     his, los, this, tlos, vecs = (refs[i * CHUNKS : (i + 1) * CHUNKS] for i in range(5))
-    zhi_ref, zlo_ref, v_ref, z_ref = refs[5 * CHUNKS :]
-    z = jnp.zeros((STATE, STATE), f32)
+    zhi_ref, zlo_ref, thi_ref, tlo_ref, v_ref, z_ref = refs[5 * CHUNKS :]
+    z = held = jnp.zeros((STATE, STATE), f32)
     v = jnp.zeros((8, STATE), f32)
     v_ref[...] = jnp.zeros((STEPS, STATE), f32)
     for t in range(STEPS - 1, -1, -1):
@@ -252,11 +290,17 @@
         w, o, g, p = (vecs[q][k, i : i + 1, :] for k in range(4))
         step = (his[q][i], los[q][i])
         moved = this[q][i].astype(f32) + tlos[q][i].astype(f32)
+        if t % 2 == 0:
+            put_pair(thi_ref, tlo_ref, t, moved, after)
+        after = moved
         z = three(dot_nn, split(z * g - moved * w), step)
         v = rows_by(dot_nn, v * g + first_row(w * (o - p)), step)
         if t > 0:
-            zhi_ref[t], zlo_ref[t] = split(z)
-            v_ref[t : t + 1, :] = v[0:1]
+            v_ref[t - 1 : t, :] = v[0:1]
+            if t % 2 == 0:
+                held = z
+            else:
+                put_pair(zhi_ref, zlo_ref, t - 1, z, held)
     z_ref[:STATE] = z
     z_ref[STATE:] = v
 
@@ -290,31 +334,31 @@
     m = mul_nn(inner, near[:STATE]) + near[STATE:]
     m = mul_nn(m, side_ref[:STATE]) + side_ref[STATE:]
     v = mul_nn(m, z_chip[:STATE]) + z_chip[STATE:]
-    v_ref[...] = v
+    v_ref[:8] = v
+    v_ref[8:] = jnp.zeros((40, STATE), f32)
     means_ref[:8] = v
     means_ref[8:16] = m
     means_ref[16:] = mul_nn(m, own_ref[:STATE]) + own_ref[STATE:AUG]
 
 
-def local_kernel(means_ref, sent_ref, z_other, zhi_ref, zlo_ref, v_ref, *refs):
-    this, tlos, vecs = (refs[i * CHUNKS : (i + 1) * CHUNKS] for i in range(3))
-    m_ref, h_ref, mid_ref = refs[3 * CHUNKS :]
+def local_kernel(
+    means_ref, sent_ref, z_other, zhi_ref, zlo_ref, thi_ref, tlo_ref, v_ref, *refs
+):
+    vecs = refs[:CHUNKS]
+    m_ref, h_ref, mid_ref = refs[CHUNKS:]
     mid_ref[...] = mul_nn(means_ref[16:], z_other[:STATE]) + z_other[STATE:]
     enter = jnp.where(core_of() == 0, means_ref[8:16], sent_ref[16:])
-    for q in range(CHUNKS):
-        rows = [rows_by(dot_nn, enter, (this[q][i], tlos[q][i]))[0:1] for i in range(SIZES[q])]
-        p = jnp.concatenate(rows, axis=0) + vecs[q][3]
-        e = vecs[q][0] * (vecs[q][1] - p)
-        m_ref[STARTS[q] : STARTS[q] + SIZES[q], :] = p + e
-    for t in range(STEPS - 1):
-        row = rows_by(dot_nn, enter, (zhi_ref[t + 1], zlo_ref[t + 1]))[0:1]
-        h_ref[t : t + 1, :] = row + v_ref[t + 1 : t + 2, :]
-    h_ref[STEPS - 1 :, :] = jnp.zeros((1, STATE), f32)
+    w, o, p = (
+        own_columns(jnp.concatenate([v[k] for v in vecs], axis=0)) for k in (0, 1, 3)
+    )
+    p = by_steps(enter, thi_ref, tlo_ref) + p
+    m_ref[...] = p + w * (o - p)
+    h_ref[...] = by_steps(enter, zhi_ref, zlo_ref) + own_columns(v_ref[...])
 
 
 def duo_v_kernel(sent, partner_v, own_y, partner_y, _, out_ref):
     even = lax.rem(x_of(), 2) == 0
-    mine, theirs = sent[:8], partner_v[...]
+    mine, theirs = sent[:8], partner_v[:8]
     y = jnp.where(even, own_y[:STATE], partner_y[:STATE])
     out_ref[...] = jnp.where(even, mine, theirs) + mul_nt(jnp.where(even, theirs, mine), y)
 
@@ -322,7 +366,7 @@
 def row_v_kernel(duo_v, other_v, partner_v, duo_y, other_y, partner_y, whole_ref, after_ref):
     x = x_of()
     low = x < 2
-    mine, theirs, beside = duo_v[...], other_v[...], partner_v[...]
+    mine, theirs, beside = duo_v[...], other_v[...], partner_v[:8]
     y = jnp.where(low, duo_y[:STATE], other_y[:STATE])
     whole_ref[...] = jnp.where(low, mine, theirs) + mul_nt(jnp.where(low, theirs, mine), y)
     outer = beside + mul_nt(theirs, partner_y[:STATE])
@@ -339,27 +383,11 @@
 
 def smooth_kernel(sigma_ref, sent_ref, other_ref, mid_ref, shi_ref, slo_ref, *refs):
     vecs = refs[:CHUNKS]
-    m_ref, h_ref, filt_ref, smooth_ref = refs[CHUNKS:]
-    place = lax.axis_index("state")
+    m_ref, h_ref, smooth_ref = refs[CHUNKS:]
     crossed = mul_nt(sent_ref[...], other_ref[PART_Y : PART_Y + STATE]) + mid_ref[...]
     sigma = jnp.where(core_of() == 0, crossed, sigma_ref[...])
-    rows = []
-    for t in range(STEPS):
-        if t == STEPS - 1:
-            rows.append(sigma[0:1])
-        else:
-            rows.append(rows_by(dot_nn, sigma, (shi_ref[t + 1], slo_ref[t + 1]))[0:1])
-    gain = jnp.concatenate([v[2] for v in vecs], axis=0)
-    filt = m_ref[...]
-    smooth = filt + gain * (h_ref[...] + jnp.concatenate(rows, axis=0))
-    out_f = filt[:, :BLOCK]
-    out_s = smooth[:, :BLOCK]
-    for b in range(1, BLOCKS):
-        part = slice(b * BLOCK, (b + 1) * BLOCK)
-        out_f = jnp.where(place == b, filt[:, part], out_f)
-        out_s = jnp.where(place == b, smooth[:, part], out_s)
-    filt_ref[...] = out_f
-    smooth_ref[...] = out_s
+    gain = own_columns(jnp.concatenate([v[2] for v in vecs], axis=0))
+    smooth_ref[...] = m_ref[...] + gain * (h_ref[...] + by_steps(sigma, shi_ref, slo_ref))
 
 
 def over_z(a, s):
@@ -438,17 +466,17 @@
     other = over_core(own)
     (side_own,) = call(pair_kernel, 0, [arr(AUG, STATE)], [own, other])
     partner = over_x(side_own, beside)
-    zhi, zlo, v_all, z_own = call(
+    zhi, zlo, thi, tlo, v_all, z_own = call(
         suffix_z_kernel,
         0,
-        [arr(STEPS, STATE, STATE, dtype=bf16)] * 2 + [arr(STEPS, STATE), arr(AUG, STATE)],
+        [arr(STEPS // 4, STATE, STATE, dtype=bf16)] * 4 + [arr(STEPS, STATE), arr(AUG, STATE)],
         his + los + this + tlos + vecs,
     )
     (duo,) = call(duo_kernel, 0, [arr(AUG, STATE)], [side_own, partner, z_own])
     other_duo = over_x(duo, opposite)
     z_other = over_core(z_own)
     shi, slo = call(
-        suffix_kernel, 0, [arr(STEPS, STATE, STATE, dtype=bf16)] * 2, his + los + vecs
+        suffix_kernel, 0, [arr(STEPS // 4, STATE, STATE, dtype=bf16)] * 2, his + los + vecs
     )
     whole, side, tail = call(
         row_kernel,
@@ -463,16 +491,16 @@
     means, v_chip = call(
         enter_kernel,
         0,
-        [arr(24, STATE), arr(8, STATE)],
+        [arr(24, STATE), arr(48, STATE)],
         [near, far, tail, side, own, z_chip],
     )
     partner_v = over_x(v_chip, beside, ((0, 1),))
     sent = over_core(means)
-    m_all, h_all, mid = call(
+    filtered, h_all, mid = call(
         local_kernel,
         0,
-        [arr(STEPS, STATE)] * 2 + [arr(8, STATE)],
-        [means, sent, z_other, zhi, zlo, v_all] + this + tlos + vecs,
+        [arr(STEPS, BLOCK)] * 2 + [arr(8, STATE)],
+        [means, sent, z_other, zhi, zlo, thi, tlo, v_all] + vecs,
     )
     (duo_v,) = call(
         duo_v_kernel, 0, [arr(8, STATE)], [sent, partner_v, side_own, partner, h_all]
@@ -491,11 +519,11 @@
     ]
     (sigma,) = call(leave_kernel, 0, [arr(8, STATE)], v_rows + [near, far, side, v_after])
     crossed = over_core(sigma)
-    filtered, smoothed = call(
+    (smoothed,) = call(
         smooth_kernel,
         0,
-        [arr(STEPS, BLOCK)] * 2,
-        [sigma, crossed, other, mid, shi, slo] + vecs + [m_all, h_all],
+        [arr(STEPS, BLOCK)],
+        [sigma, crossed, other, mid, shi, slo] + vecs + [filtered, h_all],
     )
     return filtered, smoothed
 

time: 92.7 us -> 90.6 us (0.977)
  starting transfers between devices: 49.5 us -> 46.9 us
    ppermute x4, starting transfers between devices: 12.1 us -> 10.5 us  [over_core(): return lax.ppermute(a, 'tm', [(i, i ^ 1) for i in range(32)])]
    ppermute x4, waiting for transfers between devices: 2.75 us -> 3.93 us  [over_core(): return lax.ppermute(a, 'tm', [(i, i ^ 1) for i in range(32)])]
    ppermute x4, starting transfers between devices: 7.55 us -> 6.55 us  [over_x(): return lax.ppermute(a, 'tm', route)]
where the time goes in v3:
time: 90.6 us; the launch traced here: 89.1 us
  starting transfers between devices  46.9 us (52%)
  Pallas kernels  23.5 us (26%)
  waiting for transfers between devices  16.8 us (19%)
  local copies, waits for them, and re-layouts  0.95 us (1%)
  between operations  0.92 us (1%)
    pallas_call x17, Pallas kernels, call(): pl.pallas_call(kernel, out_shape=outs, in_specs=[pl.BlockSpec(memory_spac...  23.5 us
    ppermute x12, starting transfers between devices, over_z(): return lax.ppermute(a, 'state', [(i, (i + s) % 4) for i in range(4)])  18.9 us
    ppermute x6, starting transfers between devices, over_y(): return lax.ppermute(a, 'tm', route)  11 us
    ppermute x4, starting transfers between devices, over_core(): return lax.ppermute(a, 'tm', [(i, i ^ 1) for i in range(32)])  10.5 us
    ppermute x4, starting transfers between devices, over_x(): return lax.ppermute(a, 'tm', route)  6.55 us
    ppermute x12, waiting for transfers between devices, over_z(): return lax.ppermute(a, 'state', [(i, (i + s) % 4) for i in range(4)])  6.1 us
    ppermute x4, waiting for transfers between devices, over_x(): return lax.ppermute(a, 'tm', route)  4.46 us
    ppermute x4, waiting for transfers between devices, over_core(): return lax.ppermute(a, 'tm', [(i, i ^ 1) for i in range(32)])  3.93 us
  transfers between devices with their start and end apart: 26, of which 11 were waited for; matrix products, arithmetic and copies ran while one was open for 0% of the time, Pallas kernels for 17%

profile of v3, /device:TPU:0, one launch (start us, length us, event | category | flops | bytes accessed | tf_op | source)
XLA Modules:
  0.0 89.1 jit_solution(18266754858951769004)
XLA Ops:
  0.6 2.6 %shard_map.77 = (f32[392,128]{1,0:T(8,128)}, f32[392,128]{1,0:T(8,128)}, f32[392,128]{1,0:T(8,128)}, f32[392,128]{1,0:T(8,128)}) custom-call(f32[16,12288]{1,0:T(8,128)} %dyn_hbm.1, s32[2,16]{1,0:T(2,128)} %bitcast.3, f32[16,64]{1,0:T(8,128)} %obs_hbm.1, s32[16,64]{1,0:T(8,128)} %mask_hbm.1, f32[16,64]{1,0:T(8,128)} %fgain_hbm.1, f32[16,64]{1,0:T(8,128)} %sgain_hbm.1), custom_call_target="tpu_custom_call" | custom-call | bytes 1605760 | tf_op jit(solution)/shard_map/pallas_call | solution.py:81
  3.2 2.1 %collective-permute-start.9 = (f32[392,128]{1,0:T(8,128)}, f32[392,128]{1,0:T(8,128)S(1)}, u32[]{:S(2)}, u32[]{:S(2)}) collective-permute-start(f32[392,128]{1,0:T(8,128)} %get-tuple-element.51.refs_0_), channel_id=1, source_target_pairs={{0,1},{1,2},{2,3},{3,0},{4,5},{5,6},{6,7},{7,4},{8,9},{9,10},{10,1... | collective-permute-start | bytes 602120 | tf_op jit(solution)/shard_map/ppermute | solution.py:394
  5.3 2.2 %collective-permute-start.4 = (f32[392,128]{1,0:T(8,128)}, f32[392,128]{1,0:T(8,128)S(1)}, u32[]{:S(2)}, u32[]{:S(2)}) collective-permute-start(f32[392,128]{1,0:T(8,128)} %get-tuple-element.49.refs_0_), channel_id=1, source_target_pairs={{0,3},{1,0},{2,1},{3,2},{4,7},{5,4},{6,5},{7,6},{8,11},{9,8},{10,9... | collective-permute-start | bytes 602120 | tf_op jit(solution)/shard_map/ppermute | solution.py:394
  7.5 0.0 collective-permute-start.6
  7.5 3.2 %collective-permute-start.11 = (f32[392,128]{1,0:T(8,128)}, f32[392,128]{1,0:T(8,128)S(1)}, u32[]{:S(2)}, u32[]{:S(2)}) collective-permute-start(f32[392,128]{1,0:T(8,128)} %get-tuple-element.51.refs_0_), channel_id=1, source_target_pairs={{0,3},{1,0},{2,1},{3,2},{4,7},{5,4},{6,5},{7,6},{8,11},{9,8},{10,9... | collective-permute-start | bytes 602120 | tf_op jit(solution)/shard_map/ppermute | solution.py:394
  10.7 2.7 %collective-permute-done.9.refs_1_ = f32[392,128]{1,0:T(8,128)S(1)} collective-permute-done((f32[392,128]{1,0:T(8,128)}, f32[392,128]{1,0:T(8,128)S(1)}, u32[]{:S(2)}, u32[]{:S(2)}) %collective-permute-start.9) | collective-permute-done | bytes 200736 | tf_op jit(solution)/shard_map/ppermute | solution.py:394
  13.4 0.0 collective-permute-start.10
  13.4 3.2 %collective-permute-start.1 = (f32[392,128]{1,0:T(8,128)}, f32[392,128]{1,0:T(8,128)S(1)}, u32[]{:S(2)}, u32[]{:S(2)}) collective-permute-start(f32[392,128]{1,0:T(8,128)} %get-tuple-element.48.refs_0_), channel_id=1, source_target_pairs={{0,3},{1,0},{2,1},{3,2},{4,7},{5,4},{6,5},{7,6},{8,11},{9,8},{10,9... | collective-permute-start | bytes 602120 | tf_op jit(solution)/shard_map/ppermute | solution.py:394
  16.7 0.0 collective-permute-done.4.refs_3_
  16.7 0.8 collective-permute-start.8
  17.5 0.2 collective-permute-done.6.refs_1_
  17.7 1.0 %collective-permute-start.7 = (f32[392,128]{1,0:T(8,128)S(1)}, f32[392,128]{1,0:T(8,128)S(1)}, u32[]{:S(2)}, u32[]{:S(2)}) collective-permute-start(f32[392,128]{1,0:T(8,128)S(1)} %collective-permute-done.6.refs_1_), channel_id=1, source_target_pairs={{0,1},{1,2},{2,3},{3,0},{4,5},{5,6},{6,7},{7,4},{8,9},{9,10},{10,1... | collective-permute-start | bytes 602120 | tf_op jit(solution)/shard_map/ppermute | solution.py:394
  18.7 0.0 collective-permute-done.11.refs_3_
  18.7 0.9 %collective-permute-start.3 = (f32[392,128]{1,0:T(8,128)}, f32[392,128]{1,0:T(8,128)S(1)}, u32[]{:S(2)}, u32[]{:S(2)}) collective-permute-start(f32[392,128]{1,0:T(8,128)} %get-tuple-element.49.refs_0_), channel_id=1, source_target_pairs={{0,1},{1,2},{2,3},{3,0},{4,5},{5,6},{6,7},{7,4},{8,9},{9,10},{10,1... | collective-permute-start | bytes 602120 | tf_op jit(solution)/shard_map/ppermute | solution.py:394
  19.6 2.7 %collective-permute-done.10.refs_2_ = f32[392,128]{1,0:T(8,128)S(1)} collective-permute-done((f32[392,128]{1,0:T(8,128)S(1)}, f32[392,128]{1,0:T(8,128)S(1)}, u32[]{:S(2)}, u32[]{:S(2)}) %collective-permute-start.10) | collective-permute-done | bytes 200736 | tf_op jit(solution)/shard_map/ppermute | solution.py:394
  22.3 1.7 %collective-permute-start.5 = (f32[392,128]{1,0:T(8,128)S(1)}, f32[392,128]{1,0:T(8,128)S(1)}, u32[]{:S(2)}, u32[]{:S(2)}) collective-permute-start(f32[392,128]{1,0:T(8,128)S(1)} %collective-permute-done.4.refs_3_), channel_id=1, source_target_pairs={{0,3},{1,0},{2,1},{3,2},{4,7},{5,4},{6,5},{7,6},{8,11},{9,8},{10,9... | collective-permute-start | bytes 602120 | tf_op jit(solution)/shard_map/ppermute | solution.py:394
  24.1 0.9 %copy-done.4 = f32[392,128]{1,0:T(8,128)S(1)} copy-done((f32[392,128]{1,0:T(8,128)S(1)}, f32[392,128]{1,0:T(8,128)}, u32[]{:S(2)}) %copy-start.4) | copy-done | bytes 200728
  25.0 1.6 %shard_map.78 = (bf16[4,256,256]{2,1,0:T(8,128)(2,1)S(1)}, bf16[4,256,256]{2,1,0:T(8,128)(2,1)S(1)}, bf16[4,256,256]{2,1,0:T(8,128)(2,1)S(1)}, bf16[4,256,256]{2...) custom-call(f32[392,128]{1,0:T(8,128)S(1)} %copy-done.4, ...), custom_call_target="tpu_custom_call" | custom-call | flops 1600000000 | bytes 3457024 | tf_op jit(solution)/shard_map/pallas_call | solution.py:81
  26.7 0.0 collective-permute-done.1.refs_3_
  26.7 0.4 collective-permute-start
  27.0 0.0 collective-permute-done.8.refs_3_
  27.0 3.3 %collective-permute-start.2 = (f32[392,128]{1,0:T(8,128)S(1)}, f32[392,128]{1,0:T(8,128)S(1)}, u32[]{:S(2)}, u32[]{:S(2)}) collective-permute-start(f32[392,128]{1,0:T(8,128)S(1)} %collective-permute-done.1.refs_3_), channel_id=1, source_target_pairs={{0,3},{1,0},{2,1},{3,2},{4,7},{5,4},{6,5},{7,6},{8,11},{9,8},{10,9... | collective-permute-start | bytes 602120 | tf_op jit(solution)/shard_map/ppermute | solution.py:394
  30.3 0.0 collective-permute-done.7.refs_2_
  30.3 1.6 %shard_map.79 = (bf16[4,256,256]{2,1,0:T(8,128)(2,1)S(1)}, bf16[4,256,256]{2,1,0:T(8,128)(2,1)S(1)}, bf16[4,256,256]{2,1,0:T(8,128)(2,1)S(1)}, bf16[4,256,256]{2...) custom-call(f32[392,128]{1,0:T(8,128)S(1)} %copy-done.3, ...), custom_call_target="tpu_custom_call" | custom-call | flops 1600000000 | bytes 3997696 | tf_op jit(solution)/shard_map/pallas_call | solution.py:81
  32.0 0.0 collective-permute-done.3.refs_1_
  32.0 0.0 collective-permute-done.5.refs_2_
  32.0 1.6 %shard_map.80 = (bf16[4,256,256]{2,1,0:T(8,128)(2,1)S(1)}, bf16[4,256,256]{2,1,0:T(8,128)(2,1)S(1)}, bf16[4,256,256]{2,1,0:T(8,128)(2,1)S(1)}, bf16[4,256,256]{2...) custom-call(f32[392,128]{1,0:T(8,128)S(1)} %copy-done.2, ...), custom_call_target="tpu_custom_call" | custom-call | flops 1600000000 | bytes 3997696 | tf_op jit(solution)/shard_map/pallas_call | solution.py:81
  33.7 0.4 collective-permute-done.refs_1_
  34.1 1.6 %shard_map.81 = (bf16[4,256,256]{2,1,0:T(8,128)(2,1)S(1)}, bf16[4,256,256]{2,1,0:T(8,128)(2,1)S(1)}, bf16[4,256,256]{2,1,0:T(8,128)(2,1)S(1)}, bf16[4,256,256]{2...) custom-call(f32[392,128]{1,0:T(8,128)S(1)} %copy-done.1, ...), custom_call_target="tpu_custom_call" | custom-call | flops 1600000000 | bytes 3997696 | tf_op jit(solution)/shard_map/pallas_call | solution.py:81
  35.7 0.1 collective-permute-start.12
  35.8 1.9 %collective-permute-done.12.other_ref = f32[528,256]{1,0:T(8,128)S(1)} collective-permute-done((f32[528,256]{1,0:T(8,128)S(1)}, f32[528,256]{1,0:T(8,128)S(1)}, u32[]{:S(2)}, u32[]{:S(2)}) %collective-permute-start.12) | collective-permute-done | bytes 540704 | tf_op jit(solution)/shard_map/ppermute | solution.py:402
  37.7 0.3 shard_map.82.own.own_y
  38.0 1.7 %collective-permute-start.13 = (f32[264,256]{1,0:T(8,128)S(1)}, f32[264,256]{1,0:T(8,128)S(1)}, u32[]{:S(2)}, u32[]{:S(2)}) collective-permute-start(f32[264,256]{1,0:T(8,128)S(1)} %shard_map.82.own.own_y), channel_id=1, source_target_pairs={{0,8},{4,12},{8,0},{12,4},{16,24},{20,28},{24,16},{28,20},{32,40},... | collective-permute-start | bytes 811016 | tf_op jit(solution)/shard_map/ppermute | solution.py:409
  39.8 4.6 %shard_map.83 = (bf16[4,256,256]{2,1,0:T(8,128)(2,1)S(1)}, bf16[4,256,256]{2,1,0:T(8,128)(2,1)S(1)}, bf16[4,256,256]{2,1,0:T(8,128)(2,1)S(1)}, bf16[4,256,256]{2...) custom-call(bf16[4,256,256]{2,1,0:T(8,128)(2,1)S(1)} %get-tuple-element.56.refs_0_, ...), custom_call_target="tpu_custom_call" | custom-call | bytes 10838016 | tf_op jit(solution)/shard_map/pallas_call | solution.py:81
  44.4 0.1 collective-permute-start.15
  44.5 2.3 %collective-permute-done.13.partner.partner_y = f32[264,256]{1,0:T(8,128)S(1)} collective-permute-done((f32[264,256]{1,0:T(8,128)S(1)}, f32[264,256]{1,0:T(8,128)S(1)}, u32[]{:S(2)}, u32[]{:S(2)}) %collective-permute-start.13) | collective-permute-done | bytes 270368 | tf_op jit(solution)/shard_map/ppermute | solution.py:409
  46.8 0.3 shard_map.84.duo.duo_y
  47.1 2.8 %collective-permute-start.14 = (f32[264,256]{1,0:T(8,128)S(1)}, f32[264,256]{1,0:T(8,128)S(1)}, u32[]{:S(2)}, u32[]{:S(2)}) collective-permute-start(f32[264,256]{1,0:T(8,128)S(1)} %shard_map.84.duo.duo_y), channel_id=1, source_target_pairs={{0,24},{4,28},{8,16},{12,20},{16,8},{20,12},{24,0},{28,4},{32,56},... | collective-permute-start | bytes 811016 | tf_op jit(solution)/shard_map/ppermute | solution.py:409
  50.0 4.0 %shard_map.85 = (bf16[4,256,256]{2,1,0:T(8,128)(2,1)S(1)}, bf16[4,256,256]{2,1,0:T(8,128)(2,1)S(1)}) custom-call(bf16[4,256,256]{2,1,0:T(8,128)(2,1)S(1)} %get-tuple-element.56.refs_0_, bf16[4,256,256]{2,1,0:T(8,128)(2,1)S(1)} %get-tuple-element.57.refs_1_, bf16[4,256,256]{2,1,0:T(8,128)(2,1)S(1)} %get-tuple-element.58.refs_2_, ...), custom_call_target="tpu_custom_call" | custom-call | bytes 5308416 | tf_op jit(solution)/shard_map/pallas_call | solution.py:81
  54.0 2.1 %collective-permute-done.14.other_duo.other_y = f32[264,256]{1,0:T(8,128)S(1)} collective-permute-done((f32[264,256]{1,0:T(8,128)S(1)}, f32[264,256]{1,0:T(8,128)S(1)}, u32[]{:S(2)}, u32[]{:S(2)}) %collective-permute-start.14) | collective-permute-done | bytes 270368 | tf_op jit(solution)/shard_map/ppermute | solution.py:409
  56.1 0.5 shard_map.86
  56.6 5.1 %collective-permute-start.17 = (f32[264,256]{1,0:T(8,128)S(1)}, f32[264,256]{1,0:T(8,128)S(1)}, u32[]{:S(2)}, u32[]{:S(2)}) collective-permute-start(f32[264,256]{1,0:T(8,128)S(1)} %get-tuple-element.78), channel_id=1, source_target_pairs={{0,64},{8,72},{16,80},{24,88},{32,96},{40,104},{48,112},{56,120},{... | collective-permute-start | bytes 811016 | tf_op jit(solution)/shard_map/ppermute | solution.py:423
  61.7 2.6 %collective-permute-start.16 = (f32[264,256]{1,0:T(8,128)S(1)}, f32[264,256]{1,0:T(8,128)S(1)}, u32[]{:S(2)}, u32[]{:S(2)}) collective-permute-start(f32[264,256]{1,0:T(8,128)S(1)} %get-tuple-element.78), channel_id=1, source_target_pairs={{0,32},{8,40},{16,48},{24,56},{32,64},{40,72},{48,80},{56,88},{64,... | collective-permute-start | bytes 811016 | tf_op jit(solution)/shard_map/ppermute | solution.py:423
  64.3 1.3 %collective-permute-start.18 = (f32[8,256]{1,0:T(8,128)S(1)}, f32[8,256]{1,0:T(8,128)S(1)}, u32[]{:S(2)}, u32[]{:S(2)}) collective-permute-start(f32[8,256]{1,0:T(8,128)S(1)} %get-tuple-element.79), channel_id=1, source_target_pairs={{0,96},{8,104},{16,112},{24,120},{1,97},{9,105},{17,113},{25,121},... | collective-permute-start | bytes 24584 | tf_op jit(solution)/shard_map/ppermute | solution.py:423
  65.6 0.6 shard_map.87.z_chip
  66.2 0.7 collective-permute-done.18.tail
  67.0 1.6 %collective-permute-done.16.near = f32[264,256]{1,0:T(8,128)S(1)} collective-permute-done((f32[264,256]{1,0:T(8,128)S(1)}, f32[264,256]{1,0:T(8,128)S(1)}, u32[]{:S(2)}, u32[]{:S(2)}) %collective-permute-start.16) | collective-permute-done | bytes 270368 | tf_op jit(solution)/shard_map/ppermute | solution.py:423
  68.6 0.6 shard_map.88
  69.2 1.3 %collective-permute-start.20 = (f32[48,256]{1,0:T(8,128)S(1)}, f32[48,256]{1,0:T(8,128)S(1)}, u32[]{:S(2)}, u32[]{:S(2)}) collective-permute-start(f32[48,256]{1,0:T(8,128)S(1)} %get-tuple-element.88), channel_id=1, source_target_pairs={{0,12},{8,4},{16,28},{24,20},{32,44},{40,36},{48,60},{56,52},{64,7... | collective-permute-start | bytes 147464 | tf_op jit(solution)/shard_map/ppermute | solution.py:409
  70.5 0.1 collective-permute-start.19
  70.6 1.2 %collective-permute-done.19.sent_ref.sent = f32[24,256]{1,0:T(8,128)S(1)} collective-permute-done((f32[24,256]{1,0:T(8,128)S(1)}, f32[24,256]{1,0:T(8,128)S(1)}, u32[]{:S(2)}, u32[]{:S(2)}) %collective-permute-start.19) | collective-permute-done | bytes 24608 | tf_op jit(solution)/shard_map/ppermute | solution.py:402
  71.8 1.1 %shard_map.89 = (f32[16,64]{1,0:T(8,128)}, f32[16,64]{1,0:T(8,128)S(1)}, f32[8,256]{1,0:T(8,128)S(1)}) custom-call(f32[24,256]{1,0:T(8,128)S(1)} %get-tuple-element.81.means_ref, f32[24,256]{1,0:T(8,128)S(1)} %collective-permute-done.19.sent_ref.sent, f32[264,256]{1,0:T(8,128)S(1)} %collective-permute-done.15.refs_0_.z_other, ...), custom_call_target="tpu_custom_call" | custom-call | bytes 2514944 | tf_op jit(solution)/shard_map/pallas_call | solution.py:81
  72.9 0.2 shard_map.90.duo_v
  73.1 0.7 collective-permute-start.21
  73.7 0.3 shard_map.91
  74.0 0.7 collective-permute-start.24
  74.7 0.7 collective-permute-start.23
  75.4 0.7 collective-permute-start.22
  76.0 0.0 collective-permute-done.24.v3
  76.1 0.0 copy-start
  76.1 0.5 shard_map.92.sigma_ref
  76.6 10.3 %collective-permute-start.25 = (f32[8,256]{1,0:T(8,128)S(1)}, f32[8,256]{1,0:T(8,128)S(1)}, u32[]{:S(2)}, u32[]{:S(2)}) collective-permute-start(f32[8,256]{1,0:T(8,128)S(1)} %shard_map.92.sigma_ref), channel_id=1, source_target_pairs={{0,4},{4,0},{8,12},{12,8},{16,20},{20,16},{24,28},{28,24},{32,36},... | collective-permute-start | bytes 24584 | tf_op jit(solution)/shard_map/ppermute | solution.py:402
  86.9 0.8 collective-permute-done.25.sent_ref
  87.7 1.4 %shard_map.93 = f32[16,64]{1,0:T(8,128)} custom-call(f32[8,256]{1,0:T(8,128)S(1)} %shard_map.92.sigma_ref, f32[8,256]{1,0:T(8,128)S(1)} %collective-permute-done.25.sent_ref, f32[528,256]{1,0:T(8,128)S(1)} %collective-permute-done.12.other_ref, f32[8,256]{1,0:T(8,128)S(1)} %get-tuple-element.92.mid_ref, ...), custom_call_target="tpu_custom_call" | custom-call | bytes 1691648 | tf_op jit(solution)/shard_map/pallas_call | solution.py:81
  (15 shorter events, 0.0 us)
Async XLA Ops:
  3.2 10.2 %collective-permute-start.9 = (f32[392,128]{1,0:T(8,128)}, f32[392,128]{1,0:T(8,128)S(1)}, u32[]{:S(2)}, u32[]{:S(2)}) collective-permute-start(f32[392,128]{1,0:T(8,128)} %get-tuple-element.51.refs_0_), channel_id=1, source_target_pairs={{0,1},{1,2},{2,3},{3,0},{4,5},{5,6},{6,7},{7,4},{8,9},{9,10},{10,1... | collective-permute-start | bytes 602120 | tf_op jit(solution)/shard_map/ppermute | solution.py:394
  5.3 11.4 %collective-permute-start.4 = (f32[392,128]{1,0:T(8,128)}, f32[392,128]{1,0:T(8,128)S(1)}, u32[]{:S(2)}, u32[]{:S(2)}) collective-permute-start(f32[392,128]{1,0:T(8,128)} %get-tuple-element.49.refs_0_), channel_id=1, source_target_pairs={{0,3},{1,0},{2,1},{3,2},{4,7},{5,4},{6,5},{7,6},{8,11},{9,8},{10,9... | collective-permute-start | bytes 602120 | tf_op jit(solution)/shard_map/ppermute | solution.py:394
  7.5 10.2 %collective-permute-start.6 = (f32[392,128]{1,0:T(8,128)}, f32[392,128]{1,0:T(8,128)S(1)}, u32[]{:S(2)}, u32[]{:S(2)}) collective-permute-start(f32[392,128]{1,0:T(8,128)} %get-tuple-element.50.refs_0_), channel_id=1, source_target_pairs={{0,1},{1,2},{2,3},{3,0},{4,5},{5,6},{6,7},{7,4},{8,9},{9,10},{10,1... | collective-permute-start | bytes 602120 | tf_op jit(solution)/shard_map/ppermute | solution.py:394
  7.5 11.2 %collective-permute-start.11 = (f32[392,128]{1,0:T(8,128)}, f32[392,128]{1,0:T(8,128)S(1)}, u32[]{:S(2)}, u32[]{:S(2)}) collective-permute-start(f32[392,128]{1,0:T(8,128)} %get-tuple-element.51.refs_0_), channel_id=1, source_target_pairs={{0,3},{1,0},{2,1},{3,2},{4,7},{5,4},{6,5},{7,6},{8,11},{9,8},{10,9... | collective-permute-start | bytes 602120 | tf_op jit(solution)/shard_map/ppermute | solution.py:394
  13.4 8.9 %collective-permute-start.10 = (f32[392,128]{1,0:T(8,128)S(1)}, f32[392,128]{1,0:T(8,128)S(1)}, u32[]{:S(2)}, u32[]{:S(2)}) collective-permute-start(f32[392,128]{1,0:T(8,128)S(1)} %collective-permute-done.9.refs_1_), channel_id=1, source_target_pairs={{0,1},{1,2},{2,3},{3,0},{4,5},{5,6},{6,7},{7,4},{8,9},{9,10},{10,1... | collective-permute-start | bytes 602120 | tf_op jit(solution)/shard_map/ppermute | solution.py:394
  13.4 13.2 %copy-start.1 = (f32[392,128]{1,0:T(8,128)S(1)}, f32[392,128]{1,0:T(8,128)}, u32[]{:S(2)}) copy-start(f32[392,128]{1,0:T(8,128)} %get-tuple-element.48.refs_0_) | copy-start | bytes 602116
  13.4 16.9 %copy-start.3 = (f32[392,128]{1,0:T(8,128)S(1)}, f32[392,128]{1,0:T(8,128)}, u32[]{:S(2)}) copy-start(f32[392,128]{1,0:T(8,128)} %get-tuple-element.50.refs_0_) | copy-start | bytes 602116
  13.4 13.2 %collective-permute-start.1 = (f32[392,128]{1,0:T(8,128)}, f32[392,128]{1,0:T(8,128)S(1)}, u32[]{:S(2)}, u32[]{:S(2)}) collective-permute-start(f32[392,128]{1,0:T(8,128)} %get-tuple-element.48.refs_0_), channel_id=1, source_target_pairs={{0,3},{1,0},{2,1},{3,2},{4,7},{5,4},{6,5},{7,6},{8,11},{9,8},{10,9... | collective-permute-start | bytes 602120 | tf_op jit(solution)/shard_map/ppermute | solution.py:394
  16.7 10.4 %collective-permute-start.8 = (f32[392,128]{1,0:T(8,128)}, f32[392,128]{1,0:T(8,128)S(1)}, u32[]{:S(2)}, u32[]{:S(2)}) collective-permute-start(f32[392,128]{1,0:T(8,128)} %get-tuple-element.50.refs_0_), channel_id=1, source_target_pairs={{0,3},{1,0},{2,1},{3,2},{4,7},{5,4},{6,5},{7,6},{8,11},{9,8},{10,9... | collective-permute-start | bytes 602120 | tf_op jit(solution)/shard_map/ppermute | solution.py:394
  17.7 12.6 %collective-permute-start.7 = (f32[392,128]{1,0:T(8,128)S(1)}, f32[392,128]{1,0:T(8,128)S(1)}, u32[]{:S(2)}, u32[]{:S(2)}) collective-permute-start(f32[392,128]{1,0:T(8,128)S(1)} %collective-permute-done.6.refs_1_), channel_id=1, source_target_pairs={{0,1},{1,2},{2,3},{3,0},{4,5},{5,6},{6,7},{7,4},{8,9},{9,10},{10,1... | collective-permute-start | bytes 602120 | tf_op jit(solution)/shard_map/ppermute | solution.py:394
  18.7 13.3 %collective-permute-start.3 = (f32[392,128]{1,0:T(8,128)}, f32[392,128]{1,0:T(8,128)S(1)}, u32[]{:S(2)}, u32[]{:S(2)}) collective-permute-start(f32[392,128]{1,0:T(8,128)} %get-tuple-element.49.refs_0_), channel_id=1, source_target_pairs={{0,1},{1,2},{2,3},{3,0},{4,5},{5,6},{6,7},{7,4},{8,9},{9,10},{10,1... | collective-permute-start | bytes 602120 | tf_op jit(solution)/shard_map/ppermute | solution.py:394
  22.3 9.6 %collective-permute-start.5 = (f32[392,128]{1,0:T(8,128)S(1)}, f32[392,128]{1,0:T(8,128)S(1)}, u32[]{:S(2)}, u32[]{:S(2)}) collective-permute-start(f32[392,128]{1,0:T(8,128)S(1)} %collective-permute-done.4.refs_3_), channel_id=1, source_target_pairs={{0,3},{1,0},{2,1},{3,2},{4,7},{5,4},{6,5},{7,6},{8,11},{9,8},{10,9... | collective-permute-start | bytes 602120 | tf_op jit(solution)/shard_map/ppermute | solution.py:394
  24.1 0.9 %copy-start.4 = (f32[392,128]{1,0:T(8,128)S(1)}, f32[392,128]{1,0:T(8,128)}, u32[]{:S(2)}) copy-start(f32[392,128]{1,0:T(8,128)} %get-tuple-element.51.refs_0_) | copy-start | bytes 602116
  26.7 7.4 %collective-permute-start = (f32[392,128]{1,0:T(8,128)S(1)}, f32[392,128]{1,0:T(8,128)S(1)}, u32[]{:S(2)}, u32[]{:S(2)}) collective-permute-start(f32[392,128]{1,0:T(8,128)S(1)} %copy-done.1), channel_id=1, source_target_pairs={{0,1},{1,2},{2,3},{3,0},{4,5},{5,6},{6,7},{7,4},{8,9},{9,10},{10,1... | collective-permute-start | bytes 602120 | tf_op jit(solution)/shard_map/ppermute | solution.py:394
  27.0 7.1 %collective-permute-start.2 = (f32[392,128]{1,0:T(8,128)S(1)}, f32[392,128]{1,0:T(8,128)S(1)}, u32[]{:S(2)}, u32[]{:S(2)}) collective-permute-start(f32[392,128]{1,0:T(8,128)S(1)} %collective-permute-done.1.refs_3_), channel_id=1, source_target_pairs={{0,3},{1,0},{2,1},{3,2},{4,7},{5,4},{6,5},{7,6},{8,11},{9,8},{10,9... | collective-permute-start | bytes 602120 | tf_op jit(solution)/shard_map/ppermute | solution.py:394
  30.3 1.7 %copy-start.2 = (f32[392,128]{1,0:T(8,128)S(1)}, f32[392,128]{1,0:T(8,128)}, u32[]{:S(2)}) copy-start(f32[392,128]{1,0:T(8,128)} %get-tuple-element.49.refs_0_) | copy-start | bytes 602116
  35.7 2.0 %collective-permute-start.12 = (f32[528,256]{1,0:T(8,128)S(1)}, f32[528,256]{1,0:T(8,128)S(1)}, u32[]{:S(2)}, u32[]{:S(2)}) collective-permute-start(f32[528,256]{1,0:T(8,128)S(1)} %get-tuple-element.55.own_ref), channel_id=1, source_target_pairs={{0,4},{4,0},{8,12},{12,8},{16,20},{20,16},{24,28},{28,24},{32,36},... | collective-permute-start | bytes 1622024 | tf_op jit(solution)/shard_map/ppermute | solution.py:402
  38.0 8.8 %collective-permute-start.13 = (f32[264,256]{1,0:T(8,128)S(1)}, f32[264,256]{1,0:T(8,128)S(1)}, u32[]{:S(2)}, u32[]{:S(2)}) collective-permute-start(f32[264,256]{1,0:T(8,128)S(1)} %shard_map.82.own.own_y), channel_id=1, source_target_pairs={{0,8},{4,12},{8,0},{12,4},{16,24},{20,28},{24,16},{28,20},{32,40},... | collective-permute-start | bytes 811016 | tf_op jit(solution)/shard_map/ppermute | solution.py:409
  44.4 9.5 %collective-permute-start.15 = (f32[264,256]{1,0:T(8,128)S(1)}, f32[264,256]{1,0:T(8,128)S(1)}, u32[]{:S(2)}, u32[]{:S(2)}) collective-permute-start(f32[264,256]{1,0:T(8,128)S(1)} %get-tuple-element.76._.z_own), channel_id=1, source_target_pairs={{0,4},{4,0},{8,12},{12,8},{16,20},{20,16},{24,28},{28,24},{32,36},... | collective-permute-start | bytes 811016 | tf_op jit(solution)/shard_map/ppermute | solution.py:402
  47.1 9.0 %collective-permute-start.14 = (f32[264,256]{1,0:T(8,128)S(1)}, f32[264,256]{1,0:T(8,128)S(1)}, u32[]{:S(2)}, u32[]{:S(2)}) collective-permute-start(f32[264,256]{1,0:T(8,128)S(1)} %shard_map.84.duo.duo_y), channel_id=1, source_target_pairs={{0,24},{4,28},{8,16},{12,20},{16,8},{20,12},{24,0},{28,4},{32,56},... | collective-permute-start | bytes 811016 | tf_op jit(solution)/shard_map/ppermute | solution.py:409
  56.6 10.4 %collective-permute-start.17 = (f32[264,256]{1,0:T(8,128)S(1)}, f32[264,256]{1,0:T(8,128)S(1)}, u32[]{:S(2)}, u32[]{:S(2)}) collective-permute-start(f32[264,256]{1,0:T(8,128)S(1)} %get-tuple-element.78), channel_id=1, source_target_pairs={{0,64},{8,72},{16,80},{24,88},{32,96},{40,104},{48,112},{56,120},{... | collective-permute-start | bytes 811016 | tf_op jit(solution)/shard_map/ppermute | solution.py:423
  61.7 6.9 %collective-permute-start.16 = (f32[264,256]{1,0:T(8,128)S(1)}, f32[264,256]{1,0:T(8,128)S(1)}, u32[]{:S(2)}, u32[]{:S(2)}) collective-permute-start(f32[264,256]{1,0:T(8,128)S(1)} %get-tuple-element.78), channel_id=1, source_target_pairs={{0,32},{8,40},{16,48},{24,56},{32,64},{40,72},{48,80},{56,88},{64,... | collective-permute-start | bytes 811016 | tf_op jit(solution)/shard_map/ppermute | solution.py:423
  64.3 2.6 %collective-permute-start.18 = (f32[8,256]{1,0:T(8,128)S(1)}, f32[8,256]{1,0:T(8,128)S(1)}, u32[]{:S(2)}, u32[]{:S(2)}) collective-permute-start(f32[8,256]{1,0:T(8,128)S(1)} %get-tuple-element.79), channel_id=1, source_target_pairs={{0,96},{8,104},{16,112},{24,120},{1,97},{9,105},{17,113},{25,121},... | collective-permute-start | bytes 24584 | tf_op jit(solution)/shard_map/ppermute | solution.py:423
  69.2 3.7 %collective-permute-start.20 = (f32[48,256]{1,0:T(8,128)S(1)}, f32[48,256]{1,0:T(8,128)S(1)}, u32[]{:S(2)}, u32[]{:S(2)}) collective-permute-start(f32[48,256]{1,0:T(8,128)S(1)} %get-tuple-element.88), channel_id=1, source_target_pairs={{0,12},{8,4},{16,28},{24,20},{32,44},{40,36},{48,60},{56,52},{64,7... | collective-permute-start | bytes 147464 | tf_op jit(solution)/shard_map/ppermute | solution.py:409
  70.5 1.3 %collective-permute-start.19 = (f32[24,256]{1,0:T(8,128)S(1)}, f32[24,256]{1,0:T(8,128)S(1)}, u32[]{:S(2)}, u32[]{:S(2)}) collective-permute-start(f32[24,256]{1,0:T(8,128)S(1)} %get-tuple-element.81.means_ref), channel_id=1, source_target_pairs={{0,4},{4,0},{8,12},{12,8},{16,20},{20,16},{24,28},{28,24},{32,36},... | collective-permute-start | bytes 73736 | tf_op jit(solution)/shard_map/ppermute | solution.py:402
  73.1 0.7 collective-permute-start.21
  74.0 2.0 %collective-permute-start.24 = (f32[8,256]{1,0:T(8,128)S(1)}, f32[8,256]{1,0:T(8,128)S(1)}, u32[]{:S(2)}, u32[]{:S(2)}) collective-permute-start(f32[8,256]{1,0:T(8,128)S(1)} %get-tuple-element.90), channel_id=1, source_target_pairs={{100,4},{108,12},{116,20},{124,28},{101,5},{109,13},{117,21},{125,... | collective-permute-start | bytes 24584 | tf_op jit(solution)/shard_map/ppermute | solution.py:423
  74.7 1.4 %collective-permute-start.23 = (f32[8,256]{1,0:T(8,128)S(1)}, f32[8,256]{1,0:T(8,128)S(1)}, u32[]{:S(2)}, u32[]{:S(2)}) collective-permute-start(f32[8,256]{1,0:T(8,128)S(1)} %get-tuple-element.90), channel_id=1, source_target_pairs={{100,36},{108,44},{116,52},{124,60},{68,4},{76,12},{84,20},{92,28}... | collective-permute-start | bytes 24584 | tf_op jit(solution)/shard_map/ppermute | solution.py:423
  75.4 0.7 collective-permute-start.22
  76.1 11.7 %copy-start = (f32[16,64]{1,0:T(8,128)S(1)}, f32[16,64]{1,0:T(8,128)}, u32[]{:S(2)}) copy-start(f32[16,64]{1,0:T(8,128)} %get-tuple-element.46.refs_4_) | copy-start | bytes 12292
  76.6 11.1 %collective-permute-start.25 = (f32[8,256]{1,0:T(8,128)S(1)}, f32[8,256]{1,0:T(8,128)S(1)}, u32[]{:S(2)}, u32[]{:S(2)}) collective-permute-start(f32[8,256]{1,0:T(8,128)S(1)} %shard_map.92.sigma_ref), channel_id=1, source_target_pairs={{0,4},{4,0},{8,12},{12,8},{16,20},{20,16},{24,28},{28,24},{32,36},... | collective-permute-start | bytes 24584 | tf_op jit(solution)/shard_map/ppermute | solution.py:402

commit v4 on v3

--- a/solution.py
+++ b/solution.py
@@ -312,14 +312,16 @@
 
 
 def row_kernel(partner, duo, other_duo, *refs):
-    whole_ref, side_ref, tail_ref = refs[-3:]
+    whole_ref, side_ref, tail_ref, wide_ref = refs[-4:]
     x = x_of()
     lead = core_of() == 0
     low = x < 2
     mine, theirs, beside = duo[...], other_duo[...], partner[...]
     whole = then(jnp.where(low, mine, theirs), jnp.where(low, theirs, mine))
     whole_ref[...] = whole
-    tail_ref[...] = whole[STATE:]
+    wide_ref[:AUG] = whole
+    wide_ref[AUG:] = jnp.zeros((8, STATE), f32)
+    tail_ref[:8] = whole[STATE:]
     outer = then(jnp.where(lead, theirs, beside), jnp.where(lead, beside, theirs))
     nothing = jnp.concatenate([identity_matrix(), jnp.zeros((8, STATE), f32)], axis=0)
     depth = jnp.where(lead, x, 3 - x)
@@ -327,11 +329,11 @@
     side_ref[...] = jnp.where(depth == 3, outer, side)
 
 
-def enter_kernel(near, far, tail, side_ref, own_ref, z_chip, means_ref, v_ref):
+def enter_kernel(near, far, tail2, tail3, side_ref, own_ref, z_chip, means_ref, v_ref):
     y = y_of()
-    through = mul_nn(tail[...], far[:STATE]) + far[STATE:]
-    inner = jnp.where(y == 3, through, jnp.where(y == 2, far[STATE:], 0.0))
-    m = mul_nn(inner, near[:STATE]) + near[STATE:]
+    through = mul_nn(tail3[...], far[:STATE]) + far[STATE:]
+    inner = jnp.where(y == 3, through, tail2[...])
+    m = mul_nn(inner, near[:STATE]) + near[STATE:AUG]
     m = mul_nn(m, side_ref[:STATE]) + side_ref[STATE:]
     v = mul_nn(m, z_chip[:STATE]) + z_chip[STATE:]
     v_ref[:8] = v
@@ -478,21 +480,21 @@
     shi, slo = call(
         suffix_kernel, 0, [arr(STEPS // 4, STATE, STATE, dtype=bf16)] * 2, his + los + vecs
     )
-    whole, side, tail = call(
+    whole, side, tail, wide = call(
         row_kernel,
         0,
-        [arr(AUG, STATE)] * 2 + [arr(8, STATE)],
+        [arr(AUG, STATE)] * 2 + [arr(8, STATE), arr(AUG + 8, STATE)],
         [partner, duo, other_duo, z_other, shi],
     )
-    tail = over_y(tail, ((0, 3),))
-    near = over_y(whole, ((0, 1), (1, 2), (2, 3)), ((2, 1), (1, 0)))
-    far = over_y(whole, ((0, 2), (1, 3)), ((2, 0),))
+    tails = [over_y(tail, ((0, 2),)), over_y(tail, ((0, 3),))]
+    near = over_y(wide, ((0, 1), (1, 2), (2, 3)), ((2, 1), (1, 0)))
+    far = over_y(whole, ((1, 3),), ((2, 0),))
     (z_chip,) = call(pair_z_kernel, 0, [arr(AUG, STATE)], [own, other, z_own, z_other])
     means, v_chip = call(
         enter_kernel,
         0,
         [arr(24, STATE), arr(48, STATE)],
-        [near, far, tail, side, own, z_chip],
+        [near, far] + tails + [side, own, z_chip],
     )
     partner_v = over_x(v_chip, beside, ((0, 1),))
     sent = over_core(means)

time: 90.6 us -> 89.6 us (0.989)
  waiting for transfers between devices: 16.8 us -> 15.2 us
    ppermute x6 -> x7, waiting for transfers between devices: 2.32 us -> 0.7 us  [over_y(): return lax.ppermute(a, 'tm', route)]
    ppermute x6 -> x7, starting transfers between devices: 11 us -> 11.6 us  [over_y(): return lax.ppermute(a, 'tm', route)]
  transfers between devices with their start and end apart: 26 -> 27, of which waited for: 11 -> 10; matrix products, arithmetic and copies ran while one was open for 0% -> 0% of each run, Pallas kernels for 17% -> 18%
where the time goes in v4:
time: 89.6 us; the launch traced here: 88.1 us
  starting transfers between devices  47.6 us (53%)
  Pallas kernels  23.5 us (26%)
  waiting for transfers between devices  15.2 us (17%)
  local copies, waits for them, and re-layouts  0.95 us (1%)
  between operations  0.93 us (1%)
    pallas_call x17, Pallas kernels, call(): pl.pallas_call(kernel, out_shape=outs, in_specs=[pl.BlockSpec(memory_spac...  23.5 us
    ppermute x12, starting transfers between devices, over_z(): return lax.ppermute(a, 'state', [(i, (i + s) % 4) for i in range(4)])  18.9 us
    ppermute x7, starting transfers between devices, over_y(): return lax.ppermute(a, 'tm', route)  11.6 us
    ppermute x4, starting transfers between devices, over_core(): return lax.ppermute(a, 'tm', [(i, i ^ 1) for i in range(32)])  10.5 us
    ppermute x4, starting transfers between devices, over_x(): return lax.ppermute(a, 'tm', route)  6.55 us
    ppermute x12, waiting for transfers between devices, over_z(): return lax.ppermute(a, 'state', [(i, (i + s) % 4) for i in range(4)])  6.11 us
    ppermute x4, waiting for transfers between devices, over_x(): return lax.ppermute(a, 'tm', route)  4.46 us
    ppermute x4, waiting for transfers between devices, over_core(): return lax.ppermute(a, 'tm', [(i, i ^ 1) for i in range(32)])  3.93 us
  transfers between devices with their start and end apart: 27, of which 10 were waited for; matrix products, arithmetic and copies ran while one was open for 0% of the time, Pallas kernels for 18%

profile of v4, /device:TPU:0, one launch (start us, length us, event | category | flops | bytes accessed | tf_op | source)
XLA Modules:
  0.0 88.1 jit_solution(13167736314813164234)
XLA Ops:
  0.6 2.6 %shard_map.77 = (f32[392,128]{1,0:T(8,128)}, f32[392,128]{1,0:T(8,128)}, f32[392,128]{1,0:T(8,128)}, f32[392,128]{1,0:T(8,128)}) custom-call(f32[16,12288]{1,0:T(8,128)} %dyn_hbm.1, s32[2,16]{1,0:T(2,128)} %bitcast.3, f32[16,64]{1,0:T(8,128)} %obs_hbm.1, s32[16,64]{1,0:T(8,128)} %mask_hbm.1, f32[16,64]{1,0:T(8,128)} %fgain_hbm.1, f32[16,64]{1,0:T(8,128)} %sgain_hbm.1), custom_call_target="tpu_custom_call" | custom-call | bytes 1605760 | tf_op jit(solution)/shard_map/pallas_call | solution.py:81
  3.2 2.1 %collective-permute-start.9 = (f32[392,128]{1,0:T(8,128)}, f32[392,128]{1,0:T(8,128)S(1)}, u32[]{:S(2)}, u32[]{:S(2)}) collective-permute-start(f32[392,128]{1,0:T(8,128)} %get-tuple-element.52.refs_0_), channel_id=1, source_target_pairs={{0,1},{1,2},{2,3},{3,0},{4,5},{5,6},{6,7},{7,4},{8,9},{9,10},{10,1... | collective-permute-start | bytes 602120 | tf_op jit(solution)/shard_map/ppermute | solution.py:396
  5.3 2.2 %collective-permute-start.4 = (f32[392,128]{1,0:T(8,128)}, f32[392,128]{1,0:T(8,128)S(1)}, u32[]{:S(2)}, u32[]{:S(2)}) collective-permute-start(f32[392,128]{1,0:T(8,128)} %get-tuple-element.50.refs_0_), channel_id=1, source_target_pairs={{0,3},{1,0},{2,1},{3,2},{4,7},{5,4},{6,5},{7,6},{8,11},{9,8},{10,9... | collective-permute-start | bytes 602120 | tf_op jit(solution)/shard_map/ppermute | solution.py:396
  7.5 3.2 %collective-permute-start.11 = (f32[392,128]{1,0:T(8,128)}, f32[392,128]{1,0:T(8,128)S(1)}, u32[]{:S(2)}, u32[]{:S(2)}) collective-permute-start(f32[392,128]{1,0:T(8,128)} %get-tuple-element.52.refs_0_), channel_id=1, source_target_pairs={{0,3},{1,0},{2,1},{3,2},{4,7},{5,4},{6,5},{7,6},{8,11},{9,8},{10,9... | collective-permute-start | bytes 602120 | tf_op jit(solution)/shard_map/ppermute | solution.py:396
  10.7 2.7 %collective-permute-done.9.refs_1_ = f32[392,128]{1,0:T(8,128)S(1)} collective-permute-done((f32[392,128]{1,0:T(8,128)}, f32[392,128]{1,0:T(8,128)S(1)}, u32[]{:S(2)}, u32[]{:S(2)}) %collective-permute-start.9) | collective-permute-done | bytes 200736 | tf_op jit(solution)/shard_map/ppermute | solution.py:396
  13.4 0.0 collective-permute-start.10
  13.4 3.2 %collective-permute-start.1 = (f32[392,128]{1,0:T(8,128)}, f32[392,128]{1,0:T(8,128)S(1)}, u32[]{:S(2)}, u32[]{:S(2)}) collective-permute-start(f32[392,128]{1,0:T(8,128)} %get-tuple-element.49.refs_0_), channel_id=1, source_target_pairs={{0,3},{1,0},{2,1},{3,2},{4,7},{5,4},{6,5},{7,6},{8,11},{9,8},{10,9... | collective-permute-start | bytes 602120 | tf_op jit(solution)/shard_map/ppermute | solution.py:396
  16.7 0.0 collective-permute-done.4.refs_3_
  16.7 0.8 collective-permute-start.8
  17.5 0.2 collective-permute-done.6.refs_1_
  17.7 1.0 %collective-permute-start.7 = (f32[392,128]{1,0:T(8,128)S(1)}, f32[392,128]{1,0:T(8,128)S(1)}, u32[]{:S(2)}, u32[]{:S(2)}) collective-permute-start(f32[392,128]{1,0:T(8,128)S(1)} %collective-permute-done.6.refs_1_), channel_id=1, source_target_pairs={{0,1},{1,2},{2,3},{3,0},{4,5},{5,6},{6,7},{7,4},{8,9},{9,10},{10,1... | collective-permute-start | bytes 602120 | tf_op jit(solution)/shard_map/ppermute | solution.py:396
  18.7 0.0 collective-permute-done.11.refs_3_
  18.7 0.9 %collective-permute-start.3 = (f32[392,128]{1,0:T(8,128)}, f32[392,128]{1,0:T(8,128)S(1)}, u32[]{:S(2)}, u32[]{:S(2)}) collective-permute-start(f32[392,128]{1,0:T(8,128)} %get-tuple-element.50.refs_0_), channel_id=1, source_target_pairs={{0,1},{1,2},{2,3},{3,0},{4,5},{5,6},{6,7},{7,4},{8,9},{9,10},{10,1... | collective-permute-start | bytes 602120 | tf_op jit(solution)/shard_map/ppermute | solution.py:396
  19.6 2.7 %collective-permute-done.10.refs_2_ = f32[392,128]{1,0:T(8,128)S(1)} collective-permute-done((f32[392,128]{1,0:T(8,128)S(1)}, f32[392,128]{1,0:T(8,128)S(1)}, u32[]{:S(2)}, u32[]{:S(2)}) %collective-permute-start.10) | collective-permute-done | bytes 200736 | tf_op jit(solution)/shard_map/ppermute | solution.py:396
  22.3 1.7 %collective-permute-start.5 = (f32[392,128]{1,0:T(8,128)S(1)}, f32[392,128]{1,0:T(8,128)S(1)}, u32[]{:S(2)}, u32[]{:S(2)}) collective-permute-start(f32[392,128]{1,0:T(8,128)S(1)} %collective-permute-done.4.refs_3_), channel_id=1, source_target_pairs={{0,3},{1,0},{2,1},{3,2},{4,7},{5,4},{6,5},{7,6},{8,11},{9,8},{10,9... | collective-permute-start | bytes 602120 | tf_op jit(solution)/shard_map/ppermute | solution.py:396
  24.1 0.9 %copy-done.4 = f32[392,128]{1,0:T(8,128)S(1)} copy-done((f32[392,128]{1,0:T(8,128)S(1)}, f32[392,128]{1,0:T(8,128)}, u32[]{:S(2)}) %copy-start.4) | copy-done | bytes 200728
  25.0 1.6 %shard_map.78 = (bf16[4,256,256]{2,1,0:T(8,128)(2,1)S(1)}, bf16[4,256,256]{2,1,0:T(8,128)(2,1)S(1)}, bf16[4,256,256]{2,1,0:T(8,128)(2,1)S(1)}, bf16[4,256,256]{2...) custom-call(f32[392,128]{1,0:T(8,128)S(1)} %copy-done.4, ...), custom_call_target="tpu_custom_call" | custom-call | flops 1600000000 | bytes 3457024 | tf_op jit(solution)/shard_map/pallas_call | solution.py:81
  26.7 0.0 collective-permute-done.1.refs_3_
  26.7 0.4 collective-permute-start
  27.0 0.0 collective-permute-done.8.refs_3_
  27.0 3.3 %collective-permute-start.2 = (f32[392,128]{1,0:T(8,128)S(1)}, f32[392,128]{1,0:T(8,128)S(1)}, u32[]{:S(2)}, u32[]{:S(2)}) collective-permute-start(f32[392,128]{1,0:T(8,128)S(1)} %collective-permute-done.1.refs_3_), channel_id=1, source_target_pairs={{0,3},{1,0},{2,1},{3,2},{4,7},{5,4},{6,5},{7,6},{8,11},{9,8},{10,9... | collective-permute-start | bytes 602120 | tf_op jit(solution)/shard_map/ppermute | solution.py:396
  30.3 1.6 %shard_map.79 = (bf16[4,256,256]{2,1,0:T(8,128)(2,1)S(1)}, bf16[4,256,256]{2,1,0:T(8,128)(2,1)S(1)}, bf16[4,256,256]{2,1,0:T(8,128)(2,1)S(1)}, bf16[4,256,256]{2...) custom-call(f32[392,128]{1,0:T(8,128)S(1)} %copy-done.3, ...), custom_call_target="tpu_custom_call" | custom-call | flops 1600000000 | bytes 3997696 | tf_op jit(solution)/shard_map/pallas_call | solution.py:81
  32.0 0.0 collective-permute-done.5.refs_2_
  32.0 1.6 %shard_map.80 = (bf16[4,256,256]{2,1,0:T(8,128)(2,1)S(1)}, bf16[4,256,256]{2,1,0:T(8,128)(2,1)S(1)}, bf16[4,256,256]{2,1,0:T(8,128)(2,1)S(1)}, bf16[4,256,256]{2...) custom-call(f32[392,128]{1,0:T(8,128)S(1)} %copy-done.2, ...), custom_call_target="tpu_custom_call" | custom-call | flops 1600000000 | bytes 3997696 | tf_op jit(solution)/shard_map/pallas_call | solution.py:81
  33.7 0.5 collective-permute-done.refs_1_
  34.1 0.0 collective-permute-done.2.refs_2_
  34.1 1.6 %shard_map.81 = (bf16[4,256,256]{2,1,0:T(8,128)(2,1)S(1)}, bf16[4,256,256]{2,1,0:T(8,128)(2,1)S(1)}, bf16[4,256,256]{2,1,0:T(8,128)(2,1)S(1)}, bf16[4,256,256]{2...) custom-call(f32[392,128]{1,0:T(8,128)S(1)} %copy-done.1, ...), custom_call_target="tpu_custom_call" | custom-call | flops 1600000000 | bytes 3997696 | tf_op jit(solution)/shard_map/pallas_call | solution.py:81
  35.7 0.1 collective-permute-start.12
  35.8 1.9 %collective-permute-done.12.other_ref = f32[528,256]{1,0:T(8,128)S(1)} collective-permute-done((f32[528,256]{1,0:T(8,128)S(1)}, f32[528,256]{1,0:T(8,128)S(1)}, u32[]{:S(2)}, u32[]{:S(2)}) %collective-permute-start.12) | collective-permute-done | bytes 540704 | tf_op jit(solution)/shard_map/ppermute | solution.py:404
  37.8 0.3 shard_map.82.own.own_y
  38.0 1.7 %collective-permute-start.13 = (f32[264,256]{1,0:T(8,128)S(1)}, f32[264,256]{1,0:T(8,128)S(1)}, u32[]{:S(2)}, u32[]{:S(2)}) collective-permute-start(f32[264,256]{1,0:T(8,128)S(1)} %shard_map.82.own.own_y), channel_id=1, source_target_pairs={{0,8},{4,12},{8,0},{12,4},{16,24},{20,28},{24,16},{28,20},{32,40},... | collective-permute-start | bytes 811016 | tf_op jit(solution)/shard_map/ppermute | solution.py:411
  39.8 4.6 %shard_map.83 = (bf16[4,256,256]{2,1,0:T(8,128)(2,1)S(1)}, bf16[4,256,256]{2,1,0:T(8,128)(2,1)S(1)}, bf16[4,256,256]{2,1,0:T(8,128)(2,1)S(1)}, bf16[4,256,256]{2...) custom-call(bf16[4,256,256]{2,1,0:T(8,128)(2,1)S(1)} %get-tuple-element.57.refs_0_, ...), custom_call_target="tpu_custom_call" | custom-call | bytes 10838016 | tf_op jit(solution)/shard_map/pallas_call | solution.py:81
  44.4 0.1 collective-permute-start.15
  44.5 2.3 %collective-permute-done.13.partner.partner_y = f32[264,256]{1,0:T(8,128)S(1)} collective-permute-done((f32[264,256]{1,0:T(8,128)S(1)}, f32[264,256]{1,0:T(8,128)S(1)}, u32[]{:S(2)}, u32[]{:S(2)}) %collective-permute-start.13) | collective-permute-done | bytes 270368 | tf_op jit(solution)/shard_map/ppermute | solution.py:411
  46.8 0.3 shard_map.84.duo.duo_y
  47.1 2.8 %collective-permute-start.14 = (f32[264,256]{1,0:T(8,128)S(1)}, f32[264,256]{1,0:T(8,128)S(1)}, u32[]{:S(2)}, u32[]{:S(2)}) collective-permute-start(f32[264,256]{1,0:T(8,128)S(1)} %shard_map.84.duo.duo_y), channel_id=1, source_target_pairs={{0,24},{4,28},{8,16},{12,20},{16,8},{20,12},{24,0},{28,4},{32,56},... | collective-permute-start | bytes 811016 | tf_op jit(solution)/shard_map/ppermute | solution.py:411
  50.0 4.0 %shard_map.85 = (bf16[4,256,256]{2,1,0:T(8,128)(2,1)S(1)}, bf16[4,256,256]{2,1,0:T(8,128)(2,1)S(1)}) custom-call(bf16[4,256,256]{2,1,0:T(8,128)(2,1)S(1)} %get-tuple-element.57.refs_0_, bf16[4,256,256]{2,1,0:T(8,128)(2,1)S(1)} %get-tuple-element.58.refs_1_, bf16[4,256,256]{2,1,0:T(8,128)(2,1)S(1)} %get-tuple-element.59.refs_2_, ...), custom_call_target="tpu_custom_call" | custom-call | bytes 5308416 | tf_op jit(solution)/shard_map/pallas_call | solution.py:81
  54.0 0.0 collective-permute-done.15.refs_0_.z_other
  54.0 2.1 %collective-permute-done.14.other_duo.other_y = f32[264,256]{1,0:T(8,128)S(1)} collective-permute-done((f32[264,256]{1,0:T(8,128)S(1)}, f32[264,256]{1,0:T(8,128)S(1)}, u32[]{:S(2)}, u32[]{:S(2)}) %collective-permute-start.14) | collective-permute-done | bytes 270368 | tf_op jit(solution)/shard_map/ppermute | solution.py:411
  56.1 0.5 shard_map.86
  56.6 3.5 %collective-permute-start.16 = (f32[272,256]{1,0:T(8,128)S(1)}, f32[272,256]{1,0:T(8,128)S(1)}, u32[]{:S(2)}, u32[]{:S(2)}) collective-permute-start(f32[272,256]{1,0:T(8,128)S(1)} %get-tuple-element.79), channel_id=1, source_target_pairs={{0,32},{8,40},{16,48},{24,56},{32,64},{40,72},{48,80},{56,88},{64,... | collective-permute-start | bytes 835592 | tf_op jit(solution)/shard_map/ppermute | solution.py:425
  60.1 0.7 collective-permute-start.17
  60.8 3.3 %collective-permute-start.19 = (f32[8,256]{1,0:T(8,128)S(1)}, f32[8,256]{1,0:T(8,128)S(1)}, u32[]{:S(2)}, u32[]{:S(2)}) collective-permute-start(f32[8,256]{1,0:T(8,128)S(1)} %get-tuple-element.81), channel_id=1, source_target_pairs={{0,96},{8,104},{16,112},{24,120},{1,97},{9,105},{17,113},{25,121},... | collective-permute-start | bytes 24584 | tf_op jit(solution)/shard_map/ppermute | solution.py:425
  64.1 2.1 %collective-permute-start.18 = (f32[8,256]{1,0:T(8,128)S(1)}, f32[8,256]{1,0:T(8,128)S(1)}, u32[]{:S(2)}, u32[]{:S(2)}) collective-permute-start(f32[8,256]{1,0:T(8,128)S(1)} %get-tuple-element.81), channel_id=1, source_target_pairs={{0,64},{8,72},{16,80},{24,88},{1,65},{9,73},{17,81},{25,89},{2,66}... | collective-permute-start | bytes 24584 | tf_op jit(solution)/shard_map/ppermute | solution.py:425
  66.2 0.6 shard_map.87.z_chip
  66.9 0.0 collective-permute-done.19.tail3
  66.9 0.7 collective-permute-done.18.tail2
  67.6 0.0 collective-permute-done.17.far
  67.6 0.6 shard_map.88
  68.2 1.3 %collective-permute-start.21 = (f32[48,256]{1,0:T(8,128)S(1)}, f32[48,256]{1,0:T(8,128)S(1)}, u32[]{:S(2)}, u32[]{:S(2)}) collective-permute-start(f32[48,256]{1,0:T(8,128)S(1)} %get-tuple-element.90), channel_id=1, source_target_pairs={{0,12},{8,4},{16,28},{24,20},{32,44},{40,36},{48,60},{56,52},{64,7... | collective-permute-start | bytes 147464 | tf_op jit(solution)/shard_map/ppermute | solution.py:411
  69.5 0.1 collective-permute-start.20
  69.6 1.2 %collective-permute-done.20.sent_ref.sent = f32[24,256]{1,0:T(8,128)S(1)} collective-permute-done((f32[24,256]{1,0:T(8,128)S(1)}, f32[24,256]{1,0:T(8,128)S(1)}, u32[]{:S(2)}, u32[]{:S(2)}) %collective-permute-start.20) | collective-permute-done | bytes 24608 | tf_op jit(solution)/shard_map/ppermute | solution.py:404
  70.8 1.1 %shard_map.89 = (f32[16,64]{1,0:T(8,128)}, f32[16,64]{1,0:T(8,128)S(1)}, f32[8,256]{1,0:T(8,128)S(1)}) custom-call(f32[24,256]{1,0:T(8,128)S(1)} %get-tuple-element.83.means_ref, f32[24,256]{1,0:T(8,128)S(1)} %collective-permute-done.20.sent_ref.sent, f32[264,256]{1,0:T(8,128)S(1)} %collective-permute-done.15.refs_0_.z_other, ...), custom_call_target="tpu_custom_call" | custom-call | bytes 2514944 | tf_op jit(solution)/shard_map/pallas_call | solution.py:81
  71.9 0.2 shard_map.90.duo_v
  72.1 0.7 collective-permute-start.22
  72.8 0.3 shard_map.91
  73.0 0.7 collective-permute-start.25
  73.7 0.7 collective-permute-start.24
  74.4 0.7 collective-permute-start.23
  75.1 0.0 copy-start
  75.1 0.5 shard_map.92.sigma_ref
  75.6 10.3 %collective-permute-start.26 = (f32[8,256]{1,0:T(8,128)S(1)}, f32[8,256]{1,0:T(8,128)S(1)}, u32[]{:S(2)}, u32[]{:S(2)}) collective-permute-start(f32[8,256]{1,0:T(8,128)S(1)} %shard_map.92.sigma_ref), channel_id=1, source_target_pairs={{0,4},{4,0},{8,12},{12,8},{16,20},{20,16},{24,28},{28,24},{32,36},... | collective-permute-start | bytes 24584 | tf_op jit(solution)/shard_map/ppermute | solution.py:404
  85.9 0.8 collective-permute-done.26.sent_ref
  86.7 1.4 %shard_map.93 = f32[16,64]{1,0:T(8,128)} custom-call(f32[8,256]{1,0:T(8,128)S(1)} %shard_map.92.sigma_ref, f32[8,256]{1,0:T(8,128)S(1)} %collective-permute-done.26.sent_ref, f32[528,256]{1,0:T(8,128)S(1)} %collective-permute-done.12.other_ref, f32[8,256]{1,0:T(8,128)S(1)} %get-tuple-element.94.mid_ref, ...), custom_call_target="tpu_custom_call" | custom-call | bytes 1691648 | tf_op jit(solution)/shard_map/pallas_call | solution.py:81
  (17 shorter events, 0.0 us)
Async XLA Ops:
  3.2 10.2 %collective-permute-start.9 = (f32[392,128]{1,0:T(8,128)}, f32[392,128]{1,0:T(8,128)S(1)}, u32[]{:S(2)}, u32[]{:S(2)}) collective-permute-start(f32[392,128]{1,0:T(8,128)} %get-tuple-element.52.refs_0_), channel_id=1, source_target_pairs={{0,1},{1,2},{2,3},{3,0},{4,5},{5,6},{6,7},{7,4},{8,9},{9,10},{10,1... | collective-permute-start | bytes 602120 | tf_op jit(solution)/shard_map/ppermute | solution.py:396
  5.3 11.4 %collective-permute-start.4 = (f32[392,128]{1,0:T(8,128)}, f32[392,128]{1,0:T(8,128)S(1)}, u32[]{:S(2)}, u32[]{:S(2)}) collective-permute-start(f32[392,128]{1,0:T(8,128)} %get-tuple-element.50.refs_0_), channel_id=1, source_target_pairs={{0,3},{1,0},{2,1},{3,2},{4,7},{5,4},{6,5},{7,6},{8,11},{9,8},{10,9... | collective-permute-start | bytes 602120 | tf_op jit(solution)/shard_map/ppermute | solution.py:396
  7.5 10.2 %collective-permute-start.6 = (f32[392,128]{1,0:T(8,128)}, f32[392,128]{1,0:T(8,128)S(1)}, u32[]{:S(2)}, u32[]{:S(2)}) collective-permute-start(f32[392,128]{1,0:T(8,128)} %get-tuple-element.51.refs_0_), channel_id=1, source_target_pairs={{0,1},{1,2},{2,3},{3,0},{4,5},{5,6},{6,7},{7,4},{8,9},{9,10},{10,1... | collective-permute-start | bytes 602120 | tf_op jit(solution)/shard_map/ppermute | solution.py:396
  7.5 11.2 %collective-permute-start.11 = (f32[392,128]{1,0:T(8,128)}, f32[392,128]{1,0:T(8,128)S(1)}, u32[]{:S(2)}, u32[]{:S(2)}) collective-permute-start(f32[392,128]{1,0:T(8,128)} %get-tuple-element.52.refs_0_), channel_id=1, source_target_pairs={{0,3},{1,0},{2,1},{3,2},{4,7},{5,4},{6,5},{7,6},{8,11},{9,8},{10,9... | collective-permute-start | bytes 602120 | tf_op jit(solution)/shard_map/ppermute | solution.py:396
  13.4 8.9 %collective-permute-start.10 = (f32[392,128]{1,0:T(8,128)S(1)}, f32[392,128]{1,0:T(8,128)S(1)}, u32[]{:S(2)}, u32[]{:S(2)}) collective-permute-start(f32[392,128]{1,0:T(8,128)S(1)} %collective-permute-done.9.refs_1_), channel_id=1, source_target_pairs={{0,1},{1,2},{2,3},{3,0},{4,5},{5,6},{6,7},{7,4},{8,9},{9,10},{10,1... | collective-permute-start | bytes 602120 | tf_op jit(solution)/shard_map/ppermute | solution.py:396
  13.4 13.2 %copy-start.1 = (f32[392,128]{1,0:T(8,128)S(1)}, f32[392,128]{1,0:T(8,128)}, u32[]{:S(2)}) copy-start(f32[392,128]{1,0:T(8,128)} %get-tuple-element.49.refs_0_) | copy-start | bytes 602116
  13.4 16.9 %copy-start.3 = (f32[392,128]{1,0:T(8,128)S(1)}, f32[392,128]{1,0:T(8,128)}, u32[]{:S(2)}) copy-start(f32[392,128]{1,0:T(8,128)} %get-tuple-element.51.refs_0_) | copy-start | bytes 602116
  13.4 13.2 %collective-permute-start.1 = (f32[392,128]{1,0:T(8,128)}, f32[392,128]{1,0:T(8,128)S(1)}, u32[]{:S(2)}, u32[]{:S(2)}) collective-permute-start(f32[392,128]{1,0:T(8,128)} %get-tuple-element.49.refs_0_), channel_id=1, source_target_pairs={{0,3},{1,0},{2,1},{3,2},{4,7},{5,4},{6,5},{7,6},{8,11},{9,8},{10,9... | collective-permute-start | bytes 602120 | tf_op jit(solution)/shard_map/ppermute | solution.py:396
  16.7 10.4 %collective-permute-start.8 = (f32[392,128]{1,0:T(8,128)}, f32[392,128]{1,0:T(8,128)S(1)}, u32[]{:S(2)}, u32[]{:S(2)}) collective-permute-start(f32[392,128]{1,0:T(8,128)} %get-tuple-element.51.refs_0_), channel_id=1, source_target_pairs={{0,3},{1,0},{2,1},{3,2},{4,7},{5,4},{6,5},{7,6},{8,11},{9,8},{10,9... | collective-permute-start | bytes 602120 | tf_op jit(solution)/shard_map/ppermute | solution.py:396
  17.7 12.6 %collective-permute-start.7 = (f32[392,128]{1,0:T(8,128)S(1)}, f32[392,128]{1,0:T(8,128)S(1)}, u32[]{:S(2)}, u32[]{:S(2)}) collective-permute-start(f32[392,128]{1,0:T(8,128)S(1)} %collective-permute-done.6.refs_1_), channel_id=1, source_target_pairs={{0,1},{1,2},{2,3},{3,0},{4,5},{5,6},{6,7},{7,4},{8,9},{9,10},{10,1... | collective-permute-start | bytes 602120 | tf_op jit(solution)/shard_map/ppermute | solution.py:396
  18.7 13.3 %collective-permute-start.3 = (f32[392,128]{1,0:T(8,128)}, f32[392,128]{1,0:T(8,128)S(1)}, u32[]{:S(2)}, u32[]{:S(2)}) collective-permute-start(f32[392,128]{1,0:T(8,128)} %get-tuple-element.50.refs_0_), channel_id=1, source_target_pairs={{0,1},{1,2},{2,3},{3,0},{4,5},{5,6},{6,7},{7,4},{8,9},{9,10},{10,1... | collective-permute-start | bytes 602120 | tf_op jit(solution)/shard_map/ppermute | solution.py:396
  22.3 9.6 %collective-permute-start.5 = (f32[392,128]{1,0:T(8,128)S(1)}, f32[392,128]{1,0:T(8,128)S(1)}, u32[]{:S(2)}, u32[]{:S(2)}) collective-permute-start(f32[392,128]{1,0:T(8,128)S(1)} %collective-permute-done.4.refs_3_), channel_id=1, source_target_pairs={{0,3},{1,0},{2,1},{3,2},{4,7},{5,4},{6,5},{7,6},{8,11},{9,8},{10,9... | collective-permute-start | bytes 602120 | tf_op jit(solution)/shard_map/ppermute | solution.py:396
  24.1 0.9 %copy-start.4 = (f32[392,128]{1,0:T(8,128)S(1)}, f32[392,128]{1,0:T(8,128)}, u32[]{:S(2)}) copy-start(f32[392,128]{1,0:T(8,128)} %get-tuple-element.52.refs_0_) | copy-start | bytes 602116
  26.7 7.4 %collective-permute-start = (f32[392,128]{1,0:T(8,128)S(1)}, f32[392,128]{1,0:T(8,128)S(1)}, u32[]{:S(2)}, u32[]{:S(2)}) collective-permute-start(f32[392,128]{1,0:T(8,128)S(1)} %copy-done.1), channel_id=1, source_target_pairs={{0,1},{1,2},{2,3},{3,0},{4,5},{5,6},{6,7},{7,4},{8,9},{9,10},{10,1... | collective-permute-start | bytes 602120 | tf_op jit(solution)/shard_map/ppermute | solution.py:396
  27.0 7.1 %collective-permute-start.2 = (f32[392,128]{1,0:T(8,128)S(1)}, f32[392,128]{1,0:T(8,128)S(1)}, u32[]{:S(2)}, u32[]{:S(2)}) collective-permute-start(f32[392,128]{1,0:T(8,128)S(1)} %collective-permute-done.1.refs_3_), channel_id=1, source_target_pairs={{0,3},{1,0},{2,1},{3,2},{4,7},{5,4},{6,5},{7,6},{8,11},{9,8},{10,9... | collective-permute-start | bytes 602120 | tf_op jit(solution)/shard_map/ppermute | solution.py:396
  30.3 1.7 %copy-start.2 = (f32[392,128]{1,0:T(8,128)S(1)}, f32[392,128]{1,0:T(8,128)}, u32[]{:S(2)}) copy-start(f32[392,128]{1,0:T(8,128)} %get-tuple-element.50.refs_0_) | copy-start | bytes 602116
  35.7 2.0 %collective-permute-start.12 = (f32[528,256]{1,0:T(8,128)S(1)}, f32[528,256]{1,0:T(8,128)S(1)}, u32[]{:S(2)}, u32[]{:S(2)}) collective-permute-start(f32[528,256]{1,0:T(8,128)S(1)} %get-tuple-element.56.own_ref), channel_id=1, source_target_pairs={{0,4},{4,0},{8,12},{12,8},{16,20},{20,16},{24,28},{28,24},{32,36},... | collective-permute-start | bytes 1622024 | tf_op jit(solution)/shard_map/ppermute | solution.py:404
  38.0 8.8 %collective-permute-start.13 = (f32[264,256]{1,0:T(8,128)S(1)}, f32[264,256]{1,0:T(8,128)S(1)}, u32[]{:S(2)}, u32[]{:S(2)}) collective-permute-start(f32[264,256]{1,0:T(8,128)S(1)} %shard_map.82.own.own_y), channel_id=1, source_target_pairs={{0,8},{4,12},{8,0},{12,4},{16,24},{20,28},{24,16},{28,20},{32,40},... | collective-permute-start | bytes 811016 | tf_op jit(solution)/shard_map/ppermute | solution.py:411
  44.4 9.5 %collective-permute-start.15 = (f32[264,256]{1,0:T(8,128)S(1)}, f32[264,256]{1,0:T(8,128)S(1)}, u32[]{:S(2)}, u32[]{:S(2)}) collective-permute-start(f32[264,256]{1,0:T(8,128)S(1)} %get-tuple-element.77._.z_own), channel_id=1, source_target_pairs={{0,4},{4,0},{8,12},{12,8},{16,20},{20,16},{24,28},{28,24},{32,36},... | collective-permute-start | bytes 811016 | tf_op jit(solution)/shard_map/ppermute | solution.py:404
  47.1 9.0 %collective-permute-start.14 = (f32[264,256]{1,0:T(8,128)S(1)}, f32[264,256]{1,0:T(8,128)S(1)}, u32[]{:S(2)}, u32[]{:S(2)}) collective-permute-start(f32[264,256]{1,0:T(8,128)S(1)} %shard_map.84.duo.duo_y), channel_id=1, source_target_pairs={{0,24},{4,28},{8,16},{12,20},{16,8},{20,12},{24,0},{28,4},{32,56},... | collective-permute-start | bytes 811016 | tf_op jit(solution)/shard_map/ppermute | solution.py:411
  56.6 11.0 %collective-permute-start.16 = (f32[272,256]{1,0:T(8,128)S(1)}, f32[272,256]{1,0:T(8,128)S(1)}, u32[]{:S(2)}, u32[]{:S(2)}) collective-permute-start(f32[272,256]{1,0:T(8,128)S(1)} %get-tuple-element.79), channel_id=1, source_target_pairs={{0,32},{8,40},{16,48},{24,56},{32,64},{40,72},{48,80},{56,88},{64,... | collective-permute-start | bytes 835592 | tf_op jit(solution)/shard_map/ppermute | solution.py:425
  60.1 7.5 %collective-permute-start.17 = (f32[264,256]{1,0:T(8,128)S(1)}, f32[264,256]{1,0:T(8,128)S(1)}, u32[]{:S(2)}, u32[]{:S(2)}) collective-permute-start(f32[264,256]{1,0:T(8,128)S(1)} %get-tuple-element.80), channel_id=1, source_target_pairs={{32,96},{40,104},{48,112},{56,120},{68,4},{76,12},{84,20},{92,28},... | collective-permute-start | bytes 811016 | tf_op jit(solution)/shard_map/ppermute | solution.py:425
  60.8 6.1 %collective-permute-start.19 = (f32[8,256]{1,0:T(8,128)S(1)}, f32[8,256]{1,0:T(8,128)S(1)}, u32[]{:S(2)}, u32[]{:S(2)}) collective-permute-start(f32[8,256]{1,0:T(8,128)S(1)} %get-tuple-element.81), channel_id=1, source_target_pairs={{0,96},{8,104},{16,112},{24,120},{1,97},{9,105},{17,113},{25,121},... | collective-permute-start | bytes 24584 | tf_op jit(solution)/shard_map/ppermute | solution.py:425
  64.1 3.5 %collective-permute-start.18 = (f32[8,256]{1,0:T(8,128)S(1)}, f32[8,256]{1,0:T(8,128)S(1)}, u32[]{:S(2)}, u32[]{:S(2)}) collective-permute-start(f32[8,256]{1,0:T(8,128)S(1)} %get-tuple-element.81), channel_id=1, source_target_pairs={{0,64},{8,72},{16,80},{24,88},{1,65},{9,73},{17,81},{25,89},{2,66}... | collective-permute-start | bytes 24584 | tf_op jit(solution)/shard_map/ppermute | solution.py:425
  68.2 3.7 %collective-permute-start.21 = (f32[48,256]{1,0:T(8,128)S(1)}, f32[48,256]{1,0:T(8,128)S(1)}, u32[]{:S(2)}, u32[]{:S(2)}) collective-permute-start(f32[48,256]{1,0:T(8,128)S(1)} %get-tuple-element.90), channel_id=1, source_target_pairs={{0,12},{8,4},{16,28},{24,20},{32,44},{40,36},{48,60},{56,52},{64,7... | collective-permute-start | bytes 147464 | tf_op jit(solution)/shard_map/ppermute | solution.py:411
  69.5 1.3 %collective-permute-start.20 = (f32[24,256]{1,0:T(8,128)S(1)}, f32[24,256]{1,0:T(8,128)S(1)}, u32[]{:S(2)}, u32[]{:S(2)}) collective-permute-start(f32[24,256]{1,0:T(8,128)S(1)} %get-tuple-element.83.means_ref), channel_id=1, source_target_pairs={{0,4},{4,0},{8,12},{12,8},{16,20},{20,16},{24,28},{28,24},{32,36},... | collective-permute-start | bytes 73736 | tf_op jit(solution)/shard_map/ppermute | solution.py:404
  72.1 0.7 collective-permute-start.22
  73.0 2.0 %collective-permute-start.25 = (f32[8,256]{1,0:T(8,128)S(1)}, f32[8,256]{1,0:T(8,128)S(1)}, u32[]{:S(2)}, u32[]{:S(2)}) collective-permute-start(f32[8,256]{1,0:T(8,128)S(1)} %get-tuple-element.92), channel_id=1, source_target_pairs={{100,4},{108,12},{116,20},{124,28},{101,5},{109,13},{117,21},{125,... | collective-permute-start | bytes 24584 | tf_op jit(solution)/shard_map/ppermute | solution.py:425
  73.7 1.4 %collective-permute-start.24 = (f32[8,256]{1,0:T(8,128)S(1)}, f32[8,256]{1,0:T(8,128)S(1)}, u32[]{:S(2)}, u32[]{:S(2)}) collective-permute-start(f32[8,256]{1,0:T(8,128)S(1)} %get-tuple-element.92), channel_id=1, source_target_pairs={{100,36},{108,44},{116,52},{124,60},{68,4},{76,12},{84,20},{92,28}... | collective-permute-start | bytes 24584 | tf_op jit(solution)/shard_map/ppermute | solution.py:425
  74.4 0.7 collective-permute-start.23
  75.1 11.7 %copy-start = (f32[16,64]{1,0:T(8,128)S(1)}, f32[16,64]{1,0:T(8,128)}, u32[]{:S(2)}) copy-start(f32[16,64]{1,0:T(8,128)} %get-tuple-element.47.refs_4_) | copy-start | bytes 12292
  75.6 11.1 %collective-permute-start.26 = (f32[8,256]{1,0:T(8,128)S(1)}, f32[8,256]{1,0:T(8,128)S(1)}, u32[]{:S(2)}, u32[]{:S(2)}) collective-permute-start(f32[8,256]{1,0:T(8,128)S(1)} %shard_map.92.sigma_ref), channel_id=1, source_target_pairs={{0,4},{4,0},{8,12},{12,8},{16,20},{20,16},{24,28},{28,24},{32,36},... | collective-permute-start | bytes 24584 | tf_op jit(solution)/shard_map/ppermute | solution.py:404

commit v5 on v4

--- a/solution.py
+++ b/solution.py
@@ -329,7 +329,7 @@
     side_ref[...] = jnp.where(depth == 3, outer, side)
 
 
-def enter_kernel(near, far, tail2, tail3, side_ref, own_ref, z_chip, means_ref, v_ref):
+def enter_kernel(near, far, tail2, tail3, side_ref, z_chip, means_ref, v_ref):
     y = y_of()
     through = mul_nn(tail3[...], far[:STATE]) + far[STATE:]
     inner = jnp.where(y == 3, through, tail2[...])
@@ -339,17 +339,20 @@
     v_ref[:8] = v
     v_ref[8:] = jnp.zeros((40, STATE), f32)
     means_ref[:8] = v
-    means_ref[8:16] = m
-    means_ref[16:] = mul_nn(m, own_ref[:STATE]) + own_ref[STATE:AUG]
+    means_ref[8:] = m
 
 
 def local_kernel(
-    means_ref, sent_ref, z_other, zhi_ref, zlo_ref, thi_ref, tlo_ref, v_ref, *refs
+    means_ref, sent_ref, x_own, x_other, z_other, zhi_ref, zlo_ref, thi_ref, tlo_ref, v_ref, *refs
 ):
     vecs = refs[:CHUNKS]
     m_ref, h_ref, mid_ref = refs[CHUNKS:]
-    mid_ref[...] = mul_nn(means_ref[16:], z_other[:STATE]) + z_other[STATE:]
-    enter = jnp.where(core_of() == 0, means_ref[8:16], sent_ref[16:])
+    lead = core_of() == 0
+    m = jnp.where(lead, means_ref[8:], sent_ref[8:])
+    x = jnp.where(lead, x_own[:AUG], x_other[:AUG])
+    mid = mul_nn(m, x[:STATE]) + x[STATE:]
+    mid_ref[...] = mul_nn(mid, z_other[:STATE]) + z_other[STATE:]
+    enter = jnp.where(lead, m, mid)
     w, o, p = (
         own_columns(jnp.concatenate([v[k] for v in vecs], axis=0)) for k in (0, 1, 3)
     )
@@ -493,8 +496,8 @@
     means, v_chip = call(
         enter_kernel,
         0,
-        [arr(24, STATE), arr(48, STATE)],
-        [near, far] + tails + [side, own, z_chip],
+        [arr(16, STATE), arr(48, STATE)],
+        [near, far] + tails + [side, z_chip],
     )
     partner_v = over_x(v_chip, beside, ((0, 1),))
     sent = over_core(means)
@@ -502,7 +505,7 @@
         local_kernel,
         0,
         [arr(STEPS, BLOCK)] * 2 + [arr(8, STATE)],
-        [means, sent, z_other, zhi, zlo, thi, tlo, v_all] + vecs,
+        [means, sent, own, other, z_other, zhi, zlo, thi, tlo, v_all] + vecs,
     )
     (duo_v,) = call(
         duo_v_kernel, 0, [arr(8, STATE)], [sent, partner_v, side_own, partner, h_all]

time: 89.6 us -> 89.9 us (level)
  no operation moved by 1% of the time
where the time goes in v5:
time: 89.9 us; the launch traced here: 88.3 us
  starting transfers between devices  47.6 us (53%)
  Pallas kernels  23.7 us (26%)
  waiting for transfers between devices  15.2 us (17%)
  local copies, waits for them, and re-layouts  0.95 us (1%)
  between operations  0.93 us (1%)
    pallas_call x17, Pallas kernels, call(): pl.pallas_call(kernel, out_shape=outs, in_specs=[pl.BlockSpec(memory_spac...  23.7 us
    ppermute x12, starting transfers between devices, over_z(): return lax.ppermute(a, 'state', [(i, (i + s) % 4) for i in range(4)])  18.9 us
    ppermute x7, starting transfers between devices, over_y(): return lax.ppermute(a, 'tm', route)  11.6 us
    ppermute x4, starting transfers between devices, over_core(): return lax.ppermute(a, 'tm', [(i, i ^ 1) for i in range(32)])  10.5 us
    ppermute x4, starting transfers between devices, over_x(): return lax.ppermute(a, 'tm', route)  6.55 us
    ppermute x12, waiting for transfers between devices, over_z(): return lax.ppermute(a, 'state', [(i, (i + s) % 4) for i in range(4)])  6.11 us
    ppermute x4, waiting for transfers between devices, over_x(): return lax.ppermute(a, 'tm', route)  4.46 us
    ppermute x4, waiting for transfers between devices, over_core(): return lax.ppermute(a, 'tm', [(i, i ^ 1) for i in range(32)])  3.92 us
  transfers between devices with their start and end apart: 27, of which 10 were waited for; matrix products, arithmetic and copies ran while one was open for 0% of the time, Pallas kernels for 18%

profile of v5, /device:TPU:0, one launch (start us, length us, event | category | flops | bytes accessed | tf_op | source)
XLA Modules:
  0.0 88.3 jit_solution(14238138734071548433)
XLA Ops:
  0.6 2.6 %shard_map.77 = (f32[392,128]{1,0:T(8,128)}, f32[392,128]{1,0:T(8,128)}, f32[392,128]{1,0:T(8,128)}, f32[392,128]{1,0:T(8,128)}) custom-call(f32[16,12288]{1,0:T(8,128)} %dyn_hbm.1, s32[2,16]{1,0:T(2,128)} %bitcast.3, f32[16,64]{1,0:T(8,128)} %obs_hbm.1, s32[16,64]{1,0:T(8,128)} %mask_hbm.1, f32[16,64]{1,0:T(8,128)} %fgain_hbm.1, f32[16,64]{1,0:T(8,128)} %sgain_hbm.1), custom_call_target="tpu_custom_call" | custom-call | bytes 1605760 | tf_op jit(solution)/shard_map/pallas_call | solution.py:81
  3.2 2.1 %collective-permute-start.9 = (f32[392,128]{1,0:T(8,128)}, f32[392,128]{1,0:T(8,128)S(1)}, u32[]{:S(2)}, u32[]{:S(2)}) collective-permute-start(f32[392,128]{1,0:T(8,128)} %get-tuple-element.52.refs_0_), channel_id=1, source_target_pairs={{0,1},{1,2},{2,3},{3,0},{4,5},{5,6},{6,7},{7,4},{8,9},{9,10},{10,1... | collective-permute-start | bytes 602120 | tf_op jit(solution)/shard_map/ppermute | solution.py:399
  5.3 2.2 %collective-permute-start.4 = (f32[392,128]{1,0:T(8,128)}, f32[392,128]{1,0:T(8,128)S(1)}, u32[]{:S(2)}, u32[]{:S(2)}) collective-permute-start(f32[392,128]{1,0:T(8,128)} %get-tuple-element.50.refs_0_), channel_id=1, source_target_pairs={{0,3},{1,0},{2,1},{3,2},{4,7},{5,4},{6,5},{7,6},{8,11},{9,8},{10,9... | collective-permute-start | bytes 602120 | tf_op jit(solution)/shard_map/ppermute | solution.py:399
  7.5 3.2 %collective-permute-start.11 = (f32[392,128]{1,0:T(8,128)}, f32[392,128]{1,0:T(8,128)S(1)}, u32[]{:S(2)}, u32[]{:S(2)}) collective-permute-start(f32[392,128]{1,0:T(8,128)} %get-tuple-element.52.refs_0_), channel_id=1, source_target_pairs={{0,3},{1,0},{2,1},{3,2},{4,7},{5,4},{6,5},{7,6},{8,11},{9,8},{10,9... | collective-permute-start | bytes 602120 | tf_op jit(solution)/shard_map/ppermute | solution.py:399
  10.7 2.7 %collective-permute-done.9.refs_1_ = f32[392,128]{1,0:T(8,128)S(1)} collective-permute-done((f32[392,128]{1,0:T(8,128)}, f32[392,128]{1,0:T(8,128)S(1)}, u32[]{:S(2)}, u32[]{:S(2)}) %collective-permute-start.9) | collective-permute-done | bytes 200736 | tf_op jit(solution)/shard_map/ppermute | solution.py:399
  13.4 0.0 collective-permute-start.10
  13.4 3.2 %collective-permute-start.1 = (f32[392,128]{1,0:T(8,128)}, f32[392,128]{1,0:T(8,128)S(1)}, u32[]{:S(2)}, u32[]{:S(2)}) collective-permute-start(f32[392,128]{1,0:T(8,128)} %get-tuple-element.49.refs_0_), channel_id=1, source_target_pairs={{0,3},{1,0},{2,1},{3,2},{4,7},{5,4},{6,5},{7,6},{8,11},{9,8},{10,9... | collective-permute-start | bytes 602120 | tf_op jit(solution)/shard_map/ppermute | solution.py:399
  16.7 0.0 collective-permute-done.4.refs_3_
  16.7 0.8 collective-permute-start.8
  17.5 0.2 collective-permute-done.6.refs_1_
  17.7 1.0 %collective-permute-start.7 = (f32[392,128]{1,0:T(8,128)S(1)}, f32[392,128]{1,0:T(8,128)S(1)}, u32[]{:S(2)}, u32[]{:S(2)}) collective-permute-start(f32[392,128]{1,0:T(8,128)S(1)} %collective-permute-done.6.refs_1_), channel_id=1, source_target_pairs={{0,1},{1,2},{2,3},{3,0},{4,5},{5,6},{6,7},{7,4},{8,9},{9,10},{10,1... | collective-permute-start | bytes 602120 | tf_op jit(solution)/shard_map/ppermute | solution.py:399
  18.7 0.9 %collective-permute-start.3 = (f32[392,128]{1,0:T(8,128)}, f32[392,128]{1,0:T(8,128)S(1)}, u32[]{:S(2)}, u32[]{:S(2)}) collective-permute-start(f32[392,128]{1,0:T(8,128)} %get-tuple-element.50.refs_0_), channel_id=1, source_target_pairs={{0,1},{1,2},{2,3},{3,0},{4,5},{5,6},{6,7},{7,4},{8,9},{9,10},{10,1... | collective-permute-start | bytes 602120 | tf_op jit(solution)/shard_map/ppermute | solution.py:399
  19.6 2.7 %collective-permute-done.10.refs_2_ = f32[392,128]{1,0:T(8,128)S(1)} collective-permute-done((f32[392,128]{1,0:T(8,128)S(1)}, f32[392,128]{1,0:T(8,128)S(1)}, u32[]{:S(2)}, u32[]{:S(2)}) %collective-permute-start.10) | collective-permute-done | bytes 200736 | tf_op jit(solution)/shard_map/ppermute | solution.py:399
  22.3 1.7 %collective-permute-start.5 = (f32[392,128]{1,0:T(8,128)S(1)}, f32[392,128]{1,0:T(8,128)S(1)}, u32[]{:S(2)}, u32[]{:S(2)}) collective-permute-start(f32[392,128]{1,0:T(8,128)S(1)} %collective-permute-done.4.refs_3_), channel_id=1, source_target_pairs={{0,3},{1,0},{2,1},{3,2},{4,7},{5,4},{6,5},{7,6},{8,11},{9,8},{10,9... | collective-permute-start | bytes 602120 | tf_op jit(solution)/shard_map/ppermute | solution.py:399
  24.1 0.9 %copy-done.4 = f32[392,128]{1,0:T(8,128)S(1)} copy-done((f32[392,128]{1,0:T(8,128)S(1)}, f32[392,128]{1,0:T(8,128)}, u32[]{:S(2)}) %copy-start.4) | copy-done | bytes 200728
  25.0 1.6 %shard_map.78 = (bf16[4,256,256]{2,1,0:T(8,128)(2,1)S(1)}, bf16[4,256,256]{2,1,0:T(8,128)(2,1)S(1)}, bf16[4,256,256]{2,1,0:T(8,128)(2,1)S(1)}, bf16[4,256,256]{2...) custom-call(f32[392,128]{1,0:T(8,128)S(1)} %copy-done.4, ...), custom_call_target="tpu_custom_call" | custom-call | flops 1600000000 | bytes 3457024 | tf_op jit(solution)/shard_map/pallas_call | solution.py:81
  26.7 0.0 collective-permute-done.1.refs_3_
  26.7 0.4 collective-permute-start
  27.0 0.0 collective-permute-done.8.refs_3_
  27.0 3.3 %collective-permute-start.2 = (f32[392,128]{1,0:T(8,128)S(1)}, f32[392,128]{1,0:T(8,128)S(1)}, u32[]{:S(2)}, u32[]{:S(2)}) collective-permute-start(f32[392,128]{1,0:T(8,128)S(1)} %collective-permute-done.1.refs_3_), channel_id=1, source_target_pairs={{0,3},{1,0},{2,1},{3,2},{4,7},{5,4},{6,5},{7,6},{8,11},{9,8},{10,9... | collective-permute-start | bytes 602120 | tf_op jit(solution)/shard_map/ppermute | solution.py:399
  30.3 1.6 %shard_map.79 = (bf16[4,256,256]{2,1,0:T(8,128)(2,1)S(1)}, bf16[4,256,256]{2,1,0:T(8,128)(2,1)S(1)}, bf16[4,256,256]{2,1,0:T(8,128)(2,1)S(1)}, bf16[4,256,256]{2...) custom-call(f32[392,128]{1,0:T(8,128)S(1)} %copy-done.3, ...), custom_call_target="tpu_custom_call" | custom-call | flops 1600000000 | bytes 3997696 | tf_op jit(solution)/shard_map/pallas_call | solution.py:81
  32.0 0.0 collective-permute-done.3.refs_1_
  32.0 1.6 %shard_map.80 = (bf16[4,256,256]{2,1,0:T(8,128)(2,1)S(1)}, bf16[4,256,256]{2,1,0:T(8,128)(2,1)S(1)}, bf16[4,256,256]{2,1,0:T(8,128)(2,1)S(1)}, bf16[4,256,256]{2...) custom-call(f32[392,128]{1,0:T(8,128)S(1)} %copy-done.2, ...), custom_call_target="tpu_custom_call" | custom-call | flops 1600000000 | bytes 3997696 | tf_op jit(solution)/shard_map/pallas_call | solution.py:81
  33.6 0.5 collective-permute-done.refs_1_
  34.1 0.0 collective-permute-done.2.refs_2_
  34.1 1.6 %shard_map.81 = (bf16[4,256,256]{2,1,0:T(8,128)(2,1)S(1)}, bf16[4,256,256]{2,1,0:T(8,128)(2,1)S(1)}, bf16[4,256,256]{2,1,0:T(8,128)(2,1)S(1)}, bf16[4,256,256]{2...) custom-call(f32[392,128]{1,0:T(8,128)S(1)} %copy-done.1, ...), custom_call_target="tpu_custom_call" | custom-call | flops 1600000000 | bytes 3997696 | tf_op jit(solution)/shard_map/pallas_call | solution.py:81
  35.7 0.1 collective-permute-start.12
  35.8 1.9 %collective-permute-done.12.other_ref.x_other = f32[528,256]{1,0:T(8,128)S(1)} collective-permute-done((f32[528,256]{1,0:T(8,128)S(1)}, f32[528,256]{1,0:T(8,128)S(1)}, u32[]{:S(2)}, u32[]{:S(2)}) %collective-permute-start.12) | collective-permute-done | bytes 540704 | tf_op jit(solution)/shard_map/ppermute | solution.py:407
  37.8 0.3 shard_map.82.own.own_y
  38.0 1.7 %collective-permute-start.13 = (f32[264,256]{1,0:T(8,128)S(1)}, f32[264,256]{1,0:T(8,128)S(1)}, u32[]{:S(2)}, u32[]{:S(2)}) collective-permute-start(f32[264,256]{1,0:T(8,128)S(1)} %shard_map.82.own.own_y), channel_id=1, source_target_pairs={{0,8},{4,12},{8,0},{12,4},{16,24},{20,28},{24,16},{28,20},{32,40},... | collective-permute-start | bytes 811016 | tf_op jit(solution)/shard_map/ppermute | solution.py:414
  39.8 4.6 %shard_map.83 = (bf16[4,256,256]{2,1,0:T(8,128)(2,1)S(1)}, bf16[4,256,256]{2,1,0:T(8,128)(2,1)S(1)}, bf16[4,256,256]{2,1,0:T(8,128)(2,1)S(1)}, bf16[4,256,256]{2...) custom-call(bf16[4,256,256]{2,1,0:T(8,128)(2,1)S(1)} %get-tuple-element.57.refs_0_, ...), custom_call_target="tpu_custom_call" | custom-call | bytes 10838016 | tf_op jit(solution)/shard_map/pallas_call | solution.py:81
  44.4 0.1 collective-permute-start.15
  44.5 2.3 %collective-permute-done.13.partner.partner_y = f32[264,256]{1,0:T(8,128)S(1)} collective-permute-done((f32[264,256]{1,0:T(8,128)S(1)}, f32[264,256]{1,0:T(8,128)S(1)}, u32[]{:S(2)}, u32[]{:S(2)}) %collective-permute-start.13) | collective-permute-done | bytes 270368 | tf_op jit(solution)/shard_map/ppermute | solution.py:414
  46.8 0.3 shard_map.84.duo.duo_y
  47.1 2.8 %collective-permute-start.14 = (f32[264,256]{1,0:T(8,128)S(1)}, f32[264,256]{1,0:T(8,128)S(1)}, u32[]{:S(2)}, u32[]{:S(2)}) collective-permute-start(f32[264,256]{1,0:T(8,128)S(1)} %shard_map.84.duo.duo_y), channel_id=1, source_target_pairs={{0,24},{4,28},{8,16},{12,20},{16,8},{20,12},{24,0},{28,4},{32,56},... | collective-permute-start | bytes 811016 | tf_op jit(solution)/shard_map/ppermute | solution.py:414
  50.0 4.0 %shard_map.85 = (bf16[4,256,256]{2,1,0:T(8,128)(2,1)S(1)}, bf16[4,256,256]{2,1,0:T(8,128)(2,1)S(1)}) custom-call(bf16[4,256,256]{2,1,0:T(8,128)(2,1)S(1)} %get-tuple-element.57.refs_0_, bf16[4,256,256]{2,1,0:T(8,128)(2,1)S(1)} %get-tuple-element.58.refs_1_, bf16[4,256,256]{2,1,0:T(8,128)(2,1)S(1)} %get-tuple-element.59.refs_2_, ...), custom_call_target="tpu_custom_call" | custom-call | bytes 5308416 | tf_op jit(solution)/shard_map/pallas_call | solution.py:81
  54.0 0.0 collective-permute-done.15.refs_0_.z_other
  54.0 2.1 %collective-permute-done.14.other_duo.other_y = f32[264,256]{1,0:T(8,128)S(1)} collective-permute-done((f32[264,256]{1,0:T(8,128)S(1)}, f32[264,256]{1,0:T(8,128)S(1)}, u32[]{:S(2)}, u32[]{:S(2)}) %collective-permute-start.14) | collective-permute-done | bytes 270368 | tf_op jit(solution)/shard_map/ppermute | solution.py:414
  56.1 0.5 shard_map.86
  56.6 3.5 %collective-permute-start.16 = (f32[272,256]{1,0:T(8,128)S(1)}, f32[272,256]{1,0:T(8,128)S(1)}, u32[]{:S(2)}, u32[]{:S(2)}) collective-permute-start(f32[272,256]{1,0:T(8,128)S(1)} %get-tuple-element.79), channel_id=1, source_target_pairs={{0,32},{8,40},{16,48},{24,56},{32,64},{40,72},{48,80},{56,88},{64,... | collective-permute-start | bytes 835592 | tf_op jit(solution)/shard_map/ppermute | solution.py:428
  60.1 0.7 collective-permute-start.17
  60.8 3.3 %collective-permute-start.19 = (f32[8,256]{1,0:T(8,128)S(1)}, f32[8,256]{1,0:T(8,128)S(1)}, u32[]{:S(2)}, u32[]{:S(2)}) collective-permute-start(f32[8,256]{1,0:T(8,128)S(1)} %get-tuple-element.81), channel_id=1, source_target_pairs={{0,96},{8,104},{16,112},{24,120},{1,97},{9,105},{17,113},{25,121},... | collective-permute-start | bytes 24584 | tf_op jit(solution)/shard_map/ppermute | solution.py:428
  64.1 2.1 %collective-permute-start.18 = (f32[8,256]{1,0:T(8,128)S(1)}, f32[8,256]{1,0:T(8,128)S(1)}, u32[]{:S(2)}, u32[]{:S(2)}) collective-permute-start(f32[8,256]{1,0:T(8,128)S(1)} %get-tuple-element.81), channel_id=1, source_target_pairs={{0,64},{8,72},{16,80},{24,88},{1,65},{9,73},{17,81},{25,89},{2,66}... | collective-permute-start | bytes 24584 | tf_op jit(solution)/shard_map/ppermute | solution.py:428
  66.2 0.6 shard_map.87.z_chip
  66.9 0.0 collective-permute-done.19.tail3
  66.9 0.7 collective-permute-done.18.tail2
  67.6 0.0 collective-permute-done.17.far
  67.6 0.0 collective-permute-done.16.near
  67.6 0.6 shard_map.88
  68.2 1.3 %collective-permute-start.21 = (f32[48,256]{1,0:T(8,128)S(1)}, f32[48,256]{1,0:T(8,128)S(1)}, u32[]{:S(2)}, u32[]{:S(2)}) collective-permute-start(f32[48,256]{1,0:T(8,128)S(1)} %get-tuple-element.90), channel_id=1, source_target_pairs={{0,12},{8,4},{16,28},{24,20},{32,44},{40,36},{48,60},{56,52},{64,7... | collective-permute-start | bytes 147464 | tf_op jit(solution)/shard_map/ppermute | solution.py:414
  69.5 0.1 collective-permute-start.20
  69.6 1.2 %collective-permute-done.20.sent_ref.sent = f32[16,256]{1,0:T(8,128)S(1)} collective-permute-done((f32[16,256]{1,0:T(8,128)S(1)}, f32[16,256]{1,0:T(8,128)S(1)}, u32[]{:S(2)}, u32[]{:S(2)}) %collective-permute-start.20) | collective-permute-done | bytes 16416 | tf_op jit(solution)/shard_map/ppermute | solution.py:407
  70.8 1.3 %shard_map.89 = (f32[16,64]{1,0:T(8,128)}, f32[16,64]{1,0:T(8,128)S(1)}, f32[8,256]{1,0:T(8,128)S(1)}) custom-call(f32[16,256]{1,0:T(8,128)S(1)} %get-tuple-element.83.means_ref, f32[16,256]{1,0:T(8,128)S(1)} %collective-permute-done.20.sent_ref.sent, f32[528,256]{1,0:T(8,128)S(1)} %get-tuple-element.56.own_ref.x_own, ...), custom_call_target="tpu_custom_call" | custom-call | bytes 3579904 | tf_op jit(solution)/shard_map/pallas_call | solution.py:81
  72.1 0.2 shard_map.90.duo_v
  72.3 0.7 collective-permute-start.22
  73.0 0.3 shard_map.91
  73.3 0.7 collective-permute-start.25
  73.9 0.7 collective-permute-start.24
  74.6 0.7 collective-permute-start.23
  75.3 0.0 copy-start
  75.3 0.5 shard_map.92.sigma_ref
  75.9 10.3 %collective-permute-start.26 = (f32[8,256]{1,0:T(8,128)S(1)}, f32[8,256]{1,0:T(8,128)S(1)}, u32[]{:S(2)}, u32[]{:S(2)}) collective-permute-start(f32[8,256]{1,0:T(8,128)S(1)} %shard_map.92.sigma_ref), channel_id=1, source_target_pairs={{0,4},{4,0},{8,12},{12,8},{16,20},{20,16},{24,28},{28,24},{32,36},... | collective-permute-start | bytes 24584 | tf_op jit(solution)/shard_map/ppermute | solution.py:407
  86.1 0.8 collective-permute-done.26.sent_ref
  87.0 1.4 %shard_map.93 = f32[16,64]{1,0:T(8,128)} custom-call(f32[8,256]{1,0:T(8,128)S(1)} %shard_map.92.sigma_ref, f32[8,256]{1,0:T(8,128)S(1)} %collective-permute-done.26.sent_ref, f32[528,256]{1,0:T(8,128)S(1)} %collective-permute-done.12.other_ref.x_other, f32[8,256]{1,0:T(8,128)S(1)} %get-tuple-element.94.mid_ref, ...), custom_call_target="tpu_custom_call" | custom-call | bytes 1691648 | tf_op jit(solution)/shard_map/pallas_call | solution.py:81
  (17 shorter events, 0.0 us)
Async XLA Ops:
  3.2 10.2 %collective-permute-start.9 = (f32[392,128]{1,0:T(8,128)}, f32[392,128]{1,0:T(8,128)S(1)}, u32[]{:S(2)}, u32[]{:S(2)}) collective-permute-start(f32[392,128]{1,0:T(8,128)} %get-tuple-element.52.refs_0_), channel_id=1, source_target_pairs={{0,1},{1,2},{2,3},{3,0},{4,5},{5,6},{6,7},{7,4},{8,9},{9,10},{10,1... | collective-permute-start | bytes 602120 | tf_op jit(solution)/shard_map/ppermute | solution.py:399
  5.3 11.4 %collective-permute-start.4 = (f32[392,128]{1,0:T(8,128)}, f32[392,128]{1,0:T(8,128)S(1)}, u32[]{:S(2)}, u32[]{:S(2)}) collective-permute-start(f32[392,128]{1,0:T(8,128)} %get-tuple-element.50.refs_0_), channel_id=1, source_target_pairs={{0,3},{1,0},{2,1},{3,2},{4,7},{5,4},{6,5},{7,6},{8,11},{9,8},{10,9... | collective-permute-start | bytes 602120 | tf_op jit(solution)/shard_map/ppermute | solution.py:399
  7.5 10.2 %collective-permute-start.6 = (f32[392,128]{1,0:T(8,128)}, f32[392,128]{1,0:T(8,128)S(1)}, u32[]{:S(2)}, u32[]{:S(2)}) collective-permute-start(f32[392,128]{1,0:T(8,128)} %get-tuple-element.51.refs_0_), channel_id=1, source_target_pairs={{0,1},{1,2},{2,3},{3,0},{4,5},{5,6},{6,7},{7,4},{8,9},{9,10},{10,1... | collective-permute-start | bytes 602120 | tf_op jit(solution)/shard_map/ppermute | solution.py:399
  7.5 11.2 %collective-permute-start.11 = (f32[392,128]{1,0:T(8,128)}, f32[392,128]{1,0:T(8,128)S(1)}, u32[]{:S(2)}, u32[]{:S(2)}) collective-permute-start(f32[392,128]{1,0:T(8,128)} %get-tuple-element.52.refs_0_), channel_id=1, source_target_pairs={{0,3},{1,0},{2,1},{3,2},{4,7},{5,4},{6,5},{7,6},{8,11},{9,8},{10,9... | collective-permute-start | bytes 602120 | tf_op jit(solution)/shard_map/ppermute | solution.py:399
  13.4 8.9 %collective-permute-start.10 = (f32[392,128]{1,0:T(8,128)S(1)}, f32[392,128]{1,0:T(8,128)S(1)}, u32[]{:S(2)}, u32[]{:S(2)}) collective-permute-start(f32[392,128]{1,0:T(8,128)S(1)} %collective-permute-done.9.refs_1_), channel_id=1, source_target_pairs={{0,1},{1,2},{2,3},{3,0},{4,5},{5,6},{6,7},{7,4},{8,9},{9,10},{10,1... | collective-permute-start | bytes 602120 | tf_op jit(solution)/shard_map/ppermute | solution.py:399
  13.4 13.2 %copy-start.1 = (f32[392,128]{1,0:T(8,128)S(1)}, f32[392,128]{1,0:T(8,128)}, u32[]{:S(2)}) copy-start(f32[392,128]{1,0:T(8,128)} %get-tuple-element.49.refs_0_) | copy-start | bytes 602116
  13.4 16.9 %copy-start.3 = (f32[392,128]{1,0:T(8,128)S(1)}, f32[392,128]{1,0:T(8,128)}, u32[]{:S(2)}) copy-start(f32[392,128]{1,0:T(8,128)} %get-tuple-element.51.refs_0_) | copy-start | bytes 602116
  13.4 13.2 %collective-permute-start.1 = (f32[392,128]{1,0:T(8,128)}, f32[392,128]{1,0:T(8,128)S(1)}, u32[]{:S(2)}, u32[]{:S(2)}) collective-permute-start(f32[392,128]{1,0:T(8,128)} %get-tuple-element.49.refs_0_), channel_id=1, source_target_pairs={{0,3},{1,0},{2,1},{3,2},{4,7},{5,4},{6,5},{7,6},{8,11},{9,8},{10,9... | collective-permute-start | bytes 602120 | tf_op jit(solution)/shard_map/ppermute | solution.py:399
  16.7 10.4 %collective-permute-start.8 = (f32[392,128]{1,0:T(8,128)}, f32[392,128]{1,0:T(8,128)S(1)}, u32[]{:S(2)}, u32[]{:S(2)}) collective-permute-start(f32[392,128]{1,0:T(8,128)} %get-tuple-element.51.refs_0_), channel_id=1, source_target_pairs={{0,3},{1,0},{2,1},{3,2},{4,7},{5,4},{6,5},{7,6},{8,11},{9,8},{10,9... | collective-permute-start | bytes 602120 | tf_op jit(solution)/shard_map/ppermute | solution.py:399
  17.7 12.6 %collective-permute-start.7 = (f32[392,128]{1,0:T(8,128)S(1)}, f32[392,128]{1,0:T(8,128)S(1)}, u32[]{:S(2)}, u32[]{:S(2)}) collective-permute-start(f32[392,128]{1,0:T(8,128)S(1)} %collective-permute-done.6.refs_1_), channel_id=1, source_target_pairs={{0,1},{1,2},{2,3},{3,0},{4,5},{5,6},{6,7},{7,4},{8,9},{9,10},{10,1... | collective-permute-start | bytes 602120 | tf_op jit(solution)/shard_map/ppermute | solution.py:399
  18.7 13.3 %collective-permute-start.3 = (f32[392,128]{1,0:T(8,128)}, f32[392,128]{1,0:T(8,128)S(1)}, u32[]{:S(2)}, u32[]{:S(2)}) collective-permute-start(f32[392,128]{1,0:T(8,128)} %get-tuple-element.50.refs_0_), channel_id=1, source_target_pairs={{0,1},{1,2},{2,3},{3,0},{4,5},{5,6},{6,7},{7,4},{8,9},{9,10},{10,1... | collective-permute-start | bytes 602120 | tf_op jit(solution)/shard_map/ppermute | solution.py:399
  22.3 9.6 %collective-permute-start.5 = (f32[392,128]{1,0:T(8,128)S(1)}, f32[392,128]{1,0:T(8,128)S(1)}, u32[]{:S(2)}, u32[]{:S(2)}) collective-permute-start(f32[392,128]{1,0:T(8,128)S(1)} %collective-permute-done.4.refs_3_), channel_id=1, source_target_pairs={{0,3},{1,0},{2,1},{3,2},{4,7},{5,4},{6,5},{7,6},{8,11},{9,8},{10,9... | collective-permute-start | bytes 602120 | tf_op jit(solution)/shard_map/ppermute | solution.py:399
  24.1 0.9 %copy-start.4 = (f32[392,128]{1,0:T(8,128)S(1)}, f32[392,128]{1,0:T(8,128)}, u32[]{:S(2)}) copy-start(f32[392,128]{1,0:T(8,128)} %get-tuple-element.52.refs_0_) | copy-start | bytes 602116
  26.7 7.4 %collective-permute-start = (f32[392,128]{1,0:T(8,128)S(1)}, f32[392,128]{1,0:T(8,128)S(1)}, u32[]{:S(2)}, u32[]{:S(2)}) collective-permute-start(f32[392,128]{1,0:T(8,128)S(1)} %copy-done.1), channel_id=1, source_target_pairs={{0,1},{1,2},{2,3},{3,0},{4,5},{5,6},{6,7},{7,4},{8,9},{9,10},{10,1... | collective-permute-start | bytes 602120 | tf_op jit(solution)/shard_map/ppermute | solution.py:399
  27.0 7.1 %collective-permute-start.2 = (f32[392,128]{1,0:T(8,128)S(1)}, f32[392,128]{1,0:T(8,128)S(1)}, u32[]{:S(2)}, u32[]{:S(2)}) collective-permute-start(f32[392,128]{1,0:T(8,128)S(1)} %collective-permute-done.1.refs_3_), channel_id=1, source_target_pairs={{0,3},{1,0},{2,1},{3,2},{4,7},{5,4},{6,5},{7,6},{8,11},{9,8},{10,9... | collective-permute-start | bytes 602120 | tf_op jit(solution)/shard_map/ppermute | solution.py:399
  30.3 1.7 %copy-start.2 = (f32[392,128]{1,0:T(8,128)S(1)}, f32[392,128]{1,0:T(8,128)}, u32[]{:S(2)}) copy-start(f32[392,128]{1,0:T(8,128)} %get-tuple-element.50.refs_0_) | copy-start | bytes 602116
  35.7 2.0 %collective-permute-start.12 = (f32[528,256]{1,0:T(8,128)S(1)}, f32[528,256]{1,0:T(8,128)S(1)}, u32[]{:S(2)}, u32[]{:S(2)}) collective-permute-start(f32[528,256]{1,0:T(8,128)S(1)} %get-tuple-element.56.own_ref.x_own), channel_id=1, source_target_pairs={{0,4},{4,0},{8,12},{12,8},{16,20},{20,16},{24,28},{28,24},{32,36},... | collective-permute-start | bytes 1622024 | tf_op jit(solution)/shard_map/ppermute | solution.py:407
  38.0 8.8 %collective-permute-start.13 = (f32[264,256]{1,0:T(8,128)S(1)}, f32[264,256]{1,0:T(8,128)S(1)}, u32[]{:S(2)}, u32[]{:S(2)}) collective-permute-start(f32[264,256]{1,0:T(8,128)S(1)} %shard_map.82.own.own_y), channel_id=1, source_target_pairs={{0,8},{4,12},{8,0},{12,4},{16,24},{20,28},{24,16},{28,20},{32,40},... | collective-permute-start | bytes 811016 | tf_op jit(solution)/shard_map/ppermute | solution.py:414
  44.4 9.5 %collective-permute-start.15 = (f32[264,256]{1,0:T(8,128)S(1)}, f32[264,256]{1,0:T(8,128)S(1)}, u32[]{:S(2)}, u32[]{:S(2)}) collective-permute-start(f32[264,256]{1,0:T(8,128)S(1)} %get-tuple-element.77._.z_own), channel_id=1, source_target_pairs={{0,4},{4,0},{8,12},{12,8},{16,20},{20,16},{24,28},{28,24},{32,36},... | collective-permute-start | bytes 811016 | tf_op jit(solution)/shard_map/ppermute | solution.py:407
  47.1 9.0 %collective-permute-start.14 = (f32[264,256]{1,0:T(8,128)S(1)}, f32[264,256]{1,0:T(8,128)S(1)}, u32[]{:S(2)}, u32[]{:S(2)}) collective-permute-start(f32[264,256]{1,0:T(8,128)S(1)} %shard_map.84.duo.duo_y), channel_id=1, source_target_pairs={{0,24},{4,28},{8,16},{12,20},{16,8},{20,12},{24,0},{28,4},{32,56},... | collective-permute-start | bytes 811016 | tf_op jit(solution)/shard_map/ppermute | solution.py:414
  56.6 11.0 %collective-permute-start.16 = (f32[272,256]{1,0:T(8,128)S(1)}, f32[272,256]{1,0:T(8,128)S(1)}, u32[]{:S(2)}, u32[]{:S(2)}) collective-permute-start(f32[272,256]{1,0:T(8,128)S(1)} %get-tuple-element.79), channel_id=1, source_target_pairs={{0,32},{8,40},{16,48},{24,56},{32,64},{40,72},{48,80},{56,88},{64,... | collective-permute-start | bytes 835592 | tf_op jit(solution)/shard_map/ppermute | solution.py:428
  60.1 7.5 %collective-permute-start.17 = (f32[264,256]{1,0:T(8,128)S(1)}, f32[264,256]{1,0:T(8,128)S(1)}, u32[]{:S(2)}, u32[]{:S(2)}) collective-permute-start(f32[264,256]{1,0:T(8,128)S(1)} %get-tuple-element.80), channel_id=1, source_target_pairs={{32,96},{40,104},{48,112},{56,120},{68,4},{76,12},{84,20},{92,28},... | collective-permute-start | bytes 811016 | tf_op jit(solution)/shard_map/ppermute | solution.py:428
  60.8 6.1 %collective-permute-start.19 = (f32[8,256]{1,0:T(8,128)S(1)}, f32[8,256]{1,0:T(8,128)S(1)}, u32[]{:S(2)}, u32[]{:S(2)}) collective-permute-start(f32[8,256]{1,0:T(8,128)S(1)} %get-tuple-element.81), channel_id=1, source_target_pairs={{0,96},{8,104},{16,112},{24,120},{1,97},{9,105},{17,113},{25,121},... | collective-permute-start | bytes 24584 | tf_op jit(solution)/shard_map/ppermute | solution.py:428
  64.1 3.5 %collective-permute-start.18 = (f32[8,256]{1,0:T(8,128)S(1)}, f32[8,256]{1,0:T(8,128)S(1)}, u32[]{:S(2)}, u32[]{:S(2)}) collective-permute-start(f32[8,256]{1,0:T(8,128)S(1)} %get-tuple-element.81), channel_id=1, source_target_pairs={{0,64},{8,72},{16,80},{24,88},{1,65},{9,73},{17,81},{25,89},{2,66}... | collective-permute-start | bytes 24584 | tf_op jit(solution)/shard_map/ppermute | solution.py:428
  68.2 3.9 %collective-permute-start.21 = (f32[48,256]{1,0:T(8,128)S(1)}, f32[48,256]{1,0:T(8,128)S(1)}, u32[]{:S(2)}, u32[]{:S(2)}) collective-permute-start(f32[48,256]{1,0:T(8,128)S(1)} %get-tuple-element.90), channel_id=1, source_target_pairs={{0,12},{8,4},{16,28},{24,20},{32,44},{40,36},{48,60},{56,52},{64,7... | collective-permute-start | bytes 147464 | tf_op jit(solution)/shard_map/ppermute | solution.py:414
  69.5 1.3 %collective-permute-start.20 = (f32[16,256]{1,0:T(8,128)S(1)}, f32[16,256]{1,0:T(8,128)S(1)}, u32[]{:S(2)}, u32[]{:S(2)}) collective-permute-start(f32[16,256]{1,0:T(8,128)S(1)} %get-tuple-element.83.means_ref), channel_id=1, source_target_pairs={{0,4},{4,0},{8,12},{12,8},{16,20},{20,16},{24,28},{28,24},{32,36},... | collective-permute-start | bytes 49160 | tf_op jit(solution)/shard_map/ppermute | solution.py:407
  72.3 0.7 collective-permute-start.22
  73.3 2.0 %collective-permute-start.25 = (f32[8,256]{1,0:T(8,128)S(1)}, f32[8,256]{1,0:T(8,128)S(1)}, u32[]{:S(2)}, u32[]{:S(2)}) collective-permute-start(f32[8,256]{1,0:T(8,128)S(1)} %get-tuple-element.92), channel_id=1, source_target_pairs={{100,4},{108,12},{116,20},{124,28},{101,5},{109,13},{117,21},{125,... | collective-permute-start | bytes 24584 | tf_op jit(solution)/shard_map/ppermute | solution.py:428
  73.9 1.4 %collective-permute-start.24 = (f32[8,256]{1,0:T(8,128)S(1)}, f32[8,256]{1,0:T(8,128)S(1)}, u32[]{:S(2)}, u32[]{:S(2)}) collective-permute-start(f32[8,256]{1,0:T(8,128)S(1)} %get-tuple-element.92), channel_id=1, source_target_pairs={{100,36},{108,44},{116,52},{124,60},{68,4},{76,12},{84,20},{92,28}... | collective-permute-start | bytes 24584 | tf_op jit(solution)/shard_map/ppermute | solution.py:428
  74.6 0.7 collective-permute-start.23
  75.3 11.7 %copy-start = (f32[16,64]{1,0:T(8,128)S(1)}, f32[16,64]{1,0:T(8,128)}, u32[]{:S(2)}) copy-start(f32[16,64]{1,0:T(8,128)} %get-tuple-element.47.refs_4_) | copy-start | bytes 12292
  75.9 11.1 %collective-permute-start.26 = (f32[8,256]{1,0:T(8,128)S(1)}, f32[8,256]{1,0:T(8,128)S(1)}, u32[]{:S(2)}, u32[]{:S(2)}) collective-permute-start(f32[8,256]{1,0:T(8,128)S(1)} %shard_map.92.sigma_ref), channel_id=1, source_target_pairs={{0,4},{4,0},{8,12},{12,8},{16,20},{20,16},{24,28},{28,24},{32,36},... | collective-permute-start | bytes 24584 | tf_op jit(solution)/shard_map/ppermute | solution.py:407
